TPU v7x, 32 devices: a whole 2x2x4 slice. The times are simulated.
32 devices in a mesh: dp: 8 (over z, y), blk: 4 (over x, core).
Axes of the slice: x: 2, y: 2, z: 4, core: 2. Of those that a mesh axis runs over, the one named last changes fastest.
Arguments:
- tokens: float32 [96, 488, 768], P('dp', 'blk'), may hold values from -6 to 6
- kept_time: int32 [96, 48], P('dp'), may hold values from 0 to 1, as said below
- kept_bands: int32 [96, 10], P('dp'), may hold values from 0 to 1, as said below
- cotangent: float32 [96, 488, 768], P('dp', 'blk'), may hold values from -6 to 6
- weight_merged: float32 [768, 2304], P(('dp', 'blk')), may hold values from -0.21875 to 0.21875
- weight_output: float32 [768, 768], P(('dp', 'blk')), may hold values from -1.25 to 1.25
- weight_expand: float32 [768, 3072], P(('dp', 'blk')), may hold values from -0.21875 to 0.21875
- weight_shrink: float32 [3072, 768], P(('dp', 'blk')), may hold values from -0.109375 to 0.109375
- vectors: float32 [12, 768], P(None, ('dp', 'blk'))
- first_merged: float32 [768, 2304], P(('dp', 'blk')), may hold values from -0.0024414062 to 0.0024414062
- first_output: float32 [768, 768], P(('dp', 'blk')), may hold values from -0.00048828125 to 0.00048828125
- first_expand: float32 [768, 3072], P(('dp', 'blk')), may hold values from -0.0017089844 to 0.0017089844
- first_shrink: float32 [3072, 768], P(('dp', 'blk')), may hold values from -0.0029296875 to 0.0029296875
- first_vectors: float32 [12, 768], P(None, ('dp', 'blk')), may hold values from -0.0048828125 to 0.0048828125
- second_merged: float32 [768, 2304], P(('dp', 'blk')), may hold values from 1.4717196e-07 to 5.8868784e-07
- second_output: float32 [768, 768], P(('dp', 'blk')), may hold values from 5.8868785e-09 to 2.3547514e-08
- second_expand: float32 [768, 3072], P(('dp', 'blk')), may hold values from 7.211426e-08 to 2.8845704e-07
- second_shrink: float32 [3072, 768], P(('dp', 'blk')), may hold values from 2.4872062e-07 to 9.948825e-07
- second_vectors: float32 [12, 768], P(None, ('dp', 'blk')), may hold values from 5.8868784e-07 to 2.3547514e-06
Outputs:
- activations: float32 [96, 488, 768], P('dp', 'blk')
- token_grads: float32 [96, 488, 768], P('dp', 'blk')
- gradient_norm: float32 [], replicated
- clipped_merged: float32 [768, 2304], P(('dp', 'blk'))
- clipped_output: float32 [768, 768], P(('dp', 'blk'))
- clipped_expand: float32 [768, 3072], P(('dp', 'blk'))
- clipped_shrink: float32 [3072, 768], P(('dp', 'blk'))
- clipped_vectors: float32 [12, 768], P(None, ('dp', 'blk'))
- momentum_merged: float32 [768, 2304], P(('dp', 'blk'))
- momentum_output: float32 [768, 768], P(('dp', 'blk'))
- momentum_expand: float32 [768, 3072], P(('dp', 'blk'))
- momentum_shrink: float32 [3072, 768], P(('dp', 'blk'))
- momentum_vectors: float32 [12, 768], P(None, ('dp', 'blk'))
- variance_merged: float32 [768, 2304], P(('dp', 'blk'))
- variance_output: float32 [768, 768], P(('dp', 'blk'))
- variance_expand: float32 [768, 3072], P(('dp', 'blk'))
- variance_shrink: float32 [3072, 768], P(('dp', 'blk'))
- variance_vectors: float32 [12, 768], P(None, ('dp', 'blk'))
- updated_merged: float32 [768, 2304], P(('dp', 'blk'))
- updated_output: float32 [768, 768], P(('dp', 'blk'))
- updated_expand: float32 [768, 3072], P(('dp', 'blk'))
- updated_shrink: float32 [3072, 768], P(('dp', 'blk'))
- updated_vectors: float32 [12, 768], P(None, ('dp', 'blk'))
Inputs may be any that keep to these rules, and one draw needn't show every extreme that they name: `kept_time`: 0 or 1; in every clip each aligned run of 12 time columns holds at least one 1. `kept_bands`: 0 or 1; every clip keeps at least one frequency row.
All inputs are finite; a program needn't handle non-finite values.
Results may differ from a plain program's by a relative error of at most 0.012.
The roundings to bfloat16 on the way count: a program that leaves them out, or rounds other values in their place, can miss the bound.
Values may be sent and summed in bfloat16 or wider, within the bound.
A program may use at most 320 MiB of HBM per device.

v0:
```python
from functools import partial

import jax
import jax.numpy as jnp
from jax import lax
from jax.sharding import PartitionSpec as P

HEADS = 12
HEAD_DIM = 64
STEP = 5


CLIP_LIMIT = 1.0
BETA_ONE = 0.5
BETA_TWO = 0.5
ADAM_EPS = 1e-08
MATRIX_RATE = 0.1
VECTOR_RATE = 0.3
MATRIX_DECAY = 0.05


def layer_norm(values, scale_row, shift_row):
    centre = jnp.mean(values, -1, keepdims=True)
    centred = values - centre
    spread = jnp.mean(centred * centred, -1, keepdims=True)
    return centred * lax.rsqrt(spread + 1e-06) * scale_row + shift_row


def key_flags(kept_time, kept_bands, blocks):
    clip_count = kept_time.shape[0]
    columns = kept_time.shape[1] // blocks
    patches = kept_time.reshape(clip_count, blocks, columns, 1) * kept_bands[:, None, None, :]
    patches = patches.reshape(clip_count, blocks, columns * kept_bands.shape[1])
    leading = (jnp.arange(blocks, dtype=jnp.int32) == 0).astype(jnp.int32)
    special = jnp.broadcast_to(leading[None, :, None], (clip_count, blocks, 2))
    return jnp.concatenate([special, patches], 2).reshape(clip_count, -1)


def outer_sum(left_rows, right_rows):
    return lax.dot_general(
        left_rows, right_rows, (((0,), (0,)), ((), ())), preferred_element_type=jnp.float32
    )


def against(grad_rows, matrix):
    return lax.dot_general(
        grad_rows, matrix, (((1,), (1,)), ((), ())), preferred_element_type=jnp.float32
    )


def scored(queries, keys_all, live_keys):
    scores = (
        jnp.einsum("cqhe,ckhe->chqk", queries, keys_all, preferred_element_type=jnp.float32) * 0.125
    )
    return scores + jnp.where(live_keys > 0, 0.0, -1e30)[:, None, None, :]


def attend(queries, keys_all, values_all, live_keys):
    scores = scored(queries, keys_all, live_keys)
    highest = jnp.max(scores, -1, keepdims=True)
    exponent = jnp.exp(scores - highest)
    totals = jnp.sum(exponent, -1, keepdims=True)
    attention = (exponent / totals).astype(jnp.bfloat16)
    mixed = jnp.einsum("chqk,ckhe->cqhe", attention, values_all, preferred_element_type=jnp.float32)
    return (mixed, highest + jnp.log(totals))


def attend_back(queries, keys_all, values_all, live_keys, log_total, upstream):
    probs_full = jnp.exp(scored(queries, keys_all, live_keys) - log_total)
    attention = probs_full.astype(jnp.bfloat16)
    d_probs = jnp.einsum(
        "cqhe,ckhe->chqk", upstream, values_all, preferred_element_type=jnp.float32
    )
    d_scores = (probs_full * (d_probs - jnp.sum(d_probs * probs_full, -1, keepdims=True))).astype(
        jnp.bfloat16
    )
    d_queries = (
        jnp.einsum("chqk,ckhe->cqhe", d_scores, keys_all, preferred_element_type=jnp.float32)
        * 0.125
    )
    d_keys = (
        jnp.einsum("chqk,cqhe->ckhe", d_scores, queries, preferred_element_type=jnp.float32) * 0.125
    )
    d_values = jnp.einsum(
        "chqk,cqhe->ckhe", attention, upstream, preferred_element_type=jnp.float32
    )
    return (d_queries, d_keys, d_values)


def adamw(weight, first_old, second_old, grad_share, factor, step_rate, decay_rate):
    clipped = grad_share * factor
    momentum = BETA_ONE * first_old + (1.0 - BETA_ONE) * clipped
    variance = BETA_TWO * second_old + (1.0 - BETA_TWO) * clipped * clipped
    mean_hat = momentum / (1.0 - BETA_ONE**STEP)
    var_hat = variance / (1.0 - BETA_TWO**STEP)
    updated = weight - step_rate * (mean_hat / (jnp.sqrt(var_hat) + ADAM_EPS) + decay_rate * weight)
    return (clipped, momentum, variance, updated)


def shards(
    tokens,
    kept_time,
    kept_bands,
    cotangent,
    weight_merged,
    weight_output,
    weight_expand,
    weight_shrink,
    vectors,
    first_merged,
    first_output,
    first_expand,
    first_shrink,
    first_vectors,
    second_merged,
    second_output,
    second_expand,
    second_shrink,
    second_vectors,
):
    clip_count, segment, width = tokens.shape
    blocks = lax.axis_size("blk")
    row_count = clip_count * segment
    merged, output, expand, shrink, vec_low = (
        lax.all_gather(weight_merged.astype(jnp.bfloat16), ("dp", "blk"), axis=0, tiled=True),
        lax.all_gather(weight_output.astype(jnp.bfloat16), ("dp", "blk"), axis=0, tiled=True),
        lax.all_gather(weight_expand.astype(jnp.bfloat16), ("dp", "blk"), axis=0, tiled=True),
        lax.all_gather(weight_shrink.astype(jnp.bfloat16), ("dp", "blk"), axis=0, tiled=True),
        lax.all_gather(vectors.astype(jnp.bfloat16), ("dp", "blk"), axis=1, tiled=True),
    )
    params_vec = vec_low.astype(jnp.float32)
    rows_in = tokens.reshape(row_count, width)
    normed_one = layer_norm(rows_in, params_vec[0], params_vec[1]).astype(jnp.bfloat16)
    qkv_bias = jnp.concatenate([params_vec[2], jnp.zeros_like(params_vec[2]), params_vec[3]])
    packed = (jnp.dot(normed_one, merged, preferred_element_type=jnp.float32) + qkv_bias).astype(
        jnp.bfloat16
    )
    packed = packed.reshape(clip_count, segment, 3 * width)
    live_all = key_flags(kept_time, kept_bands, blocks)
    queries = packed.reshape(clip_count, segment, 3, HEADS, HEAD_DIM)[:, :, 0]
    pairs = lax.all_gather(packed[:, :, width:], "blk", axis=1, tiled=True)
    pairs = pairs.reshape(clip_count, blocks * segment, 2, HEADS, HEAD_DIM)
    keys_all = pairs[:, :, 0]
    values_all = pairs[:, :, 1]
    mixed, log_total = attend(queries, keys_all, values_all, live_all)
    mixed = mixed.astype(jnp.bfloat16).reshape(row_count, width)
    middle = rows_in + jnp.dot(mixed, output, preferred_element_type=jnp.float32) + params_vec[4]
    normed_two = layer_norm(middle, params_vec[5], params_vec[6]).astype(jnp.bfloat16)
    hidden = jnp.dot(normed_two, expand, preferred_element_type=jnp.float32) + params_vec[
        8:
    ].reshape(-1)
    gelu_out = jax.nn.gelu(hidden, approximate=False).astype(jnp.bfloat16)
    result = middle + jnp.dot(gelu_out, shrink, preferred_element_type=jnp.float32) + params_vec[7]
    d_result = cotangent.reshape(row_count, width)
    d_two = d_result.astype(jnp.bfloat16)
    grad_shrink = outer_sum(gelu_out, d_two)
    shrink_sums = jnp.sum(d_two.astype(jnp.float32), 0)
    d_gelu = against(d_two, shrink)
    _, gelu_pull = jax.vjp(partial(jax.nn.gelu, approximate=False), hidden)
    d_hidden = gelu_pull(d_gelu)[0].astype(jnp.bfloat16)
    grad_expand = outer_sum(normed_two, d_hidden)
    expand_sums = jnp.sum(d_hidden.astype(jnp.float32), 0)
    d_normed_two = against(d_hidden, expand)
    _, second_pull = jax.vjp(layer_norm, middle, params_vec[5], params_vec[6])
    d_middle, grad_gain_two, grad_shift_two = second_pull(d_normed_two)
    d_middle = d_middle + d_result
    d_one = d_middle.astype(jnp.bfloat16)
    grad_output = outer_sum(mixed, d_one)
    output_sums = jnp.sum(d_one.astype(jnp.float32), 0)
    d_mixed = against(d_one, output).astype(jnp.bfloat16)
    upstream = d_mixed.reshape(clip_count, segment, HEADS, HEAD_DIM)
    d_queries, d_keys, d_values = attend_back(
        queries, keys_all, values_all, live_all, log_total, upstream
    )
    d_pairs = jnp.stack([d_keys, d_values], 2).reshape(clip_count, blocks * segment, 2 * width)
    d_pairs = lax.psum_scatter(
        d_pairs.astype(jnp.bfloat16), "blk", scatter_dimension=1, tiled=True
    ).astype(jnp.float32)
    d_packed = jnp.concatenate([d_queries.reshape(clip_count, segment, width), d_pairs], 2)
    d_packed = d_packed.astype(jnp.bfloat16).reshape(row_count, 3 * width)
    grad_merged = outer_sum(normed_one, d_packed)
    packed_sums = jnp.sum(d_packed.astype(jnp.float32), 0)
    d_normed_one = against(d_packed, merged)
    _, first_pull = jax.vjp(layer_norm, rows_in, params_vec[0], params_vec[1])
    d_rows, grad_gain_one, grad_shift_one = first_pull(d_normed_one)
    token_grads = (d_rows + d_middle).reshape(clip_count, segment, width)
    small_rows = jnp.stack(
        [
            grad_gain_one,
            grad_shift_one,
            packed_sums[:width],
            packed_sums[2 * width :],
            output_sums,
            grad_gain_two,
            grad_shift_two,
            shrink_sums,
        ]
    )
    grad_vectors = jnp.concatenate([small_rows, expand_sums.reshape(-1, width)], 0)
    shares = (
        lax.psum_scatter(grad_merged, ("dp", "blk"), scatter_dimension=0, tiled=True),
        lax.psum_scatter(grad_output, ("dp", "blk"), scatter_dimension=0, tiled=True),
        lax.psum_scatter(grad_expand, ("dp", "blk"), scatter_dimension=0, tiled=True),
        lax.psum_scatter(grad_shrink, ("dp", "blk"), scatter_dimension=0, tiled=True),
        lax.psum_scatter(grad_vectors, ("dp", "blk"), scatter_dimension=1, tiled=True),
    )
    squares = sum((jnp.sum(share_part * share_part) for share_part in shares))
    total = lax.psum(squares, ("dp", "blk"))
    gradient_norm = jnp.sqrt(total)
    factor = CLIP_LIMIT / jnp.maximum(gradient_norm, CLIP_LIMIT)
    weights = (weight_merged, weight_output, weight_expand, weight_shrink, vectors)
    firsts = (first_merged, first_output, first_expand, first_shrink, first_vectors)
    seconds = (second_merged, second_output, second_expand, second_shrink, second_vectors)
    rates = (MATRIX_RATE, MATRIX_RATE, MATRIX_RATE, MATRIX_RATE, VECTOR_RATE)
    decays = (MATRIX_DECAY, MATRIX_DECAY, MATRIX_DECAY, MATRIX_DECAY, 0.0)
    steps_out = [
        adamw(
            weights[index],
            firsts[index],
            seconds[index],
            shares[index],
            factor,
            rates[index],
            decays[index],
        )
        for index in range(5)
    ]
    return (
        result.reshape(clip_count, segment, width),
        token_grads,
        gradient_norm,
        steps_out[0][0],
        steps_out[1][0],
        steps_out[2][0],
        steps_out[3][0],
        steps_out[4][0],
        steps_out[0][1],
        steps_out[1][1],
        steps_out[2][1],
        steps_out[3][1],
        steps_out[4][1],
        steps_out[0][2],
        steps_out[1][2],
        steps_out[2][2],
        steps_out[3][2],
        steps_out[4][2],
        steps_out[0][3],
        steps_out[1][3],
        steps_out[2][3],
        steps_out[3][3],
        steps_out[4][3],
    )


def solution(mesh):
    return jax.shard_map(
        shards,
        mesh=mesh,
        in_specs=(
            P("dp", "blk", None),
            P("dp", None),
            P("dp", None),
            P("dp", "blk", None),
            P(("dp", "blk"), None),
            P(("dp", "blk"), None),
            P(("dp", "blk"), None),
            P(("dp", "blk"), None),
            P(None, ("dp", "blk")),
            P(("dp", "blk"), None),
            P(("dp", "blk"), None),
            P(("dp", "blk"), None),
            P(("dp", "blk"), None),
            P(None, ("dp", "blk")),
            P(("dp", "blk"), None),
            P(("dp", "blk"), None),
            P(("dp", "blk"), None),
            P(("dp", "blk"), None),
            P(None, ("dp", "blk")),
        ),
        out_specs=(
            P("dp", "blk", None),
            P("dp", "blk", None),
            P(),
            P(("dp", "blk"), None),
            P(("dp", "blk"), None),
            P(("dp", "blk"), None),
            P(("dp", "blk"), None),
            P(None, ("dp", "blk")),
            P(("dp", "blk"), None),
            P(("dp", "blk"), None),
            P(("dp", "blk"), None),
            P(("dp", "blk"), None),
            P(None, ("dp", "blk")),
            P(("dp", "blk"), None),
            P(("dp", "blk"), None),
            P(("dp", "blk"), None),
            P(("dp", "blk"), None),
            P(None, ("dp", "blk")),
            P(("dp", "blk"), None),
            P(("dp", "blk"), None),
            P(("dp", "blk"), None),
            P(("dp", "blk"), None),
            P(None, ("dp", "blk")),
        ),
        check_vma=False,
    )
```

profile of v0, /device:TPU:0, one launch (start us, length us, event | category | flops | bytes accessed | tf_op | source)
XLA Modules:
  0.0 1507.4 jit_solution(1556626458954077790)
XLA Ops:
  20.8 43.7 %all-gather = bf16[32,24,12]{1,2,0:T(8,128)(2,1)S(1)} all-gather(bf16[1,24,12]{1,2,0:T(8,128)(2,1)S(1)} %convert_bitcast_fusion.2), channel_id=1, replica_groups=mesh['dp'=8,'blk'=4] {'dp','blk'}, dimensions={0}, use_global_device_ids=true | all-gather | bytes 19008 | tf_op jit(solution)/shard_map/all_gather | solution.py:129
  65.5 9.1 all-gather.7.cloned.1.call-done
  74.5 10.5 fusion.13
  109.2 21.5 %reshape.221 = bf16[12,122,3,12,64]{4,3,2,1,0:T(8,128)(2,1)} reshape(bf16[1464,2304]{1,0:T(8,128)(2,1)} %fusion.13) | data formatting | bytes 13492224 | tf_op jit(solution)/shard_map/reshape;reshape | solution.py:140
  143.6 103.8 %all-gather.9.cloned.1.call-done = bf16[12,488,1536]{2,0,1:T(8,128)(2,1)} async-done(((bf16[12,122,1536]{2,0,1:T(8,128)(2,1)}), bf16[12,488,1536]{2,0,1:T(8,128)(2,1)}) %all-gather.9.cloned.1.call-update) | async-done | bytes 17989648 | tf_op jit(solution)/shard_map/all_gather | solution.py:141
  247.4 30.7 %copy.90 = bf16[12,488,1536]{1,2,0:T(8,128)(2,1)} copy(bf16[12,488,1536]{2,0,1:T(8,128)(2,1)} %all-gather.9.cloned.1.call-done) | data formatting | bytes 35979264 | tf_op jit(solution)/shard_map/all_gather | solution.py:141
  278.1 20.6 %fusion.12 = (f32[12,12,122]{2,1,0:T(8,128)S(1)}, f32[12,12,122,488]{2,3,1,0:T(8,128)}) fusion(f32[12,488]{1,0:T(8,128)S(1)} %select_n.13, bf16[12,488,2,12,64]{1,4,3,2,0:T(8,128)(2,1)} %bitcast.80, bf16[12,122,1,12,64]{1,4,3,0,2:T(8,128)(2,1)S(1)} %copy.115), kind=kOutput, calls=%fused_computation.31 | convolution fusion | flops 1123069568 | bytes 46072320 | tf_op jit(solution)/shard_map/cqhe,ckhe->chqk/dot_general | solution.py:53
  298.7 16.2 %fusion = f32[12,12,122]{2,1,0:T(8,128)S(1)} fusion(f32[12,12,122]{2,1,0:T(8,128)S(1)} %get-tuple-element.67, f32[12,488]{1,0:T(8,128)S(1)} %select_n.13, f32[12,12,122,488]{2,3,1,0:T(8,128)} %get-tuple-element.68), kind=kLoop, calls=%fused_computation.6 | loop fusion | flops 34275168 | bytes 34456704 | tf_op jit(solution)/shard_map/reduce_sum | solution.py:62
  315.6 18.3 %convert_bitcast_fusion.1 = bf16[12,122,12,64]{1,3,2,0:T(8,128)(2,1)S(1)} fusion(f32[12,12,122]{2,1,0:T(8,128)S(1)} %fusion, f32[12,12,122]{2,1,0:T(8,128)S(1)} %get-tuple-element.67, f32[12,488]{1,0:T(8,128)S(1)} %select_n.13, f32[12,12,122,488]{2,3,1,0:T(8,128)} %get-tuple-element.68, bf16[12,488,2,12,64]{1,4,3,2,0:T(8,128)(2,1)} %bitcast.81), kind=kOutput, calls=%fused_computation.63 | convolution fusion | flops 1141357824 | bytes 47829120 | tf_op jit(solution)/shard_map/chqk,ckhe->cqhe/dot_general | solution.py:64
  348.7 22.2 %all-gather.13.cloned.1.call-done = bf16[768,3072]{1,0:T(8,128)(2,1)} async-done(((bf16[24,3072]{1,0:T(8,128)(2,1)}), bf16[768,3072]{1,0:T(8,128)(2,1)}) %all-gather.13.cloned.1.call-update) | async-done | bytes 4718608 | tf_op jit(solution)/shard_map/all_gather | solution.py:127
  370.9 52.6 %multiply_convert_fusion.2 = (bf16[1464,3072]{1,0:T(8,128)(2,1)}, f32[1464,3072]{1,0:T(8,128)}, f32[1464,3072]{1,0:T(8,128)}) fusion(f32[3072]{0:T(1024)S(1)} %add.233, bf16[768,3072]{1,0:T(8,128)(2,1)} %all-gather.13.cloned.1.call-done, f32[1464,768]{1,0:T(8,128)} %copy-done.3, f32[768]{0:T(1024)S(1)} %get-tuple-element.30, ...), kind=kOutput, calls=%fused_computation.16 | convolution fusion | flops 7210469376 | bytes 54220224 | tf_op jit(solution)/shard_map/dot_general | solution.py:149
  423.5 13.2 all-gather.15.cloned.1.call-done
  436.7 26.6 %convert_reduce_fusion = (f32[3072]{0:T(1024)}, bf16[1464,3072]{1,0:T(8,128)(2,1)}) fusion(f32[1464,3072]{1,0:T(8,128)} %get-tuple-element.64, bf16[3072,768]{1,0:T(8,128)(2,1)} %all-gather.15.cloned.1.call-done, f32[1464,768]{1,0:T(8,128)} %reshape.210, f32[1464,3072]{1,0:T(8,128)} %get-tuple-element.71, f32[3072]{0:T(1024)S(1)} %add.233), kind=kOutput, calls=%fused_computation.13 | convolution fusion | flops 6985595904 | bytes 54214656 | tf_op jit(solution)/shard_map/dot_general | solution.py:46
  463.4 13.3 multiply_reduce_fusion.2
  497.4 18.9 %convert_bitcast_fusion = bf16[12,488,1,12,64]{1,4,3,0,2:T(8,128)(2,1)} fusion(bf16[12,122,12,64]{1,3,2,0:T(8,128)(2,1)S(1)} %copy.97, f32[12,12,122]{2,1,0:T(8,128)S(1)} %copy-done.9, f32[12,488]{1,0:T(8,128)S(1)} %copy-done.6, f32[12,12,122,488]{2,3,1,0:T(8,128)} %get-tuple-element.68), kind=kOutput, calls=%fused_computation.38 | convolution fusion | flops 1136157696 | bytes 45629952 | tf_op jit(solution)/shard_map/chqk,cqhe->ckhe/dot_general | solution.py:84
  516.3 33.9 %multiply_reduce_fusion = (f32[12,12,122]{2,1,0:T(8,128)S(1)}, f32[12,12,122,488]{2,3,1,0:T(8,128)}) fusion(f32[12,12,122]{2,1,0:T(8,128)S(1)} %copy-done.9, f32[12,488]{1,0:T(8,128)S(1)} %copy-done.6, f32[12,12,122,488]{2,3,1,0:T(8,128)} %get-tuple-element.68, bf16[12,122,12,64]{1,3,2,0:T(8,128)(2,1)S(1)} %copy.97, bf16[12,488,2,12,64]{1,4,3,2,0:T(8,128)(2,1)} %bitcast.82), kind=kOutput, calls=%fused_computation.1 | convolution fusion | flops 1140215936 | bytes 82121856 | tf_op jit(solution)/shard_map/cqhe,ckhe->chqk/dot_general | solution.py:71
  550.2 30.3 %multiply_convert_fusion = bf16[12,12,122,488]{2,3,1,0:T(8,128)(2,1)} fusion(f32[12,12,122,488]{2,3,1,0:T(8,128)} %get-tuple-element.74, f32[12,12,122]{2,1,0:T(8,128)S(1)} %get-tuple-element.73, f32[12,12,122]{2,1,0:T(8,128)S(1)} %copy-done.9, f32[12,488]{1,0:T(8,128)S(1)} %copy-done.6, f32[12,12,122,488]{2,3,1,0:T(8,128)} %get-tuple-element.68), kind=kLoop, calls=%fused_computation | loop fusion | flops 51439104 | bytes 85895808 | tf_op jit(solution)/shard_map/convert_element_type | solution.py:74
  580.5 13.7 fusion.14
  594.2 9.4 pad_maximum_fusion
  617.2 14.6 fusion.37
  631.9 13.9 fusion.23
  647.6 13.5 fusion.20
  676.0 255.1 %all-reduce.4.cloned.1.call-done = bf16[12,488,1536]{1,2,0:T(8,128)(2,1)} async-done(((bf16[12,488,1536]{1,2,0:T(8,128)(2,1)}), bf16[12,488,1536]{1,2,0:T(8,128)(2,1)}) %all-reduce.4.cloned.1.call-update) | async-done | bytes 17989648
  956.1 11.8 fusion.36
  970.9 13.2 add_add_fusion.4
  989.9 46.7 %reduce-scatter.9.cloned.1.call-done = f32[24,768]{1,0:T(8,128)} async-done(((f32[768,768]{1,0:T(8,128)}), f32[24,768]{1,0:T(8,128)}) %reduce-scatter.9.cloned.1.call-update) | async-done | bytes 73744 | tf_op jit(solution)/shard_map/reduce_scatter | solution.py:202
  1042.0 13.8 multiply_reduce_fusion.3
  1055.9 40.1 %all-reduce.1 = f32[12,768]{1,0:T(8,128)S(1)} all-reduce(f32[12,768]{1,0:T(8,128)S(1)} %concatenate.23), channel_id=7, replica_groups=mesh['dp'=8,'blk'=4] {'dp','blk'}, use_global_device_ids=true, to_apply=%region_28.29.clone | all-reduce | flops 9216 | bytes 73728
  1106.2 70.7 %reduce-scatter.11.cloned.1.call-done = f32[24,3072]{1,0:T(8,128)} async-done(((f32[768,3072]{1,0:T(8,128)}), f32[24,3072]{1,0:T(8,128)}) %reduce-scatter.11.cloned.1.call-update) | async-done | bytes 294928 | tf_op jit(solution)/shard_map/reduce_scatter | solution.py:203
  1178.6 140.1 %reduce-scatter.13.cloned.1.call-done = f32[96,768]{1,0:T(8,128)} async-done(((f32[3072,768]{1,0:T(8,128)}), f32[96,768]{1,0:T(8,128)}) %reduce-scatter.13.cloned.1.call-update) | async-done | bytes 294928 | tf_op jit(solution)/shard_map/reduce_scatter | solution.py:204
  1320.4 122.0 %reduce-scatter.7.cloned.1.call-done = f32[24,2304]{1,0:T(8,128)} async-done(((f32[768,2304]{1,0:T(8,128)}), f32[24,2304]{1,0:T(8,128)}) %reduce-scatter.7.cloned.1.call-update) | async-done | bytes 221200 | tf_op jit(solution)/shard_map/reduce_scatter | solution.py:201
  1452.7 40.0 %psum.7 = f32[]{:T(128)} all-reduce(f32[]{:T(128)S(6)} %add.246), channel_id=1, replica_groups=mesh['dp'=8,'blk'=4] {'dp','blk'}, use_global_device_ids=true, to_apply=%region_30.31 | all-reduce | flops 1 | bytes 8 | tf_op jit(solution)/shard_map/psum | solution.py:208
  (236 shorter events, 182.3 us)
Async XLA Ops:
  7.2 67.3 %all-gather.7.cloned.1.call-start = ((), (), s32[]{:S(2)}) async-start(), calls=%async_computation.4 | async-start | bytes 3649536 | tf_op jit(solution)/shard_map/all_gather | solution.py:125
  8.9 238.6 %all-gather.9.cloned.1.call-start = ((), (), s32[]{:S(2)}) async-start(), calls=%async_computation.5 | async-start | bytes 29982720 | tf_op jit(solution)/shard_map/all_gather | solution.py:141
  17.1 68.0 %copy-start.36 = (f32[1464]{0:T(1024)}, f32[1464]{0:T(1024)S(1)}, u32[]{:S(2)}) copy-start(f32[1464]{0:T(1024)S(1)} %div.99) | copy-start | bytes 17572
  20.8 64.3 %copy-start.38 = (f32[1464]{0:T(1024)}, f32[1464]{0:T(1024)S(1)}, u32[]{:S(2)}) copy-start(f32[1464]{0:T(1024)S(1)} %rsqrt.22) | copy-start | bytes 17572
  65.5 305.5 %copy-start.51 = (f32[768]{0:T(1024)}, f32[768]{0:T(1024)S(1)}, u32[]{:S(2)}) copy-start(f32[768]{0:T(1024)S(1)} %get-tuple-element.30) | copy-start | bytes 9220
  100.2 239.6 %all-gather.11.cloned.1.call-start = ((), (), s32[]{:S(2)}) async-start(), calls=%async_computation.6 | async-start | bytes 1216512 | tf_op jit(solution)/shard_map/all_gather | solution.py:126
  100.9 270.0 %all-gather.13.cloned.1.call-start = ((), (), s32[]{:S(2)}) async-start(), calls=%async_computation.7 | async-start | bytes 4866048 | tf_op jit(solution)/shard_map/all_gather | solution.py:127
  101.7 335.0 %all-gather.15.cloned.1.call-start = ((), (), s32[]{:S(2)}) async-start(), calls=%async_computation.8 | async-start | bytes 4866048 | tf_op jit(solution)/shard_map/all_gather | solution.py:128
  102.5 828.7 %all-reduce.4.cloned.1.call-start = ((), (), s32[]{:S(2)}) async-start(), calls=%async_computation.13 | async-start | bytes 37748736
  103.5 212.1 %copy-start.5 = (f32[12,488]{1,0:T(8,128)}, f32[12,488]{1,0:T(8,128)S(1)}, u32[]{:S(2)}) copy-start(f32[12,488]{1,0:T(8,128)S(1)} %select_n.13) | copy-start | bytes 70276
  143.6 134.5 %copy-start.1 = (bf16[12,122,1,12,64]{1,4,3,0,2:T(8,128)(2,1)}, bf16[12,122,1,12,64]{1,4,3,0,2:T(8,128)(2,1)S(1)}, u32[]{:S(2)}) copy-start(bf16[12,122,1,12,64]{1,4,3,0,2:T(8,128)(2,1)S(1)} %copy.115) | copy-start | bytes 6746116
  610.4 426.2 %reduce-scatter.9.cloned.1.call-start = ((), (), s32[]{:S(2)}) async-start(), calls=%async_computation.10 | async-start | bytes 2433024 | tf_op jit(solution)/shard_map/reduce_scatter | solution.py:202
  617.1 559.8 %reduce-scatter.11.cloned.1.call-start = ((), (), s32[]{:S(2)}) async-start(), calls=%async_computation.11 | async-start | bytes 9732096 | tf_op jit(solution)/shard_map/reduce_scatter | solution.py:203
  631.8 686.8 %reduce-scatter.13.cloned.1.call-start = ((), (), s32[]{:S(2)}) async-start(), calls=%async_computation.12 | async-start | bytes 9732096 | tf_op jit(solution)/shard_map/reduce_scatter | solution.py:204
  645.7 796.6 %reduce-scatter.7.cloned.1.call-start = ((), (), s32[]{:S(2)}) async-start(), calls=%async_computation.9 | async-start | bytes 7299072 | tf_op jit(solution)/shard_map/reduce_scatter | solution.py:201
  1106.1 387.4 %copy-start.35 = (f32[12,24]{1,0:T(8,128)S(1)}, f32[12,24]{1,0:T(8,128)}, u32[]{:S(2)}) copy-start(f32[12,24]{1,0:T(8,128)} %param.27) | copy-start | bytes 3460
  1106.1 387.4 %copy-start.46 = (f32[12,24]{1,0:T(8,128)S(1)}, f32[12,24]{1,0:T(8,128)}, u32[]{:S(2)}) copy-start(f32[12,24]{1,0:T(8,128)} %param.37) | copy-start | bytes 3460
  1106.1 387.4 %copy-start.47 = (f32[12,24]{1,0:T(8,128)S(1)}, f32[12,24]{1,0:T(8,128)}, u32[]{:S(2)}) copy-start(f32[12,24]{1,0:T(8,128)} %param.32) | copy-start | bytes 3460
  1106.1 388.1 %copy-start.23 = (f32[24,768]{1,0:T(8,128)S(1)}, f32[24,768]{1,0:T(8,128)}, u32[]{:S(2)}) copy-start(f32[24,768]{1,0:T(8,128)} %param.24) | copy-start | bytes 221188
  1106.1 388.1 %copy-start.24 = (f32[24,768]{1,0:T(8,128)S(1)}, f32[24,768]{1,0:T(8,128)}, u32[]{:S(2)}) copy-start(f32[24,768]{1,0:T(8,128)} %reduce-scatter.9.cloned.1.call-done) | copy-start | bytes 221188
  1106.1 388.1 %copy-start.33 = (f32[24,768]{1,0:T(8,128)S(1)}, f32[24,768]{1,0:T(8,128)}, u32[]{:S(2)}) copy-start(f32[24,768]{1,0:T(8,128)} %param.34) | copy-start | bytes 221188
  1106.1 389.7 %copy-start.17 = (f32[24,2304]{1,0:T(8,128)S(1)}, f32[24,2304]{1,0:T(8,128)}, u32[]{:S(2)}) copy-start(f32[24,2304]{1,0:T(8,128)} %param.23) | copy-start | bytes 663556
  1106.1 389.7 %copy-start.25 = (f32[24,2304]{1,0:T(8,128)S(1)}, f32[24,2304]{1,0:T(8,128)}, u32[]{:S(2)}) copy-start(f32[24,2304]{1,0:T(8,128)} %param.33) | copy-start | bytes 663556
  1106.1 389.7 %copy-start.26 = (f32[24,2304]{1,0:T(8,128)S(1)}, f32[24,2304]{1,0:T(8,128)}, u32[]{:S(2)}) copy-start(f32[24,2304]{1,0:T(8,128)} %param.28) | copy-start | bytes 663556
  1106.1 390.7 %copy-start.11 = (f32[96,768]{1,0:T(8,128)S(1)}, f32[96,768]{1,0:T(8,128)}, u32[]{:S(2)}) copy-start(f32[96,768]{1,0:T(8,128)} %param.26) | copy-start | bytes 884740
  1106.2 390.7 %copy-start.18 = (f32[96,768]{1,0:T(8,128)S(1)}, f32[96,768]{1,0:T(8,128)}, u32[]{:S(2)}) copy-start(f32[96,768]{1,0:T(8,128)} %param.36) | copy-start | bytes 884740
  1106.2 390.6 %copy-start.19 = (f32[96,768]{1,0:T(8,128)S(1)}, f32[96,768]{1,0:T(8,128)}, u32[]{:S(2)}) copy-start(f32[96,768]{1,0:T(8,128)} %param.31) | copy-start | bytes 884740
  1318.6 178.2 %copy-start.15 = (f32[96,768]{1,0:T(8,128)S(1)}, f32[96,768]{1,0:T(8,128)}, u32[]{:S(2)}) copy-start(f32[96,768]{1,0:T(8,128)} %reduce-scatter.13.cloned.1.call-done) | copy-start | bytes 884740
  1320.4 177.5 %copy-start.13 = (f32[24,3072]{1,0:T(8,128)S(1)}, f32[24,3072]{1,0:T(8,128)}, u32[]{:S(2)}) copy-start(f32[24,3072]{1,0:T(8,128)} %param.25) | copy-start | bytes 884740
  1320.4 177.5 %copy-start.14 = (f32[24,3072]{1,0:T(8,128)S(1)}, f32[24,3072]{1,0:T(8,128)}, u32[]{:S(2)}) copy-start(f32[24,3072]{1,0:T(8,128)} %reduce-scatter.11.cloned.1.call-done) | copy-start | bytes 884740
  1320.4 177.5 %copy-start.20 = (f32[24,3072]{1,0:T(8,128)S(1)}, f32[24,3072]{1,0:T(8,128)}, u32[]{:S(2)}) copy-start(f32[24,3072]{1,0:T(8,128)} %param.35) | copy-start | bytes 884740
  1320.4 177.6 %copy-start.21 = (f32[24,3072]{1,0:T(8,128)S(1)}, f32[24,3072]{1,0:T(8,128)}, u32[]{:S(2)}) copy-start(f32[24,3072]{1,0:T(8,128)} %param.30) | copy-start | bytes 884740
  (40 other events, 477.4 us)
Sparse Core Ops, SparseCore 0:
  11.5 62.9 all-gather.6
  100.3 147.0 all-gather.8
  250.9 54.0 all-gather.10
  308.3 62.5 all-gather.12
  374.2 62.4 all-gather.14
  610.5 320.5 all-reduce.3
  937.3 99.2 reduce-scatter.8
  1042.5 134.4 reduce-scatter.10
  1183.8 134.7 reduce-scatter.12
  1324.2 118.1 reduce-scatter.6
where the time goes:
time: 1520 us; the launch traced here: 1510 us
  waiting for transfers between devices  783 us (52%)
  matrix products  302 us (20%)
  local copies, waits for them, and re-layouts  178 us (12%)
  blocking collectives  124 us (8%)
  other arithmetic  98.7 us (6%)
  between operations  21.2 us (1%)
    unnamed x11, waiting for transfers between devices  255 us
    reduce_scatter x1, waiting for transfers between devices, shards(): lax.psum_scatter(grad_shrink, ('dp', 'blk'), scatter_dimension=0, tiled=T...  140 us
    reduce_scatter x1, waiting for transfers between devices, shards(): lax.psum_scatter(grad_merged, ('dp', 'blk'), scatter_dimension=0, tiled=T...  122 us
    all_gather x1, waiting for transfers between devices, shards(): pairs = lax.all_gather(packed[:, :, width:], 'blk', axis=1, tiled=True)  104 us
    reduce_scatter x1, waiting for transfers between devices, shards(): lax.psum_scatter(grad_expand, ('dp', 'blk'), scatter_dimension=0, tiled=T...  70.7 us
    dot_general x4, matrix products, against(): lax.dot_general(grad_rows, matrix, (((1,), (1,)), ((), ())), preferred_el...  55.7 us
    dot_general x1, matrix products, shards(): jnp.dot(normed_two, expand, preferred_element_type=jnp.float32)  52.6 us
    reduce_scatter x1, waiting for transfers between devices, shards(): lax.psum_scatter(grad_output, ('dp', 'blk'), scatter_dimension=0, tiled=T...  46.7 us
  transfers between devices with their start and end apart: 10, of which 9 were waited for; matrix products, arithmetic and copies ran while one was open for 24% of the time, Pallas kernels for 0%

commit v1 on v0

v1 whole, which is shorter than its diff:
```python
import functools
import jax
import jax.numpy as jnp
from jax import lax
from jax.experimental import pallas as pl
from jax.experimental.pallas import tpu as pltpu
from jax.sharding import PartitionSpec as P

HEADS = 12
STEP = 5
CLIP_LIMIT = 1.0
BETA_ONE = 0.5
BETA_TWO = 0.5
ADAM_EPS = 1e-08
MATRIX_RATE = 0.1
VECTOR_RATE = 0.3
MATRIX_DECAY = 0.05

F32, BF16 = jnp.float32, jnp.bfloat16
EPS = 1e-06
HALF = 64
LANES = 128
LIMIT = 60 * 1024 * 1024


def nn(a, b):
    return lax.dot_general(a, b, (((1,), (0,)), ((), ())), preferred_element_type=F32)


def nt(a, b):
    return lax.dot_general(a, b, (((1,), (1,)), ((), ())), preferred_element_type=F32)


def tn(a, b):
    return lax.dot_general(a, b, (((0,), (0,)), ((), ())), preferred_element_type=F32)


def norm_stats(v):
    centre = jnp.mean(v, -1, keepdims=True)
    c = v - centre
    spread = jnp.mean(c * c, -1, keepdims=True)
    r = lax.rsqrt(spread + EPS)
    return c * r, r


def norm_back(xhat, r, dy, gain):
    dx = dy * gain
    m1 = jnp.mean(dx, -1, keepdims=True)
    m2 = jnp.mean(dx * xhat, -1, keepdims=True)
    return (dx - m1 - xhat * m2) * r


def gelu_pair(x):
    z = jnp.abs(x)
    t = 1.0 / (1.0 + 0.3275911 * 0.7071067811865476 * z)
    e = jnp.exp(-0.5 * x * x)
    poly = t * (0.127414796 + t * (-0.142248368 + t * (0.7107068705 + t * (-0.7265760135 + t * 0.5307027145))))
    tail = poly * e
    phi = jnp.where(x >= 0, 1.0 - tail, tail)
    return x * phi, phi + (0.3989422804014327 * x) * e


def ffn_kernel(mid_ref, xc_ref, cot_ref, exp_ref, shr_ref, vec_ref,
               act_ref, dmid_ref, ge_ref, gs_ref, sums_ref,
               n2_s, y_s, dn_s, ae_s, as_s):
    f, i = pl.program_id(0), pl.program_id(1)
    nf, ni = pl.num_programs(0), pl.num_programs(1)
    rows = mid_ref.shape[0]
    here = pl.ds(pl.multiple_of(i * rows, rows), rows)

    @pl.when((f == 0) & (i == 0))
    def _():
        sums_ref[...] = jnp.zeros_like(sums_ref)

    @pl.when(f == 0)
    def _():
        xhat, _ = norm_stats(mid_ref[...])
        n2_s[here, :] = (xhat * vec_ref[5:6, :] + vec_ref[6:7, :]).astype(BF16)

    n2 = n2_s[here, :]
    d2 = cot_ref[...]
    h = nn(n2, exp_ref[...]) + vec_ref[pl.ds(8 + f, 1), :]
    dg = nt(d2, shr_ref[...])
    g, gp = gelu_pair(h)
    g = g.astype(BF16)
    dh32 = gp * dg
    dh = dh32.astype(BF16)
    sums_ref[pl.ds(8 + f, 1), :] += jnp.sum(dh32, 0, keepdims=True)
    y = nn(g, shr_ref[...])
    dn = nt(dh, exp_ref[...])
    ge = tn(n2, dh)
    gs = tn(g, d2)

    @pl.when(f == 0)
    def _():
        y_s[here, :] = y
        dn_s[here, :] = dn

    @pl.when(f > 0)
    def _():
        y_s[here, :] += y
        dn_s[here, :] += dn

    @pl.when(i == 0)
    def _():
        ae_s[...] = ge
        as_s[...] = gs

    @pl.when((i > 0) & (i < ni - 1))
    def _():
        ae_s[...] += ge
        as_s[...] += gs

    @pl.when(i == ni - 1)
    def _():
        ge_ref[...] = (ae_s[...] + ge).astype(ge_ref.dtype)
        gs_ref[...] = (as_s[...] + gs).astype(gs_ref.dtype)

    @pl.when(f == nf - 1)
    def _():
        mid = mid_ref[...]
        cot = d2.astype(F32)
        xhat, r = norm_stats(mid)
        dy = dn_s[here, :]
        act_ref[...] = ((mid - xc_ref[...].astype(F32)) + (y_s[here, :] + vec_ref[7:8, :])).astype(BF16)
        dmid_ref[...] = cot + norm_back(xhat, r, dy, vec_ref[5:6, :])
        sums_ref[5:6, :] += jnp.sum(dy * xhat, 0, keepdims=True)
        sums_ref[6:7, :] += jnp.sum(dy, 0, keepdims=True)
        sums_ref[7:8, :] += jnp.sum(cot, 0, keepdims=True)


def ffn(mid, xc, cot, expand, shrink, vec, rows):
    total, width = mid.shape
    ff = expand.shape[1] - width
    nf, ni = ff // width, total // rows
    first = lambda f, i: (jnp.where((f == 0) | (f == nf - 1), i, ni - 1), 0)
    last = lambda f, i: (jnp.where(f == nf - 1, i, 0), 0)
    return pl.pallas_call(
        ffn_kernel,
        grid=(nf, ni),
        in_specs=[
            pl.BlockSpec((rows, width), first),
            pl.BlockSpec((rows, width), last),
            pl.BlockSpec((rows, width), lambda f, i: (i, 0)),
            pl.BlockSpec((width, width), lambda f, i: (0, f + 1)),
            pl.BlockSpec((width, width), lambda f, i: (f, 0)),
            pl.BlockSpec(vec.shape, lambda f, i: (0, 0)),
        ],
        out_specs=[
            pl.BlockSpec((rows, width), last),
            pl.BlockSpec((rows, width), last),
            pl.BlockSpec((width, width), lambda f, i: (0, f)),
            pl.BlockSpec((width, width), lambda f, i: (f, 0)),
            pl.BlockSpec((16, width), lambda f, i: (0, 0)),
        ],
        out_shape=[
            jax.ShapeDtypeStruct((total, width), BF16),
            jax.ShapeDtypeStruct((total, width), F32),
            jax.ShapeDtypeStruct((width, ff), BF16),
            jax.ShapeDtypeStruct((ff, width), BF16),
            jax.ShapeDtypeStruct((16, width), F32),
        ],
        scratch_shapes=[
            pltpu.VMEM((total, width), BF16),
            pltpu.VMEM((total, width), F32),
            pltpu.VMEM((total, width), F32),
            pltpu.VMEM((width, width), F32),
            pltpu.VMEM((width, width), F32),
        ],
        compiler_params=pltpu.CompilerParams(
            dimension_semantics=("arbitrary", "arbitrary"), vmem_limit_bytes=LIMIT),
        name="ffn",
    )(mid, xc, cot, expand, shrink, vec)


def attn_fwd_kernel(heads, xc_ref, dead_ref, mrg_ref, out_ref, vec_ref,
                    n1_ref, qa_ref, kv_ref, mix_ref, mid_ref, pk_s):
    width = xc_ref.shape[1]
    seq = xc_ref.shape[0]
    pairs = heads // 2
    xc = xc_ref[...].astype(F32)
    xhat, _ = norm_stats(xc)
    n1 = (xhat * vec_ref[0:1, :] + vec_ref[1:2, :]).astype(BF16)
    n1_ref[...] = n1
    for third in range(3):
        cols = pl.ds(third * width, width)
        part = nn(n1, mrg_ref[:, cols])
        if third != 1:
            part = part + vec_ref[2 + third // 2:3 + third // 2, :]
        part = part.astype(BF16)
        pk_s[:, cols] = part
        if third:
            kv_ref[:, pl.ds((third - 1) * width, width)] = part
    lane = lax.broadcasted_iota(jnp.int32, (seq, LANES), 1)
    low = lane < HALF
    in_half = lane % HALF
    dead = dead_ref[...]
    ones = jnp.ones((seq, LANES), BF16)

    def pair(p, _):
        qcols = pl.ds(pl.multiple_of(p * LANES, LANES), LANES)
        kcols = pl.ds(pl.multiple_of(width + p * LANES, LANES), LANES)
        vcols = pl.ds(pl.multiple_of(2 * width + p * LANES, LANES), LANES)
        q = pk_s[:, qcols] * jnp.array(0.125, BF16)
        k = pk_s[:, kcols]
        v = pk_s[:, vcols]
        outs = []
        for side in range(2):
            mine = low if side == 0 else ~low
            qs = jnp.where(mine, q, jnp.where(in_half == 0, 1.0, 0.0).astype(BF16))
            ks = jnp.where(mine, k, dead)
            vs = jnp.where(mine, v, ones)
            s = nt(qs, ks)
            top = jnp.max(s, -1, keepdims=True)
            e = jnp.exp(s - top).astype(BF16)
            o = nn(e, vs)
            swapped = pltpu.roll(o, HALF, 1)
            outs.append(o / swapped)
            lse = top + jnp.log(jnp.where(mine, swapped, o))
            hi = (-lse).astype(BF16)
            rest = -lse - hi.astype(F32)
            mid_part = rest.astype(BF16)
            lo = (rest - mid_part.astype(F32)).astype(BF16)
            extra = jnp.where(in_half == 0, 1.0, 0.0).astype(BF16)
            extra = jnp.where(in_half == 1, hi, extra)
            extra = jnp.where(in_half == 2, mid_part, extra)
            extra = jnp.where(in_half == 3, lo, extra)
            qa_ref[2 * p + side] = jnp.where(mine, q, extra)
        mix_ref[:, qcols] = jnp.where(low, outs[0], outs[1]).astype(BF16)
        return 0

    lax.fori_loop(0, pairs, pair, 0)
    mid_ref[...] = xc + nn(mix_ref[...], out_ref[...]) + vec_ref[4:5, :]


def attn_fwd(xc, dead, merged, output, vec, clips, heads):
    total, width = xc.shape
    seq = total // clips
    whole = lambda c: (0, 0)
    row = lambda c: (c, 0)
    return pl.pallas_call(
        functools.partial(attn_fwd_kernel, heads),
        grid=(clips,),
        in_specs=[
            pl.BlockSpec((seq, width), row),
            pl.BlockSpec((seq, LANES), row),
            pl.BlockSpec(merged.shape, whole),
            pl.BlockSpec((width, width), whole),
            pl.BlockSpec(vec.shape, whole),
        ],
        out_specs=[
            pl.BlockSpec((seq, width), row),
            pl.BlockSpec((heads, seq, LANES), lambda c: (0, c, 0)),
            pl.BlockSpec((seq, 2 * width), row),
            pl.BlockSpec((seq, width), row),
            pl.BlockSpec((seq, width), row),
        ],
        out_shape=[
            jax.ShapeDtypeStruct((total, width), BF16),
            jax.ShapeDtypeStruct((heads, total, LANES), BF16),
            jax.ShapeDtypeStruct((total, 2 * width), BF16),
            jax.ShapeDtypeStruct((total, width), BF16),
            jax.ShapeDtypeStruct((total, width), F32),
        ],
        scratch_shapes=[pltpu.VMEM((seq, 3 * width), BF16)],
        compiler_params=pltpu.CompilerParams(
            dimension_semantics=("arbitrary",), vmem_limit_bytes=LIMIT),
        name="attn_fwd",
    )(xc, dead, merged, output, vec)


def attn_bwd_kernel(heads, xc_ref, cot_ref, dmid_ref, dead_ref, n1_ref, qa_ref, kv_ref, mix_ref,
                    mrg_ref, out_ref, vec_ref, early_ref,
                    dlt_ref, gm_ref, go_ref,
                    dm_s, dp_s, am_s, ao_s, sums_ref):
    c = pl.program_id(0)
    n = pl.num_programs(0)
    seq, width = xc_ref.shape
    pairs = heads // 2

    @pl.when(c == 0)
    def _():
        sums_ref[...] = early_ref[...]
        am_s[...] = jnp.zeros_like(am_s)
        ao_s[...] = jnp.zeros_like(ao_s)

    d_one = dmid_ref[...].astype(BF16)
    dm_s[...] = nt(d_one, out_ref[...]).astype(BF16)
    ao_s[...] += tn(mix_ref[...], d_one)
    sums_ref[4:5, :] += jnp.sum(d_one.astype(F32), 0, keepdims=True)

    lane = lax.broadcasted_iota(jnp.int32, (seq, LANES), 1)
    low = lane < HALF
    in_half = lane % HALF
    dead = dead_ref[...]
    vone = jnp.where(in_half < 2, 1.0, 0.0).astype(BF16)

    def pair(p, _):
        qcols = pl.ds(pl.multiple_of(p * LANES, LANES), LANES)
        kcols = pl.ds(pl.multiple_of(width + p * LANES, LANES), LANES)
        vcols = pl.ds(pl.multiple_of(2 * width + p * LANES, LANES), LANES)
        k = kv_ref[:, qcols]
        v = kv_ref[:, kcols]
        dm = dm_s[:, qcols]
        prod = dm.astype(F32) * mix_ref[:, qcols].astype(F32)
        k_t = jnp.transpose(k)
        dks, dvs, dqs = [], [], []
        for side in range(2):
            mine = low if side == 0 else ~low
            qa = qa_ref[2 * p + side]
            ka = jnp.where(mine, k, dead)
            va = jnp.where(mine, v, vone)
            dd = -jnp.sum(jnp.where(mine, prod, 0.0), -1, keepdims=True)
            hi = dd.astype(BF16)
            lo = (dd - hi.astype(F32)).astype(BF16)
            da = jnp.where(mine, dm, jnp.where(in_half == 0, hi, lo))
            p_t = jnp.exp(nt(ka, qa))
            ds_t = (p_t * nt(va, da)).astype(BF16)
            dvs.append(nn(p_t.astype(BF16), da))
            dks.append(nn(ds_t, qa))
            dqs.append(nn(k_t[side * HALF:(side + 1) * HALF, :], ds_t))
        dq = jnp.transpose(jnp.concatenate(dqs, 0)) * 0.125
        dk = jnp.where(low, dks[0], dks[1])
        dv = jnp.where(low, dvs[0], dvs[1])
        sums_ref[2:3, qcols] += jnp.sum(dq, 0, keepdims=True)
        sums_ref[3:4, qcols] += jnp.sum(dv, 0, keepdims=True)
        dp_s[:, qcols] = dq.astype(BF16)
        dp_s[:, kcols] = dk.astype(BF16)
        dp_s[:, vcols] = dv.astype(BF16)
        return 0

    lax.fori_loop(0, pairs, pair, 0)
    dp = dp_s[...]
    am_s[...] += tn(n1_ref[...], dp)
    dy = nt(dp, mrg_ref[:, :3 * width])
    xhat, r = norm_stats(xc_ref[...].astype(F32))
    sums_ref[0:1, :] += jnp.sum(dy * xhat, 0, keepdims=True)
    sums_ref[1:2, :] += jnp.sum(dy, 0, keepdims=True)
    dlt_ref[...] = ((dmid_ref[...] - cot_ref[...].astype(F32))
                    + norm_back(xhat, r, dy, vec_ref[0:1, :])).astype(BF16)

    @pl.when(c == n - 1)
    def _():
        gm_ref[:, :3 * width] = am_s[...].astype(gm_ref.dtype)
        columns = jnp.transpose(sums_ref[...])
        gm_ref[:, 3 * width:] = jnp.concatenate(
            [columns, jnp.zeros((width, LANES - columns.shape[1]), F32)], 1).astype(gm_ref.dtype)
        go_ref[...] = ao_s[...].astype(go_ref.dtype)


def attn_bwd(xc, cot, dmid, dead, n1, qa, kv, mix, merged, output, vec, early, clips, heads):
    total, width = xc.shape
    seq = total // clips
    whole = lambda c: (0, 0)
    row = lambda c: (c, 0)
    return pl.pallas_call(
        functools.partial(attn_bwd_kernel, heads),
        grid=(clips,),
        in_specs=[
            pl.BlockSpec((seq, width), row),
            pl.BlockSpec((seq, width), row),
            pl.BlockSpec((seq, width), row),
            pl.BlockSpec((seq, LANES), row),
            pl.BlockSpec((seq, width), row),
            pl.BlockSpec((heads, seq, LANES), lambda c: (0, c, 0)),
            pl.BlockSpec((seq, 2 * width), row),
            pl.BlockSpec((seq, width), row),
            pl.BlockSpec(merged.shape, whole),
            pl.BlockSpec((width, width), whole),
            pl.BlockSpec(vec.shape, whole),
            pl.BlockSpec(early.shape, whole),
        ],
        out_specs=[
            pl.BlockSpec((seq, width), row),
            pl.BlockSpec(merged.shape, whole),
            pl.BlockSpec((width, width), whole),
        ],
        out_shape=[
            jax.ShapeDtypeStruct((total, width), BF16),
            jax.ShapeDtypeStruct(merged.shape, BF16),
            jax.ShapeDtypeStruct((width, width), BF16),
        ],
        scratch_shapes=[
            pltpu.VMEM((seq, width), BF16),
            pltpu.VMEM((seq, 3 * width), BF16),
            pltpu.VMEM((width, 3 * width), F32),
            pltpu.VMEM((width, width), F32),
            pltpu.VMEM((16, width), F32),
        ],
        compiler_params=pltpu.CompilerParams(
            dimension_semantics=("arbitrary",), vmem_limit_bytes=LIMIT),
        name="attn_bwd",
    )(xc, cot, dmid, dead, n1, qa, kv, mix, merged, output, vec, early)


def adamw(weight, first_old, second_old, grad_share, factor, step_rate, decay_rate):
    clipped = grad_share * factor
    momentum = BETA_ONE * first_old + (1.0 - BETA_ONE) * clipped
    variance = BETA_TWO * second_old + (1.0 - BETA_TWO) * clipped * clipped
    mean_hat = momentum / (1.0 - BETA_ONE**STEP)
    var_hat = variance / (1.0 - BETA_TWO**STEP)
    updated = weight - step_rate * (mean_hat / (jnp.sqrt(var_hat) + ADAM_EPS) + decay_rate * weight)
    return (clipped, momentum, variance, updated)


def key_columns(kept_time, kept_bands, blocks, own, segment, padded):
    clips = kept_time.shape[0] // blocks
    kept_time = lax.dynamic_slice_in_dim(kept_time, own * clips, clips)
    kept_bands = lax.dynamic_slice_in_dim(kept_bands, own * clips, clips)
    columns = kept_time.shape[1] // blocks
    patches = kept_time.reshape(clips, blocks, columns, 1) * kept_bands[:, None, None, :]
    patches = patches.reshape(clips, blocks, columns * kept_bands.shape[1])
    leading = (jnp.arange(blocks, dtype=jnp.int32) == 0).astype(jnp.int32)
    special = jnp.broadcast_to(leading[None, :, None], (clips, blocks, segment - patches.shape[2]))
    live = jnp.concatenate([special, patches, jnp.zeros((clips, blocks, padded - segment), jnp.int32)], 2)
    bias = jnp.where(live > 0, 0.0, -1e30).reshape(-1, 1)
    lane = jnp.arange(LANES, dtype=jnp.int32)[None, :] % HALF
    return jnp.where(lane == 0, bias, jnp.where(lane < 4, 1.0, 0.0)).astype(BF16)


def shards(
    tokens, kept_time, kept_bands, cotangent,
    weight_merged, weight_output, weight_expand, weight_shrink, vectors,
    first_merged, first_output, first_expand, first_shrink, first_vectors,
    second_merged, second_output, second_expand, second_shrink, second_vectors,
):
    clip_count, segment, width = tokens.shape
    blocks = lax.axis_size("blk")
    own = lax.axis_index("blk")
    clips = clip_count // blocks
    padded = -(-segment // 16) * 16
    total = clips * blocks * padded
    axes = ("dp", "blk")

    def to_clips(values):
        values = jnp.pad(values.astype(BF16), ((0, 0), (0, padded - segment), (0, 0)))
        return lax.all_to_all(values, "blk", 0, 1, tiled=True).reshape(total, width)

    def to_home(values):
        values = values.reshape(clips, blocks * padded, width)
        return lax.all_to_all(values, "blk", 1, 0, tiled=True)[:, :segment].astype(F32)

    columns = jnp.pad(vectors.T, ((0, 0), (0, LANES - vectors.shape[0])))
    merged = lax.all_gather(
        jnp.concatenate([weight_merged, columns], 1).astype(BF16), axes, axis=0, tiled=True)
    wide = lax.all_gather(
        jnp.concatenate([weight_output, weight_expand], 1).astype(BF16), axes, axis=0, tiled=True)
    shrink = lax.all_gather(weight_shrink.astype(BF16), axes, axis=0, tiled=True)
    vec = merged[:, 3 * width:3 * width + vectors.shape[0]].T.astype(F32)
    xc = to_clips(tokens - jnp.mean(tokens, -1, keepdims=True))
    cot = to_clips(cotangent)
    dead = key_columns(kept_time, kept_bands, blocks, own, segment, padded)
    n1, qa, kv, mix, mid = attn_fwd(xc, dead, merged, wide, vec, clips, HEADS)
    act, dmid, grad_expand, grad_shrink, early = ffn(mid, xc, cot, wide, shrink, vec, blocks * padded)
    dlt, grad_merged, grad_output = attn_bwd(
        xc, cot, dmid, dead, n1, qa, kv, mix, merged, wide, vec, early, clips, HEADS)
    activations = tokens + to_home(act)
    token_grads = cotangent + to_home(dlt)
    scattered = [
        lax.psum_scatter(grad, axes, scatter_dimension=0, tiled=True).astype(F32)
        for grad in (grad_merged, grad_output, grad_expand, grad_shrink)
    ]
    shares = (
        scattered[0][:, :3 * width], scattered[1], scattered[2], scattered[3],
        scattered[0][:, 3 * width:3 * width + vectors.shape[0]].T,
    )
    squares = sum(jnp.sum(share_part * share_part) for share_part in shares)
    gradient_norm = jnp.sqrt(lax.psum(squares, axes))
    factor = CLIP_LIMIT / jnp.maximum(gradient_norm, CLIP_LIMIT)
    weights = (weight_merged, weight_output, weight_expand, weight_shrink, vectors)
    firsts = (first_merged, first_output, first_expand, first_shrink, first_vectors)
    seconds = (second_merged, second_output, second_expand, second_shrink, second_vectors)
    rates = (MATRIX_RATE, MATRIX_RATE, MATRIX_RATE, MATRIX_RATE, VECTOR_RATE)
    decays = (MATRIX_DECAY, MATRIX_DECAY, MATRIX_DECAY, MATRIX_DECAY, 0.0)
    steps_out = [
        adamw(*parts, factor, rate, decay)
        for *parts, rate, decay in zip(weights, firsts, seconds, shares, rates, decays)
    ]
    return (activations, token_grads, gradient_norm) + tuple(
        steps_out[index][kind] for kind in range(4) for index in range(5))


def solution(mesh):
    return jax.shard_map(
        shards,
        mesh=mesh,
        in_specs=(
            P("dp", "blk", None),
            P("dp", None),
            P("dp", None),
            P("dp", "blk", None),
            P(("dp", "blk"), None),
            P(("dp", "blk"), None),
            P(("dp", "blk"), None),
            P(("dp", "blk"), None),
            P(None, ("dp", "blk")),
            P(("dp", "blk"), None),
            P(("dp", "blk"), None),
            P(("dp", "blk"), None),
            P(("dp", "blk"), None),
            P(None, ("dp", "blk")),
            P(("dp", "blk"), None),
            P(("dp", "blk"), None),
            P(("dp", "blk"), None),
            P(("dp", "blk"), None),
            P(None, ("dp", "blk")),
        ),
        out_specs=(
            P("dp", "blk", None),
            P("dp", "blk", None),
            P(),
            P(("dp", "blk"), None),
            P(("dp", "blk"), None),
            P(("dp", "blk"), None),
            P(("dp", "blk"), None),
            P(None, ("dp", "blk")),
            P(("dp", "blk"), None),
            P(("dp", "blk"), None),
            P(("dp", "blk"), None),
            P(("dp", "blk"), None),
            P(None, ("dp", "blk")),
            P(("dp", "blk"), None),
            P(("dp", "blk"), None),
            P(("dp", "blk"), None),
            P(("dp", "blk"), None),
            P(None, ("dp", "blk")),
            P(("dp", "blk"), None),
            P(("dp", "blk"), None),
            P(("dp", "blk"), None),
            P(("dp", "blk"), None),
            P(None, ("dp", "blk")),
        ),
        check_vma=False,
    )
```

time: 1520 us -> 852 us (0.56)
  matrix products: 302 us -> 0 us
  waiting for transfers between devices: 783 us -> 521 us
  Pallas kernels: 0 us -> 169 us
  local copies, waits for them, and re-layouts: 178 us -> 41.6 us
  blocking collectives: 124 us -> 40.1 us
  other arithmetic: 98.7 us -> 41.4 us
  starting transfers between devices: 0.59 us -> 17.8 us
    dot_general x18 -> x0, matrix products: 302 us -> none  [the longest x4 55.7 us: against(): lax.dot_general(grad_rows, matrix, (((1,), (1,)), ((), ())), preferred_el...]
    pallas_call x0 -> x3, Pallas kernels: none -> 169 us  [the longest x1 77.5 us: ffn(): pl.pallas_call(ffn_kernel, grid=(nf, ni), in_specs=[pl.BlockSpec((rows, w...]
    unnamed x11 -> x8, waiting for transfers between devices: 255 us -> 97.7 us
    reduce_scatter x4 -> x3, waiting for transfers between devices: 379 us -> 255 us  [shards(): lax.psum_scatter(grad, axes, scatter_dimension=0, tiled=True).astype(F32)]
    all_to_all x0 -> x4, waiting for transfers between devices: none -> 88.3 us  [the longest x2 56.7 us: to_clips(): return lax.all_to_all(values, 'blk', 0, 1, tiled=True).reshape(total, width)]
    all_gather x5 -> x3, waiting for transfers between devices: 148 us -> 80 us  [the longest x1 49.9 us: shards(): lax.all_gather(jnp.concatenate([weight_output, weight_expand], 1).astype(...]
    all_gather x1 -> x0, blocking collectives: 43.7 us -> none  [shards(): lax.all_gather(vectors.astype(jnp.bfloat16), ('dp', 'blk'), axis=1, tiled...]
    unnamed x1 -> x0, blocking collectives: 40.1 us -> none
  transfers between devices with their start and end apart: 10 -> 11, of which waited for: 9 -> 9; matrix products, arithmetic and copies ran while one was open for 24% -> 6% of each run, Pallas kernels for 0% -> 4%
where the time goes in v1:
time: 852 us; the launch traced here: 850 us
  waiting for transfers between devices  521 us (61%)
  Pallas kernels  169 us (20%)
  local copies, waits for them, and re-layouts  41.6 us (5%)
  other arithmetic  41.4 us (5%)
  blocking collectives  40.1 us (5%)
  between operations  19.5 us (2%)
  starting transfers between devices  17.8 us (2%)
    reduce_scatter x3, waiting for transfers between devices, shards(): lax.psum_scatter(grad, axes, scatter_dimension=0, tiled=True).astype(F32)  255 us
    unnamed x8, waiting for transfers between devices  97.7 us
    pallas_call x1, Pallas kernels, ffn(): pl.pallas_call(ffn_kernel, grid=(nf, ni), in_specs=[pl.BlockSpec((rows, w...  77.5 us
    all_to_all x2, waiting for transfers between devices, to_clips(): return lax.all_to_all(values, 'blk', 0, 1, tiled=True).reshape(total, width)  56.7 us
    pallas_call x1, Pallas kernels, attn_bwd(): pl.pallas_call(functools.partial(attn_bwd_kernel, heads), grid=(clips,),...  55.7 us
    all_gather x1, waiting for transfers between devices, shards(): lax.all_gather(jnp.concatenate([weight_output, weight_expand], 1).astype(...  49.9 us
    psum x1, blocking collectives, shards(): gradient_norm = jnp.sqrt(lax.psum(squares, axes))  40.1 us
    pallas_call x1, Pallas kernels, attn_fwd(): pl.pallas_call(functools.partial(attn_fwd_kernel, heads), grid=(clips,),...  36.1 us
  transfers between devices with their start and end apart: 11, of which 9 were waited for; matrix products, arithmetic and copies ran while one was open for 6% of the time, Pallas kernels for 4%

profile of v1, /device:TPU:0, one launch (start us, length us, event | category | flops | bytes accessed | tf_op | source)
XLA Modules:
  0.0 850.4 jit_solution(1804012248149749763)
XLA Ops:
  14.0 2.6 reduce_sum.54
  16.7 2.7 subtract_convert_fusion
  21.0 4.2 all-to-all-start
  25.2 2.6 convert_element_type.54
  29.4 27.6 %all-to-all-done = bf16[12,128,768]{2,1,0:T(8,128)(2,1)S(1)} async-done(((bf16[12,128,768]{2,1,0:T(8,128)(2,1)}), bf16[12,128,768]{2,1,0:T(8,128)(2,1)S(1)}, u32[]{:S(2)}, u32[]{:S(2)}) %all-to-all-start) | async-done | bytes 2359328 | tf_op jit(solution)/shard_map/all_to_all | solution.py:437
  57.0 4.7 all-to-all-start.1
  65.8 29.1 %all-to-all-done.1 = bf16[12,128,768]{2,1,0:T(8,128)(2,1)} async-done(((bf16[12,128,768]{2,1,0:T(8,128)(2,1)}), bf16[12,128,768]{2,1,0:T(8,128)(2,1)}, u32[]{:S(2)}, u32[]{:S(2)}) %all-to-all-start.1) | async-done | bytes 2359328 | tf_op jit(solution)/shard_map/all_to_all | solution.py:437
  94.9 3.2 copy.91
  99.8 49.9 %all-gather.6.cloned.1.call-done.out_ref.exp_ref = bf16[768,3840]{1,0:T(8,128)(2,1)} async-done(((bf16[24,3840]{1,0:T(8,128)(2,1)}), bf16[768,3840]{1,0:T(8,128)(2,1)}) %all-gather.6.cloned.1.call-update) | async-done | bytes 5898256 | tf_op jit(solution)/shard_map/all_gather | solution.py:446
  149.8 36.1 %attn_fwd.1 = (bf16[1536,768]{1,0:T(8,128)(2,1)}, bf16[12,1536,128]{2,1,0:T(8,128)(2,1)}, bf16[1536,1536]{1,0:T(8,128)(2,1)}, bf16[1536,768]{1,0:T(8,128)(2,1)}, f32[1536,768]{1,0:T(8,128)}) custom-call(bf16[1536,768]{1,0:T(8,128)(2,1)} %bitcast.27, bf16[1536,128]{1,0:T(8,128)(2,1)} %select_convert_fusion.dead_ref, ...), custom_call_target="tpu_custom_call" | custom-call | tf_op jit(solution)/shard_map/attn_fwd/pallas_call | solution.py:241
  185.8 30.1 %all-gather.8.cloned.1.call-done.shr_ref = bf16[3072,768]{1,0:T(8,128)(2,1)} async-done(((bf16[96,768]{1,0:T(8,128)(2,1)}), bf16[3072,768]{1,0:T(8,128)(2,1)}) %all-gather.8.cloned.1.call-update) | async-done | bytes 4718608 | tf_op jit(solution)/shard_map/all_gather | solution.py:448
  215.9 77.5 %ffn.1 = (bf16[1536,768]{1,0:T(8,128)(2,1)}, f32[1536,768]{1,0:T(8,128)}, bf16[768,3072]{1,0:T(8,128)(2,1)}, bf16[3072,768]{1,0:T(8,128)(2,1)}, f32[16,768]{1,0:T(8,128)}) custom-call(f32[1536,768]{1,0:T(8,128)} %get-tuple-element.36.mid_ref, bf16[1536,768]{1,0:T(8,128)(2,1)} %bitcast.28, bf16[1536,768]{1,0:T(8,128)(2,1)} %bitcast.30, ...), custom_call_target="tpu_custom_call" | custom-call | tf_op jit(solution)/shard_map/ffn/pallas_call | solution.py:138
  293.4 55.7 %attn_bwd.1 = (bf16[1536,768]{1,0:T(8,128)(2,1)}, bf16[768,2432]{1,0:T(8,128)(2,1)}, bf16[768,768]{1,0:T(8,128)(2,1)}) custom-call(bf16[1536,768]{1,0:T(8,128)(2,1)} %bitcast.29, bf16[1536,768]{1,0:T(8,128)(2,1)} %bitcast.31, f32[1536,768]{1,0:T(8,128)} %get-tuple-element.38.dmid_ref, bf16[1536,128]{1,0:T(8,128)(2,1)} %select_convert_fusion.dead_ref, ...), custom_call_target="tpu_custom_call" | custom-call | tf_op jit(solution)/shard_map/attn_bwd/pallas_call | solution.py:356
  352.0 3.7 copy.94
  355.7 3.7 all-to-all-start.3
  359.4 5.4 copy.92
  364.8 31.5 %all-to-all-done.3 = bf16[3,512,768]{2,0,1:T(4,128)(2,1)S(1)} async-done(((bf16[3,512,768]{2,0,1:T(4,128)(2,1)}), bf16[3,512,768]{2,0,1:T(4,128)(2,1)S(1)}, u32[]{:S(2)}, u32[]{:S(2)}) %all-to-all-start.3) | async-done | bytes 2359328 | tf_op jit(solution)/shard_map/all_to_all | solution.py:441
  396.3 4.9 all-to-all-start.2
  402.6 2.4 copy.97
  405.0 2.4 copy.98
  407.4 37.3 %reduce-scatter.7.cloned.1.call-done = bf16[24,768]{1,0:T(8,128)(2,1)} async-done(((bf16[768,768]{1,0:T(8,128)(2,1)}), bf16[24,768]{1,0:T(8,128)(2,1)}) %reduce-scatter.7.cloned.1.call-update) | async-done | bytes 36880 | tf_op jit(solution)/shard_map/reduce_scatter | solution.py:460
  447.9 3.7 copy.93
  451.6 95.9 %reduce-scatter.13.cloned.1.call-done = bf16[24,2432]{1,0:T(8,128)(2,1)} async-done(((bf16[768,2432]{1,0:T(8,128)(2,1)}), bf16[24,2432]{1,0:T(8,128)(2,1)}) %reduce-scatter.13.cloned.1.call-update) | async-done | bytes 116752
  551.6 107.2 %reduce-scatter.9.cloned.1.call-done = bf16[24,3072]{1,0:T(8,128)(2,1)} async-done(((bf16[768,3072]{1,0:T(8,128)(2,1)}), bf16[24,3072]{1,0:T(8,128)(2,1)}) %reduce-scatter.9.cloned.1.call-update) | async-done | bytes 147472 | tf_op jit(solution)/shard_map/reduce_scatter | solution.py:460
  661.1 110.3 %reduce-scatter.11.cloned.1.call-done = bf16[96,768]{1,0:T(8,128)(2,1)} async-done(((bf16[3072,768]{1,0:T(8,128)(2,1)}), bf16[96,768]{1,0:T(8,128)(2,1)}) %reduce-scatter.11.cloned.1.call-update) | async-done | bytes 147472 | tf_op jit(solution)/shard_map/reduce_scatter | solution.py:460
  774.2 10.4 %convert_add_fusion = (f32[12,122,768]{2,1,0:T(8,128)}, f32[12,122,768]{2,1,0:T(8,128)}) fusion(f32[12,122,768]{2,1,0:T(8,128)} %param.22, bf16[12,128,768]{2,1,0:T(8,128)(2,1)} %bitcast.33, f32[12,122,768]{2,1,0:T(8,128)} %param.19, bf16[12,128,768]{2,1,0:T(8,128)(2,1)} %bitcast.34), kind=kLoop, calls=%fused_computation | loop fusion | flops 4497408 | bytes 22487040 | tf_op jit(solution)/shard_map/add | solution.py:458
  784.6 40.1 %psum.7 = f32[]{:T(128)} all-reduce(f32[]{:T(128)S(6)} %add.136), channel_id=1, replica_groups=mesh['dp'=8,'blk'=4] {'dp','blk'}, use_global_device_ids=true, to_apply=%region_10.11 | all-reduce | flops 1 | bytes 8 | tf_op jit(solution)/shard_map/psum | solution.py:468
  825.4 4.1 multiply_subtract_fusion
  829.6 2.4 copy.101
  832.0 2.4 copy.102
  834.3 2.4 copy.103
  838.4 2.1 multiply_subtract_fusion.1
  (99 shorter events, 32.7 us)
Async XLA Ops:
  7.2 54.6 %copy-start = (s32[12,48]{1,0:T(8,128)S(1)}, s32[12,48]{1,0:T(8,128)}, u32[]{:S(2)}) copy-start(s32[12,48]{1,0:T(8,128)} %param.20) | copy-start | bytes 6916
  7.2 90.9 %all-gather.4.cloned.1.call-start = ((), (), s32[]{:S(2)}) async-start(), calls=%async_computation.8 | async-start | bytes 3852288 | tf_op jit(solution)/shard_map/all_gather | solution.py:444
  9.7 140.1 %all-gather.6.cloned.1.call-start = ((), (), s32[]{:S(2)}) async-start(), calls=%async_computation.9 | async-start | bytes 6082560 | tf_op jit(solution)/shard_map/all_gather | solution.py:446
  12.3 203.6 %all-gather.8.cloned.1.call-start = ((), (), s32[]{:S(2)}) async-start(), calls=%async_computation.10 | async-start | bytes 4866048 | tf_op jit(solution)/shard_map/all_gather | solution.py:448
  21.0 36.1 %all-to-all-start = ((bf16[12,128,768]{2,1,0:T(8,128)(2,1)}), bf16[12,128,768]{2,1,0:T(8,128)(2,1)S(1)}, u32[]{:S(2)}, u32[]{:S(2)}) async-start(bf16[12,128,768]{2,1,0:T(8,128)(2,1)} %pad.12), calls=%async_computation | async-start | bytes 4718592 | tf_op jit(solution)/shard_map/all_to_all | solution.py:437
  57.0 37.9 %all-to-all-start.1 = ((bf16[12,128,768]{2,1,0:T(8,128)(2,1)}), bf16[12,128,768]{2,1,0:T(8,128)(2,1)}, u32[]{:S(2)}, u32[]{:S(2)}) async-start(bf16[12,128,768]{2,1,0:T(8,128)(2,1)} %pad.14), calls=%async_computation.1 | async-start | bytes 4718592 | tf_op jit(solution)/shard_map/all_to_all | solution.py:437
  61.7 382.9 %reduce-scatter.7.cloned.1.call-start = ((), (), s32[]{:S(2)}) async-start(), calls=%async_computation.11 | async-start | bytes 1216512 | tf_op jit(solution)/shard_map/reduce_scatter | solution.py:460
  349.1 198.4 %reduce-scatter.13.cloned.1.call-start = ((), (), s32[]{:S(2)}) async-start(), calls=%async_computation.14 | async-start | bytes 3852288
  349.7 309.1 %reduce-scatter.9.cloned.1.call-start = ((), (), s32[]{:S(2)}) async-start(), calls=%async_computation.12 | async-start | bytes 4866048 | tf_op jit(solution)/shard_map/reduce_scatter | solution.py:460
  350.3 421.1 %reduce-scatter.11.cloned.1.call-start = ((), (), s32[]{:S(2)}) async-start(), calls=%async_computation.13 | async-start | bytes 4866048 | tf_op jit(solution)/shard_map/reduce_scatter | solution.py:460
  350.3 1.7 copy-start.4
  355.7 40.6 %all-to-all-start.3 = ((bf16[3,512,768]{2,0,1:T(4,128)(2,1)}), bf16[3,512,768]{2,0,1:T(4,128)(2,1)S(1)}, u32[]{:S(2)}, u32[]{:S(2)}) async-start(bf16[3,512,768]{2,0,1:T(4,128)(2,1)} %copy.94), calls=%async_computation.3 | async-start | bytes 6291456 | tf_op jit(solution)/shard_map/all_to_all | solution.py:441
  364.8 36.5 %copy-start.7 = (f32[24,2304]{1,0:T(8,128)S(1)}, f32[24,2304]{1,0:T(8,128)}, u32[]{:S(2)}) copy-start(f32[24,2304]{1,0:T(8,128)} %param.23) | copy-start | bytes 663556
  396.3 51.6 %all-to-all-start.2 = ((bf16[3,512,768]{2,0,1:T(4,128)(2,1)}), bf16[3,512,768]{2,0,1:T(4,128)(2,1)}, u32[]{:S(2)}, u32[]{:S(2)}) async-start(bf16[3,512,768]{2,0,1:T(4,128)(2,1)} %copy.92), calls=%async_computation.2 | async-start | bytes 6291456 | tf_op jit(solution)/shard_map/all_to_all | solution.py:441
  774.2 51.2 %copy-start.2 = (f32[24,2304]{0,1:T(8,128)S(1)}, f32[24,2304]{0,1:T(8,128)}, u32[]{:S(2)}) copy-start(f32[24,2304]{0,1:T(8,128)} %copy.100) | copy-start | bytes 663556
  829.6 7.1 copy-start.3
  831.9 5.8 copy-start.16
  832.0 5.8 copy-start.17
  832.0 5.8 copy-start.18
  832.0 6.5 copy-start.5
  832.0 6.5 copy-start.9
  834.3 6.2 copy-start.6
  834.3 6.2 copy-start.8
  837.7 2.9 copy-start.10
  837.7 2.9 copy-start.11
  837.7 3.9 copy-start.12
  837.7 3.9 copy-start.13
  837.8 3.9 copy-start.14
  837.8 3.9 copy-start.15
  837.8 4.6 copy-start.1
Sparse Core Ops, SparseCore 0:
  11.5 67.4 all-gather.3
  82.5 67.1 all-gather.5
  153.2 62.6 all-gather.7
  349.2 95.3 reduce-scatter.6
  450.2 97.2 reduce-scatter.12
  552.8 105.9 reduce-scatter.8
  665.2 106.0 reduce-scatter.10

commit v2 on v1

--- a/solution.py
+++ b/solution.py
@@ -21,6 +21,7 @@
 HALF = 64
 LANES = 128
 LIMIT = 60 * 1024 * 1024
+MESH = pl.DeviceIdType.MESH
 
 
 def nn(a, b):
@@ -393,14 +394,281 @@
     )(xc, cot, dmid, dead, n1, qa, kv, mix, merged, output, vec, early)
 
 
-def adamw(weight, first_old, second_old, grad_share, factor, step_rate, decay_rate):
-    clipped = grad_share * factor
-    momentum = BETA_ONE * first_old + (1.0 - BETA_ONE) * clipped
-    variance = BETA_TWO * second_old + (1.0 - BETA_TWO) * clipped * clipped
-    mean_hat = momentum / (1.0 - BETA_ONE**STEP)
-    var_hat = variance / (1.0 - BETA_TWO**STEP)
-    updated = weight - step_rate * (mean_hat / (jnp.sqrt(var_hat) + ADAM_EPS) + decay_rate * weight)
-    return (clipped, momentum, variance, updated)
+def bits_of(size):
+    return size.bit_length() - 1
+
+
+class Cube:
+    def __init__(self, dp, blk):
+        self.sizes = (dp, blk)
+        self.n_dp, self.n_blk = bits_of(dp), bits_of(blk)
+        self.count = self.n_dp + self.n_blk
+        self.core = self.count - 1
+        self.cross = self.count - 2
+
+    def bind(self):
+        self.at_dp, self.at_blk = lax.axis_index("dp"), lax.axis_index("blk")
+        self.mine = [lax.rem(self.at_dp // (1 << (self.n_dp - 1 - k)), 2) for k in range(self.n_dp)]
+        self.mine += [lax.rem(self.at_blk // (1 << (self.n_blk - 1 - k)), 2) for k in range(self.n_blk)]
+        return self
+
+    def partner(self, bit):
+        if bit < self.n_dp:
+            step = 1 << (self.n_dp - 1 - bit)
+            return (self.at_dp + step - 2 * step * self.mine[bit], self.at_blk)
+        step = 1 << (self.count - 1 - bit)
+        return (self.at_dp, self.at_blk + step - 2 * step * self.mine[bit])
+
+    def row_peer(self, offset):
+        return (self.at_dp, lax.rem(self.at_blk + offset, self.sizes[1]))
+
+    def column_peer(self, offset):
+        return (lax.rem(self.at_dp + offset, self.sizes[0]), self.at_blk)
+
+    def barrier(self):
+        sem = pltpu.get_barrier_semaphore()
+        others = [self.row_peer(k) for k in range(1, self.sizes[1])]
+        others += [self.column_peer(k) for k in range(1, self.sizes[0])]
+        for other in others:
+            pl.semaphore_signal(sem, inc=1, device_id=other, device_id_type=MESH)
+        pl.semaphore_wait(sem, len(others))
+
+    def order(self, letters):
+        far = [bit for bit in range(self.n_dp - 1)]
+        near = {"Y": [self.n_dp - 1], "X": [k for k in range(self.n_dp, self.count - 1)],
+                "a": far[-1:], "b": far[:-1]}
+        return [bit for letter in letters for bit in near[letter]]
+
+
+def remote(src, dst, send, recv, device):
+    return pltpu.make_async_remote_copy(
+        src_ref=src, dst_ref=dst, send_sem=send, recv_sem=recv, device_id=device, device_id_type=MESH)
+
+
+class Gather:
+    def __init__(self, cube, src, dst, cols, order, send, recv):
+        self.cube, self.src, self.dst, self.cols = cube, src, dst, cols
+        self.order = list(order) + [cube.core]
+        self.send, self.recv, self.step = send, recv, 0
+
+    def start(self):
+        cube, s = self.cube, self.step
+        sel = tuple(slice(None) if bit in self.order[:s] else cube.mine[bit] for bit in range(cube.count))
+        there = self.dst.at[sel + (slice(None), self.cols)]
+        here = self.src.at[:, self.cols] if s == 0 else there
+        self.copy = remote(here, there, self.send.at[s], self.recv.at[s], cube.partner(self.order[s]))
+        self.copy.start()
+
+    def advance(self):
+        self.copy.wait()
+        self.step += 1
+        if self.step < len(self.order):
+            self.start()
+
+
+class Reduce:
+    def __init__(self, cube, src, cols, order, held, landed, out, out_cols, send, recv, local):
+        self.cube, self.src, self.cols, self.held, self.landed = cube, src, cols, held, landed
+        self.order = [cube.core] + list(order)
+        self.out, self.out_cols = out, out_cols
+        self.send, self.recv, self.local, self.step = send, recv, local, 0
+
+    def part(self, kept):
+        cube, s = self.cube, self.step
+        sel = []
+        for bit in range(cube.count):
+            if bit in self.order[:s]:
+                pick = cube.mine[bit]
+            elif bit == self.order[s]:
+                pick = cube.mine[bit] if kept else 1 - cube.mine[bit]
+            else:
+                pick = slice(None)
+            sel.append(pick)
+        return tuple(sel)
+
+    def start(self):
+        s = self.step
+        if s == 0:
+            here = self.src.at[self.part(False) + (slice(None), self.cols)]
+            self.own = pltpu.make_async_copy(
+                self.src.at[self.part(True) + (slice(None), self.cols)], self.held, self.local)
+            self.own.start()
+        else:
+            here = self.held.at[self.part(False)[:-1]]
+        self.copy = remote(here, self.landed[s], self.send.at[s], self.recv.at[s],
+                           self.cube.partner(self.order[s]))
+        self.copy.start()
+
+    def advance(self):
+        s = self.step
+        self.copy.wait()
+        if s == 0:
+            self.own.wait()
+        keep = self.part(True)[:-1]
+        width = self.held.shape[-1]
+        if s + 1 == len(self.order):
+            self.out[:, self.out_cols] = self.held[keep].astype(F32) + self.landed[s][...].astype(F32)
+        else:
+            wide = [slice(None)] * (len(self.landed[s].shape) - 1)
+            tile = LANES * max(k for k in (1, 2, 3) if width % (LANES * k) == 0)
+
+            def add(j, _):
+                cols = (pl.ds(pl.multiple_of(j * tile, tile), tile),)
+                at = keep + (slice(None),) + cols
+                self.held[at] = self.held[at] + self.landed[s][tuple(wide) + cols]
+                return 0
+
+            lax.fori_loop(0, width // tile, add, 0)
+        self.step += 1
+        if self.step < len(self.order):
+            self.start()
+
+
+def comm_in_kernel(cube, parts, n_w, n_t, *refs):
+    cube.bind()
+    w_in, t_in = refs[:n_w], refs[n_w:n_w + n_t]
+    refs = refs[n_w + n_t:]
+    w_out, t_out = refs[:n_w], refs[n_w:n_w + n_t]
+    send, recv, local, t_send, t_recv, t_local = refs[n_w + n_t:]
+    cube.barrier()
+    gathers = [Gather(cube, w_in[a], w_out[a], pl.ds(start, size), cube.order(order), send.at[k], recv.at[k])
+               for k, (a, start, size, order) in enumerate(parts)]
+    for gather in gathers:
+        gather.start()
+    kept = []
+    for a in range(n_w):
+        kept.append(pltpu.make_async_copy(w_in[a], w_out[a].at[tuple(cube.mine)], local.at[a]))
+    exchanges = []
+    blk = cube.sizes[1]
+    for a in range(n_t):
+        clips = t_out[a].shape[0]
+        kept.append(pltpu.make_async_copy(
+            t_in[a].at[pl.ds(cube.at_blk * clips, clips)], t_out[a].at[:, cube.at_blk], t_local.at[a]))
+        for k in range(1, blk):
+            other = cube.row_peer(k)
+            exchanges.append(remote(
+                t_in[a].at[pl.ds(other[1] * clips, clips)], t_out[a].at[:, cube.at_blk],
+                t_send.at[a, k - 1], t_recv.at[a, k - 1], other))
+    for copy in kept + exchanges:
+        copy.start()
+    for copy in kept:
+        copy.wait()
+    for _ in range(cube.count):
+        for gather in gathers:
+            gather.advance()
+    for copy in exchanges:
+        copy.wait()
+
+
+def comm_in(weights, toks, dp, blk, parts, cid):
+    cube = Cube(dp, blk)
+    n_w, n_t, n_p = len(weights), len(toks), len(parts)
+    anywhere = pl.BlockSpec(memory_space=pl.ANY)
+    outs = [jax.ShapeDtypeStruct((2,) * cube.count + w.shape, w.dtype) for w in weights]
+    outs += [jax.ShapeDtypeStruct((t.shape[0] // blk, blk) + t.shape[1:], t.dtype) for t in toks]
+    return pl.pallas_call(
+        functools.partial(comm_in_kernel, cube, parts, n_w, n_t),
+        in_specs=[anywhere] * (n_w + n_t),
+        out_specs=[anywhere] * (n_w + n_t),
+        out_shape=outs,
+        scratch_shapes=[
+            pltpu.SemaphoreType.DMA((n_p, cube.count)),
+            pltpu.SemaphoreType.DMA((n_p, cube.count)),
+            pltpu.SemaphoreType.DMA((n_w,)),
+            pltpu.SemaphoreType.DMA((max(n_t, 1), blk)),
+            pltpu.SemaphoreType.DMA((max(n_t, 1), blk)),
+            pltpu.SemaphoreType.DMA((max(n_t, 1),)),
+        ],
+        compiler_params=pltpu.CompilerParams(collective_id=cid, has_side_effects=True, vmem_limit_bytes=LIMIT),
+        name="comm_in",
+    )(*weights, *toks)
+
+
+def comm_out_kernel(cube, parts, n_w, n_t, *refs):
+    cube.bind()
+    w_in, t_in = refs[:n_w], refs[n_w:n_w + n_t]
+    refs = refs[n_w + n_t:]
+    w_out, norm, t_out = refs[:n_w], refs[n_w], refs[n_w + 1:n_w + 1 + n_t]
+    refs = refs[n_w + 1 + n_t:]
+    n_p = len(parts)
+    held = refs[:n_p]
+    landed = [refs[n_p + k * cube.count:n_p + (k + 1) * cube.count] for k in range(n_p)]
+    send, recv, local, t_send, t_recv, t_local, sums, s_send, s_recv = refs[n_p * (1 + cube.count):]
+    dp, blk = cube.sizes
+    cube.barrier()
+    reduces = [
+        Reduce(cube, w_in[a], pl.ds(start, size), cube.order(order), held[k], landed[k], w_out[a],
+               pl.ds(start, size), send.at[k], recv.at[k], local.at[k])
+        for k, (a, start, size, order) in enumerate(parts)]
+    for reduce in reduces:
+        reduce.start()
+    kept, exchanges = [], []
+    for a in range(n_t):
+        clips = t_in[a].shape[0]
+        here = pl.ds(cube.at_blk * clips, clips)
+        kept.append(pltpu.make_async_copy(t_in[a].at[:, cube.at_blk], t_out[a].at[here], t_local.at[a]))
+        for k in range(1, blk):
+            other = cube.row_peer(k)
+            exchanges.append(remote(t_in[a].at[:, other[1]], t_out[a].at[here],
+                                    t_send.at[a, k - 1], t_recv.at[a, k - 1], other))
+    for copy in kept + exchanges:
+        copy.start()
+    for _ in range(cube.count):
+        for reduce in reduces:
+            reduce.advance()
+    for copy in kept + exchanges:
+        copy.wait()
+    total = jnp.zeros((), F32)
+    for out in w_out:
+        total = total + jnp.sum(out[...] * out[...])
+    for axis, (size, peer, at) in enumerate(((dp, cube.column_peer, cube.at_dp), (blk, cube.row_peer, cube.at_blk))):
+        box = sums[axis]
+        box[at] = jnp.full(box.shape[1:], total, F32)
+        copies = [remote(box.at[at], box.at[at], s_send[axis].at[k - 1], s_recv[axis].at[k - 1], peer(k))
+                  for k in range(1, size)]
+        for copy in copies:
+            copy.start()
+        for copy in copies:
+            copy.wait()
+        whole = box[0]
+        for k in range(1, size):
+            whole = whole + box[k]
+        total = whole[0, 0]
+    norm[...] = whole
+
+
+def comm_out(grads, toks, dp, blk, parts, cid):
+    cube = Cube(dp, blk)
+    n_w, n_t, n_p = len(grads), len(toks), len(parts)
+    anywhere = pl.BlockSpec(memory_space=pl.ANY)
+    inside = pl.BlockSpec(memory_space=pltpu.VMEM)
+    shards = [g.shape[-2:] for g in grads]
+    outs = [jax.ShapeDtypeStruct(s, F32) for s in shards] + [jax.ShapeDtypeStruct((8, LANES), F32)]
+    outs += [jax.ShapeDtypeStruct((t.shape[0] * blk,) + t.shape[2:], t.dtype) for t in toks]
+    held, landed = [], []
+    for a, _, size, _ in parts:
+        tail = (shards[a][0], size)
+        held.append(pltpu.VMEM((2,) * (cube.count - 1) + tail, BF16))
+        landed += [pltpu.VMEM((2,) * (cube.count - 1 - s) + tail, BF16) for s in range(cube.count)]
+    return pl.pallas_call(
+        functools.partial(comm_out_kernel, cube, parts, n_w, n_t),
+        in_specs=[anywhere] * (n_w + n_t),
+        out_specs=[inside] * (n_w + 1) + [anywhere] * n_t,
+        out_shape=outs,
+        scratch_shapes=held + landed + [
+            pltpu.SemaphoreType.DMA((n_p, cube.count)),
+            pltpu.SemaphoreType.DMA((n_p, cube.count)),
+            pltpu.SemaphoreType.DMA((n_p,)),
+            pltpu.SemaphoreType.DMA((max(n_t, 1), blk)),
+            pltpu.SemaphoreType.DMA((max(n_t, 1), blk)),
+            pltpu.SemaphoreType.DMA((max(n_t, 1),)),
+            [pltpu.VMEM((dp, 8, LANES), F32), pltpu.VMEM((blk, 8, LANES), F32)],
+            [pltpu.SemaphoreType.DMA((dp,)), pltpu.SemaphoreType.DMA((blk,))],
+            [pltpu.SemaphoreType.DMA((dp,)), pltpu.SemaphoreType.DMA((blk,))],
+        ],
+        compiler_params=pltpu.CompilerParams(collective_id=cid, has_side_effects=True, vmem_limit_bytes=LIMIT),
+        name="comm_out",
+    )(*grads, *toks)
 
 
 def key_columns(kept_time, kept_bands, blocks, own, segment, padded):
@@ -418,6 +686,74 @@
     return jnp.where(lane == 0, bias, jnp.where(lane < 4, 1.0, 0.0)).astype(BF16)
 
 
+def prepare_kernel(tok_ref, cot_ref, xc_ref, low_ref):
+    segment, extra = tok_ref.shape[1], xc_ref.shape[1] - tok_ref.shape[1]
+    values = tok_ref[...]
+    centred = (values - jnp.mean(values, -1, keepdims=True)).astype(BF16)
+    blank = jnp.zeros((values.shape[0], extra, values.shape[2]), BF16)
+    xc_ref[...] = jnp.concatenate([centred, blank], 1)
+    low_ref[...] = jnp.concatenate([cot_ref[...].astype(BF16), blank], 1)
+
+
+def prepare(tokens, cotangent, padded):
+    clips, segment, width = tokens.shape
+    wide = pl.BlockSpec((2, segment, width), lambda i: (i, 0, 0))
+    out = pl.BlockSpec((2, padded, width), lambda i: (i, 0, 0))
+    shape = jax.ShapeDtypeStruct((clips, padded, width), BF16)
+    return pl.pallas_call(
+        prepare_kernel, grid=(clips // 2,), in_specs=[wide, wide], out_specs=[out, out], out_shape=[shape, shape],
+        compiler_params=pltpu.CompilerParams(dimension_semantics=("arbitrary",), vmem_limit_bytes=LIMIT),
+        name="prepare")(tokens, cotangent)
+
+
+def finish_kernel(tok_ref, cot_ref, act_ref, dlt_ref, out_ref, grad_ref):
+    segment = tok_ref.shape[1]
+    out_ref[...] = tok_ref[...] + act_ref[...].astype(F32)[:, :segment]
+    grad_ref[...] = cot_ref[...] + dlt_ref[...].astype(F32)[:, :segment]
+
+
+def finish(tokens, cotangent, act, dlt):
+    clips, segment, width = tokens.shape
+    wide = pl.BlockSpec((2, segment, width), lambda i: (i, 0, 0))
+    low = pl.BlockSpec((2,) + act.shape[1:], lambda i: (i, 0, 0))
+    shape = jax.ShapeDtypeStruct(tokens.shape, F32)
+    return pl.pallas_call(
+        finish_kernel, grid=(clips // 2,), in_specs=[wide, wide, low, low], out_specs=[wide, wide],
+        out_shape=[shape, shape],
+        compiler_params=pltpu.CompilerParams(dimension_semantics=("arbitrary",), vmem_limit_bytes=LIMIT),
+        name="finish")(tokens, cotangent, act, dlt)
+
+
+RATES = (MATRIX_RATE, MATRIX_RATE, MATRIX_RATE, MATRIX_RATE, VECTOR_RATE)
+DECAYS = (MATRIX_DECAY, MATRIX_DECAY, MATRIX_DECAY, MATRIX_DECAY, 0.0)
+
+
+def adamw_kernel(norm_ref, *refs):
+    weights, firsts, seconds, shares = refs[:5], refs[5:10], refs[10:15], refs[15:20]
+    outs = refs[20:]
+    factor = CLIP_LIMIT / jnp.maximum(jnp.sqrt(norm_ref[0:1, 0:1]), CLIP_LIMIT)
+    for index in range(5):
+        clipped = shares[index][...] * factor
+        weight = weights[index][...]
+        momentum = BETA_ONE * firsts[index][...] + (1.0 - BETA_ONE) * clipped
+        variance = BETA_TWO * seconds[index][...] + (1.0 - BETA_TWO) * clipped * clipped
+        mean_hat = momentum / (1.0 - BETA_ONE**STEP)
+        var_hat = variance / (1.0 - BETA_TWO**STEP)
+        updated = weight - RATES[index] * (
+            mean_hat / (jnp.sqrt(var_hat) + ADAM_EPS) + DECAYS[index] * weight)
+        for kind, value in enumerate((clipped, momentum, variance, updated)):
+            outs[5 * kind + index][...] = value
+
+
+def adamw(norm, weights, firsts, seconds, shares):
+    inside = pl.BlockSpec(memory_space=pltpu.VMEM)
+    return pl.pallas_call(
+        adamw_kernel, in_specs=[inside] * 21, out_specs=[inside] * 20,
+        out_shape=[jax.ShapeDtypeStruct(w.shape, F32) for w in weights] * 4,
+        compiler_params=pltpu.CompilerParams(vmem_limit_bytes=LIMIT),
+        name="adamw")(norm, *weights, *firsts, *seconds, *shares)
+
+
 def shards(
     tokens, kept_time, kept_bands, cotangent,
     weight_merged, weight_output, weight_expand, weight_shrink, vectors,
@@ -425,59 +761,50 @@
     second_merged, second_output, second_expand, second_shrink, second_vectors,
 ):
     clip_count, segment, width = tokens.shape
-    blocks = lax.axis_size("blk")
+    dp, blk = lax.axis_size("dp"), lax.axis_size("blk")
     own = lax.axis_index("blk")
-    clips = clip_count // blocks
+    clips = clip_count // blk
     padded = -(-segment // 16) * 16
-    total = clips * blocks * padded
-    axes = ("dp", "blk")
-
-    def to_clips(values):
-        values = jnp.pad(values.astype(BF16), ((0, 0), (0, padded - segment), (0, 0)))
-        return lax.all_to_all(values, "blk", 0, 1, tiled=True).reshape(total, width)
-
-    def to_home(values):
-        values = values.reshape(clips, blocks * padded, width)
-        return lax.all_to_all(values, "blk", 1, 0, tiled=True)[:, :segment].astype(F32)
+    total = clips * blk * padded
+    rows = weight_merged.shape[0]
+    ff = weight_expand.shape[1]
+    cube = (2,) * (bits_of(dp) + bits_of(blk))
 
     columns = jnp.pad(vectors.T, ((0, 0), (0, LANES - vectors.shape[0])))
-    merged = lax.all_gather(
-        jnp.concatenate([weight_merged, columns], 1).astype(BF16), axes, axis=0, tiled=True)
-    wide = lax.all_gather(
-        jnp.concatenate([weight_output, weight_expand], 1).astype(BF16), axes, axis=0, tiled=True)
-    shrink = lax.all_gather(weight_shrink.astype(BF16), axes, axis=0, tiled=True)
+    merged_low = jnp.concatenate([weight_merged, columns], 1).astype(BF16)
+    wide_low = jnp.concatenate([weight_output, weight_expand], 1).astype(BF16)
+    xc_home, cot_home = prepare(tokens, cotangent, padded)
+    half = (merged_low.shape[1] // LANES + 1) // 2 * LANES
+    half_wide = wide_low.shape[1] // 2
+    merged, wide, shrink, xc, cot = comm_in(
+        [merged_low, wide_low, weight_shrink.astype(BF16)], [xc_home, cot_home], dp, blk,
+        [(0, 0, half, "XbYa"), (0, half, merged_low.shape[1] - half, "XabY"),
+         (1, 0, half_wide, "abXY"), (1, half_wide, half_wide, "XYab"), (2, 0, width, "bXYa")], 0)
+    merged = merged.reshape(width, merged_low.shape[1])
+    wide = wide.reshape(width, wide_low.shape[1])
+    shrink = shrink.reshape(ff, width)
+    xc, cot = xc.reshape(total, width), cot.reshape(total, width)
     vec = merged[:, 3 * width:3 * width + vectors.shape[0]].T.astype(F32)
-    xc = to_clips(tokens - jnp.mean(tokens, -1, keepdims=True))
-    cot = to_clips(cotangent)
-    dead = key_columns(kept_time, kept_bands, blocks, own, segment, padded)
+    dead = key_columns(kept_time, kept_bands, blk, own, segment, padded)
     n1, qa, kv, mix, mid = attn_fwd(xc, dead, merged, wide, vec, clips, HEADS)
-    act, dmid, grad_expand, grad_shrink, early = ffn(mid, xc, cot, wide, shrink, vec, blocks * padded)
+    act, dmid, grad_expand, grad_shrink, early = ffn(mid, xc, cot, wide, shrink, vec, blk * padded)
     dlt, grad_merged, grad_output = attn_bwd(
         xc, cot, dmid, dead, n1, qa, kv, mix, merged, wide, vec, early, clips, HEADS)
-    activations = tokens + to_home(act)
-    token_grads = cotangent + to_home(dlt)
-    scattered = [
-        lax.psum_scatter(grad, axes, scatter_dimension=0, tiled=True).astype(F32)
-        for grad in (grad_merged, grad_output, grad_expand, grad_shrink)
-    ]
-    shares = (
-        scattered[0][:, :3 * width], scattered[1], scattered[2], scattered[3],
-        scattered[0][:, 3 * width:3 * width + vectors.shape[0]].T,
-    )
-    squares = sum(jnp.sum(share_part * share_part) for share_part in shares)
-    gradient_norm = jnp.sqrt(lax.psum(squares, axes))
-    factor = CLIP_LIMIT / jnp.maximum(gradient_norm, CLIP_LIMIT)
-    weights = (weight_merged, weight_output, weight_expand, weight_shrink, vectors)
-    firsts = (first_merged, first_output, first_expand, first_shrink, first_vectors)
-    seconds = (second_merged, second_output, second_expand, second_shrink, second_vectors)
-    rates = (MATRIX_RATE, MATRIX_RATE, MATRIX_RATE, MATRIX_RATE, VECTOR_RATE)
-    decays = (MATRIX_DECAY, MATRIX_DECAY, MATRIX_DECAY, MATRIX_DECAY, 0.0)
-    steps_out = [
-        adamw(*parts, factor, rate, decay)
-        for *parts, rate, decay in zip(weights, firsts, seconds, shares, rates, decays)
-    ]
-    return (activations, token_grads, gradient_norm) + tuple(
-        steps_out[index][kind] for kind in range(4) for index in range(5))
+    grads = [g.reshape(cube + (g.shape[0] // (dp * blk), g.shape[1]))
+             for g in (grad_merged, grad_output, grad_expand, grad_shrink)]
+    sent = (clips, blk, padded, width)
+    *shares, norm, act_home, dlt_home = comm_out(
+        grads, [act.reshape(sent), dlt.reshape(sent)], dp, blk,
+        [(0, 0, merged_low.shape[1], "YXba"), (1, 0, width, "aYXb"), (2, 0, ff // 2, "YbaX"),
+         (2, ff // 2, ff // 2, "YXab"), (3, 0, width, "aYXb")], 1)
+    activations, token_grads = finish(tokens, cotangent, act_home, dlt_home)
+    shares.append(shares[0][:, 3 * width:3 * width + vectors.shape[0]].T)
+    shares[0] = shares[0][:, :3 * width]
+    steps_out = adamw(
+        norm, (weight_merged, weight_output, weight_expand, weight_shrink, vectors),
+        (first_merged, first_output, first_expand, first_shrink, first_vectors),
+        (second_merged, second_output, second_expand, second_shrink, second_vectors), shares)
+    return (activations, token_grads, jnp.sqrt(norm[0, 0]), *steps_out)
 
 
 def solution(mesh):

time: 852 us -> 452 us (0.53)
  waiting for transfers between devices: 521 us -> 0 us
  Pallas kernels: 169 us -> 432 us
  blocking collectives: 40.1 us -> 0 us
  local copies, waits for them, and re-layouts: 41.6 us -> 7.74 us
  other arithmetic: 41.4 us -> 8.28 us
  starting transfers between devices: 17.8 us -> 0 us
  between operations: 19.5 us -> 2.59 us
    pallas_call x0 -> x5, Pallas kernels: none -> 265 us  [the longest x1 143 us: comm_in(): pl.pallas_call(functools.partial(comm_in_kernel, cube, parts, n_w, n_t),...]
    reduce_scatter x3 -> x0, waiting for transfers between devices: 255 us -> none  [shards(): lax.psum_scatter(grad, axes, scatter_dimension=0, tiled=True).astype(F32)]
    unnamed x8 -> x0, waiting for transfers between devices: 97.7 us -> none
    all_to_all x4 -> x0, waiting for transfers between devices: 88.3 us -> none  [the longest x2 56.7 us: to_clips(): return lax.all_to_all(values, 'blk', 0, 1, tiled=True).reshape(total, width)]
    all_gather x3 -> x0, waiting for transfers between devices: 80 us -> none  [the longest x1 49.9 us: shards(): lax.all_gather(jnp.concatenate([weight_output, weight_expand], 1).astype(...]
    psum x1 -> x0, blocking collectives: 40.1 us -> none  [shards(): gradient_norm = jnp.sqrt(lax.psum(squares, axes))]
    all_to_all x4 -> x0, starting transfers between devices: 17.5 us -> none  [the longest x2 8.89 us: to_clips(): return lax.all_to_all(values, 'blk', 0, 1, tiled=True).reshape(total, width)]
    unnamed x47 -> x5, local copies, waits for them, and re-layouts: 15.5 us -> 0.71 us
  transfers between devices with their start and end apart: 11 -> 0, of which waited for: 9 -> 0; matrix products, arithmetic and copies ran while one was open for 6% -> 0% of each run, Pallas kernels for 4% -> 0%
where the time goes in v2:
time: 452 us; the launch traced here: 451 us
  Pallas kernels  432 us (96%)
  other arithmetic  8.28 us (2%)
  local copies, waits for them, and re-layouts  7.74 us (2%)
    pallas_call x1, Pallas kernels, comm_in(): pl.pallas_call(functools.partial(comm_in_kernel, cube, parts, n_w, n_t),...  143 us
    pallas_call x1, Pallas kernels, comm_out(): pl.pallas_call(functools.partial(comm_out_kernel, cube, parts, n_w, n_t),...  101 us
    pallas_call x1, Pallas kernels, ffn(): pl.pallas_call(ffn_kernel, grid=(nf, ni), in_specs=[pl.BlockSpec((rows, w...  76 us
    pallas_call x1, Pallas kernels, attn_bwd(): pl.pallas_call(functools.partial(attn_bwd_kernel, heads), grid=(clips,),...  55.6 us
    pallas_call x1, Pallas kernels, attn_fwd(): pl.pallas_call(functools.partial(attn_fwd_kernel, heads), grid=(clips,),...  36 us
    pallas_call x1, Pallas kernels, finish(): pl.pallas_call(finish_kernel, grid=(clips // 2,), in_specs=[wide, wide, l...  9.52 us

profile of v2, /device:TPU:0, one launch (start us, length us, event | category | flops | bytes accessed | tf_op | source)
XLA Modules:
  0.0 450.9 jit_solution(13511909749699362579)
XLA Ops:
  0.7 0.1 pad.8.clone
  0.8 0.6 copy-done
  1.4 0.7 constant_dynamic-slice_fusion
  2.1 0.1 mul.27
  2.2 0.7 convert.17
  2.9 0.1 copy.50
  3.0 0.1 mul.31
  3.1 0.9 convert.18
  4.0 0.1 mul.28
  4.1 0.1 mul.29
  4.2 0.1 fusion.2
  4.3 0.9 convert.16
  5.3 0.7 fusion.1.refs_0_
  5.9 1.0 convert.19
  6.9 0.7 pad_maximum_fusion.refs_1_
  7.6 1.6 convert_element_type.22.refs_2_
  9.2 1.0 select_convert_fusion.dead_ref
  10.3 7.2 %prepare.1 = (bf16[12,128,768]{2,1,0:T(8,128)(2,1)}, bf16[12,128,768]{2,1,0:T(8,128)(2,1)}) custom-call(f32[12,122,768]{2,1,0:T(8,128)} %tok_ref.3, f32[12,122,768]{2,1,0:T(8,128)} %cot_ref.3), custom_call_target="tpu_custom_call" | custom-call | tf_op jit(solution)/shard_map/prepare/pallas_call | solution.py:703
  17.4 142.7 %comm_in.1 = (bf16[2,2,2,2,2,24,2432]{6,5,4,3,2,1,0:T(8,128)(2,1)}, bf16[2,2,2,2,2,24,3840]{6,5,4,3,2,1,0:T(8,128)(2,1)}, bf16[2,2,2,2,2,96,768]{6,5,4,3,2,1,0:T...) custom-call(bf16[24,2432]{1,0:T(8,128)(2,1)} %fusion.1.refs_0_, ...), custom_call_target="tpu_custom_call" | custom-call | tf_op jit(solution)/shard_map/comm_in/pallas_call | solution.py:569
  160.1 0.9 slice.16
  161.0 0.1 copy.53
  161.2 0.6 convert_bitcast_fusion.vec_ref
  161.8 36.0 %attn_fwd.1 = (bf16[1536,768]{1,0:T(8,128)(2,1)}, bf16[12,1536,128]{2,1,0:T(8,128)(2,1)}, bf16[1536,1536]{1,0:T(8,128)(2,1)}, bf16[1536,768]{1,0:T(8,128)(2,1)}, f32[1536,768]{1,0:T(8,128)}) custom-call(bf16[1536,768]{1,0:T(8,128)(2,1)} %bitcast.22, bf16[1536,128]{1,0:T(8,128)(2,1)} %select_convert_fusion.dead_ref, bf16[768,2432]{1,0:T(8,128)(2,1)} %bitcast.26, ...), custom_call_target="tpu_custom_call" | custom-call | tf_op jit(solution)/shard_map/attn_fwd/pallas_call | solution.py:242
  197.8 76.0 %ffn.1 = (bf16[1536,768]{1,0:T(8,128)(2,1)}, f32[1536,768]{1,0:T(8,128)}, bf16[768,3072]{1,0:T(8,128)(2,1)}, bf16[3072,768]{1,0:T(8,128)(2,1)}, f32[16,768]{1,0:T(8,128)}) custom-call(f32[1536,768]{1,0:T(8,128)} %get-tuple-element.78.mid_ref, bf16[1536,768]{1,0:T(8,128)(2,1)} %bitcast.23, bf16[1536,768]{1,0:T(8,128)(2,1)} %bitcast.28, ...), custom_call_target="tpu_custom_call" | custom-call | tf_op jit(solution)/shard_map/ffn/pallas_call | solution.py:139
  273.8 55.6 %attn_bwd.1 = (bf16[1536,768]{1,0:T(8,128)(2,1)}, bf16[768,2432]{1,0:T(8,128)(2,1)}, bf16[768,768]{1,0:T(8,128)(2,1)}) custom-call(bf16[1536,768]{1,0:T(8,128)(2,1)} %bitcast.24, bf16[1536,768]{1,0:T(8,128)(2,1)} %bitcast.29, f32[1536,768]{1,0:T(8,128)} %get-tuple-element.80.dmid_ref, bf16[1536,128]{1,0:T(8,128)(2,1)} %select_convert_fusion.dead_ref, ...), custom_call_target="tpu_custom_call" | custom-call | tf_op jit(solution)/shard_map/attn_bwd/pallas_call | solution.py:357
  329.4 101.2 %comm_out.1 = (f32[24,2432]{1,0:T(8,128)}, f32[24,768]{1,0:T(8,128)}, f32[24,3072]{1,0:T(8,128)}, f32[96,768]{1,0:T(8,128)}, f32[8,128]{1,0:T(8,128)}, /*index=5...) custom-call(bf16[2,2,2,2,2,24,2432]{6,5,4,3,2,1,0:T(8,128)(2,1)} %bitcast.33, ...), custom_call_target="tpu_custom_call" | custom-call | tf_op jit(solution)/shard_map/comm_out/pallas_call | solution.py:653
  430.6 1.2 slice.13
  432.5 1.6 slice.14.refs_15_
  434.2 1.3 copy.52
  435.5 0.6 slice_bitcast_fusion.refs_19_
  436.1 4.1 adamw.1
  440.2 9.5 %finish.1 = (f32[12,122,768]{2,1,0:T(8,128)}, f32[12,122,768]{2,1,0:T(8,128)}) custom-call(f32[12,122,768]{2,1,0:T(8,128)} %tok_ref.3, f32[12,122,768]{2,1,0:T(8,128)} %cot_ref.3, bf16[12,128,768]{2,1,0:T(8,128)(2,1)} %get-tuple-element.92.act_ref, bf16[12,128,768]{2,1,0:T(8,128)(2,1)} %get-tuple-element.93.dlt_ref), custom_call_target="tpu_custom_call" | custom-call | tf_op jit(solution)/shard_map/finish/pallas_call | solution.py:720
  (12 shorter events, 0.1 us)
Async XLA Ops:
  0.7 0.7 copy-start
  440.2 9.5 %copy-start.1 = (s32[12,48]{1,0:T(8,128)S(1)}, s32[12,48]{1,0:T(8,128)}, u32[]{:S(2)}) copy-start(s32[12,48]{1,0:T(8,128)} %param.20) | copy-start | bytes 6916

commit v3 on v2

--- a/solution.py
+++ b/solution.py
@@ -20,8 +20,13 @@
 EPS = 1e-06
 HALF = 64
 LANES = 128
-LIMIT = 60 * 1024 * 1024
+LIMIT = 62 * 1024 * 1024
 MESH = pl.DeviceIdType.MESH
+
+FWD_PLAN = {1: [0, 2], 2: [1, 4], 4: [-1, 3], 5: [2], 6: [0, 1], 7: [-2], 10: [3, 4], 12: [0, 1], 14: [3], 15: [2],
+            16: [4], -1: [-3, 1, 0, 3, 2, 4, 1, 0, 3, 2, 4]}
+BWD_PLAN = {0: [-1], 1: [0, 1], 2: [2], 3: [3, -2], 4: [4], 6: [1], 8: [-3, 0, 2], 9: [3], 10: [4], 12: [0, 1, 4],
+            15: [0, 3], 16: [2, 1], 17: [0], -1: [4, 3, 2, 1, 4, 3, 2]}
 
 
 def nn(a, b):
@@ -61,12 +66,12 @@
     return x * phi, phi + (0.3989422804014327 * x) * e
 
 
-def ffn_kernel(mid_ref, xc_ref, cot_ref, exp_ref, shr_ref, vec_ref,
+def ffn_kernel(mix_ref, xc_ref, cot_ref, prj_ref, exp_ref, shr_ref, vec_ref,
                act_ref, dmid_ref, ge_ref, gs_ref, sums_ref,
-               n2_s, y_s, dn_s, ae_s, as_s):
+               mid_s, n2_s, y_s, dn_s, ae_s, as_s):
     f, i = pl.program_id(0), pl.program_id(1)
     nf, ni = pl.num_programs(0), pl.num_programs(1)
-    rows = mid_ref.shape[0]
+    rows = mix_ref.shape[0]
     here = pl.ds(pl.multiple_of(i * rows, rows), rows)
 
     @pl.when((f == 0) & (i == 0))
@@ -75,7 +80,9 @@
 
     @pl.when(f == 0)
     def _():
-        xhat, _ = norm_stats(mid_ref[...])
+        mid = xc_ref[...].astype(F32) + nn(mix_ref[...], prj_ref[...]) + vec_ref[4:5, :]
+        mid_s[here, :] = mid
+        xhat, _ = norm_stats(mid)
         n2_s[here, :] = (xhat * vec_ref[5:6, :] + vec_ref[6:7, :]).astype(BF16)
 
     n2 = n2_s[here, :]
@@ -119,7 +126,7 @@
 
     @pl.when(f == nf - 1)
     def _():
-        mid = mid_ref[...]
+        mid = mid_s[here, :]
         cot = d2.astype(F32)
         xhat, r = norm_stats(mid)
         dy = dn_s[here, :]
@@ -130,8 +137,8 @@
         sums_ref[7:8, :] += jnp.sum(cot, 0, keepdims=True)
 
 
-def ffn(mid, xc, cot, expand, shrink, vec, rows):
-    total, width = mid.shape
+def ffn(mix, xc, cot, expand, shrink, vec, rows):
+    total, width = xc.shape
     ff = expand.shape[1] - width
     nf, ni = ff // width, total // rows
     first = lambda f, i: (jnp.where((f == 0) | (f == nf - 1), i, ni - 1), 0)
@@ -140,9 +147,10 @@
         ffn_kernel,
         grid=(nf, ni),
         in_specs=[
+            pl.BlockSpec((rows, width), lambda f, i: (jnp.where(f == 0, i, ni - 1), 0)),
             pl.BlockSpec((rows, width), first),
-            pl.BlockSpec((rows, width), last),
             pl.BlockSpec((rows, width), lambda f, i: (i, 0)),
+            pl.BlockSpec((width, width), lambda f, i: (0, 0)),
             pl.BlockSpec((width, width), lambda f, i: (0, f + 1)),
             pl.BlockSpec((width, width), lambda f, i: (f, 0)),
             pl.BlockSpec(vec.shape, lambda f, i: (0, 0)),
@@ -162,6 +170,7 @@
             jax.ShapeDtypeStruct((16, width), F32),
         ],
         scratch_shapes=[
+            pltpu.VMEM((total, width), F32),
             pltpu.VMEM((total, width), BF16),
             pltpu.VMEM((total, width), F32),
             pltpu.VMEM((total, width), F32),
@@ -171,14 +180,34 @@
         compiler_params=pltpu.CompilerParams(
             dimension_semantics=("arbitrary", "arbitrary"), vmem_limit_bytes=LIMIT),
         name="ffn",
-    )(mid, xc, cot, expand, shrink, vec)
-
-
-def attn_fwd_kernel(heads, xc_ref, dead_ref, mrg_ref, out_ref, vec_ref,
-                    n1_ref, qa_ref, kv_ref, mix_ref, mid_ref, pk_s):
+    )(mix, xc, cot, expand, expand, shrink, vec)
+
+
+def attn_fwd_kernel(cube, parts, plan, heads, xc_ref, dead_ref, mrg_ref, vec_ref, wide_in, shrink_in, cot_in,
+                    n1_ref, qa_ref, kv_ref, mix_ref, wide_out, shrink_out, cot_out,
+                    pk_s, send, recv, local, t_send, t_recv, t_local):
     width = xc_ref.shape[1]
     seq = xc_ref.shape[0]
     pairs = heads // 2
+    cube.bind()
+    clip = pl.program_id(0)
+    own = [pltpu.make_async_copy(wide_in, wide_out.at[tuple(cube.mine)], local.at[0]),
+           pltpu.make_async_copy(shrink_in, shrink_out.at[tuple(cube.mine)], local.at[1])]
+    gathers = [Gather(cube, (wide_in, shrink_in)[a], (wide_out, shrink_out)[a], pl.ds(first, size), letters,
+                      send.at[n], recv.at[n]) for n, (a, first, size, letters) in enumerate(parts)]
+    exchange = Exchange(cube, cot_in, cot_out, False, t_send, t_recv, t_local)
+    points = Points(plan, gathers, exchange)
+
+    @pl.when(clip == 0)
+    def _():
+        cube.barrier()
+        for gather in gathers:
+            gather.start()
+        for copy in own:
+            copy.start()
+        for copy in own:
+            copy.wait()
+
     xc = xc_ref[...].astype(F32)
     xhat, _ = norm_stats(xc)
     n1 = (xhat * vec_ref[0:1, :] + vec_ref[1:2, :]).astype(BF16)
@@ -199,6 +228,7 @@
     ones = jnp.ones((seq, LANES), BF16)
 
     def pair(p, _):
+        points.visit(clip * pairs + p, False)
         qcols = pl.ds(pl.multiple_of(p * LANES, LANES), LANES)
         kcols = pl.ds(pl.multiple_of(width + p * LANES, LANES), LANES)
         vcols = pl.ds(pl.multiple_of(2 * width + p * LANES, LANES), LANES)
@@ -231,56 +261,111 @@
         return 0
 
     lax.fori_loop(0, pairs, pair, 0)
-    mid_ref[...] = xc + nn(mix_ref[...], out_ref[...]) + vec_ref[4:5, :]
-
-
-def attn_fwd(xc, dead, merged, output, vec, clips, heads):
+
+    @pl.when(clip == pl.num_programs(0) - 1)
+    def _():
+        points.finish()
+        for part in range(exchange.clips):
+            exchange.wait(part)
+
+
+class Points:
+    def __init__(self, plan, movers, exchange):
+        self.plan, self.movers, self.exchange = plan, movers, exchange
+
+    def act(self, which):
+        if which < 0:
+            self.exchange.start(-1 - which)
+        else:
+            self.movers[which].advance()
+
+    def visit(self, now, last):
+        for point in sorted(p for p in self.plan if p >= 0):
+            @pl.when(now == point)
+            def _():
+                for which in self.plan[point]:
+                    self.act(which)
+
+    def finish(self):
+        for which in self.plan[-1]:
+            self.act(which)
+
+
+def attn_fwd(xc, dead, merged, vec, wide, shrink, cot, clips, heads, dp, blk, cid):
     total, width = xc.shape
     seq = total // clips
+    cube = Cube(dp, blk)
     whole = lambda c: (0, 0)
     row = lambda c: (c, 0)
+    anywhere = pl.BlockSpec(memory_space=pl.ANY)
+    third, half = wide.shape[1] // 3, shrink.shape[1] // 2
+    parts = [(0, 0, third, "XbYa"), (0, third, third, "baXY"), (0, 2 * third, third, "YXba"),
+             (1, 0, half, "baYX"), (1, half, half, "XbaY")]
     return pl.pallas_call(
-        functools.partial(attn_fwd_kernel, heads),
+        functools.partial(attn_fwd_kernel, cube, parts, FWD_PLAN, heads),
         grid=(clips,),
         in_specs=[
             pl.BlockSpec((seq, width), row),
             pl.BlockSpec((seq, LANES), row),
             pl.BlockSpec(merged.shape, whole),
-            pl.BlockSpec((width, width), whole),
             pl.BlockSpec(vec.shape, whole),
+            pl.BlockSpec(wide.shape, whole),
+            pl.BlockSpec(shrink.shape, whole),
+            anywhere,
         ],
         out_specs=[
             pl.BlockSpec((seq, width), row),
             pl.BlockSpec((heads, seq, LANES), lambda c: (0, c, 0)),
             pl.BlockSpec((seq, 2 * width), row),
             pl.BlockSpec((seq, width), row),
-            pl.BlockSpec((seq, width), row),
+            anywhere, anywhere, anywhere,
         ],
         out_shape=[
             jax.ShapeDtypeStruct((total, width), BF16),
             jax.ShapeDtypeStruct((heads, total, LANES), BF16),
             jax.ShapeDtypeStruct((total, 2 * width), BF16),
             jax.ShapeDtypeStruct((total, width), BF16),
-            jax.ShapeDtypeStruct((total, width), F32),
-        ],
-        scratch_shapes=[pltpu.VMEM((seq, 3 * width), BF16)],
+            jax.ShapeDtypeStruct((2,) * cube.count + wide.shape, BF16),
+            jax.ShapeDtypeStruct((2,) * cube.count + shrink.shape, BF16),
+            jax.ShapeDtypeStruct((clips, blk) + cot.shape[1:], BF16),
+        ],
+        scratch_shapes=[
+            pltpu.VMEM((seq, 3 * width), BF16),
+            pltpu.SemaphoreType.DMA((len(parts), cube.count)),
+            pltpu.SemaphoreType.DMA((len(parts), cube.count)),
+            pltpu.SemaphoreType.DMA((2,)),
+        ] + exchange_semaphores(clips, blk),
         compiler_params=pltpu.CompilerParams(
-            dimension_semantics=("arbitrary",), vmem_limit_bytes=LIMIT),
+            dimension_semantics=("arbitrary",), vmem_limit_bytes=LIMIT, collective_id=cid, has_side_effects=True),
         name="attn_fwd",
-    )(xc, dead, merged, output, vec)
-
-
-def attn_bwd_kernel(heads, xc_ref, cot_ref, dmid_ref, dead_ref, n1_ref, qa_ref, kv_ref, mix_ref,
+    )(xc, dead, merged, vec, wide, shrink, cot)
+
+
+def attn_bwd_kernel(cube, parts, plan, heads, xc_ref, cot_ref, dmid_ref, dead_ref, n1_ref, qa_ref, kv_ref, mix_ref,
                     mrg_ref, out_ref, vec_ref, early_ref,
-                    dlt_ref, gm_ref, go_ref,
-                    dm_s, dp_s, am_s, ao_s, sums_ref):
+                    ge_in, gs_in, act_in,
+                    dlt_ref, gm_ref, go_ref, ge_out, gs_out, act_out,
+                    dm_s, dp_s, am_s, ao_s, sums_ref, *refs):
     c = pl.program_id(0)
     n = pl.num_programs(0)
     seq, width = xc_ref.shape
     pairs = heads // 2
+    cube.bind()
+    n_p = len(parts)
+    held = refs[:n_p]
+    landed = [refs[n_p + k * cube.count:n_p + (k + 1) * cube.count] for k in range(n_p)]
+    send, recv, local, t_send, t_recv, t_local = refs[n_p * (1 + cube.count):]
+    reduces = [Reduce(cube, (ge_in, gs_in)[a], pl.ds(first, size), letters, held[k], landed[k], (ge_out, gs_out)[a],
+                      send.at[k], recv.at[k], local.at[k])
+               for k, (a, first, size, letters) in enumerate(parts)]
+    exchange = Exchange(cube, act_in, act_out, True, t_send, t_recv, t_local)
+    points = Points(plan, reduces, exchange)
 
     @pl.when(c == 0)
     def _():
+        cube.barrier()
+        for reduce in reduces:
+            reduce.start()
         sums_ref[...] = early_ref[...]
         am_s[...] = jnp.zeros_like(am_s)
         ao_s[...] = jnp.zeros_like(ao_s)
@@ -297,6 +382,7 @@
     vone = jnp.where(in_half < 2, 1.0, 0.0).astype(BF16)
 
     def pair(p, _):
+        points.visit(c * pairs + p, False)
         qcols = pl.ds(pl.multiple_of(p * LANES, LANES), LANES)
         kcols = pl.ds(pl.multiple_of(width + p * LANES, LANES), LANES)
         vcols = pl.ds(pl.multiple_of(2 * width + p * LANES, LANES), LANES)
@@ -347,15 +433,26 @@
         gm_ref[:, 3 * width:] = jnp.concatenate(
             [columns, jnp.zeros((width, LANES - columns.shape[1]), F32)], 1).astype(gm_ref.dtype)
         go_ref[...] = ao_s[...].astype(go_ref.dtype)
-
-
-def attn_bwd(xc, cot, dmid, dead, n1, qa, kv, mix, merged, output, vec, early, clips, heads):
+        points.finish()
+        for part in range(exchange.clips):
+            exchange.wait(part)
+
+
+def attn_bwd(xc, cot, dmid, dead, n1, qa, kv, mix, merged, output, vec, early,
+             grad_expand, grad_shrink, act, clips, heads, dp, blk, cid):
     total, width = xc.shape
     seq = total // clips
+    cube = Cube(dp, blk)
     whole = lambda c: (0, 0)
     row = lambda c: (c, 0)
+    once = pl.Buffered(1)
+    anywhere = pl.BlockSpec(memory_space=pl.ANY)
+    shards = [grad_expand.shape[-2:], grad_shrink.shape[-2:]]
+    third, half = shards[0][1] // 3, shards[1][1] // 2
+    parts = [(0, 0, third, "bYaX"), (0, third, third, "YaXb"), (0, 2 * third, third, "YXab"),
+             (1, 0, half, "XbYa"), (1, half, half, "aYbX")]
     return pl.pallas_call(
-        functools.partial(attn_bwd_kernel, heads),
+        functools.partial(attn_bwd_kernel, cube, parts, BWD_PLAN, heads),
         grid=(clips,),
         in_specs=[
             pl.BlockSpec((seq, width), row),
@@ -366,20 +463,27 @@
             pl.BlockSpec((heads, seq, LANES), lambda c: (0, c, 0)),
             pl.BlockSpec((seq, 2 * width), row),
             pl.BlockSpec((seq, width), row),
-            pl.BlockSpec(merged.shape, whole),
-            pl.BlockSpec((width, width), whole),
+            pl.BlockSpec(merged.shape, whole, pipeline_mode=once),
+            pl.BlockSpec((width, width), whole, pipeline_mode=once),
             pl.BlockSpec(vec.shape, whole),
             pl.BlockSpec(early.shape, whole),
+            anywhere, anywhere, anywhere,
         ],
         out_specs=[
             pl.BlockSpec((seq, width), row),
-            pl.BlockSpec(merged.shape, whole),
-            pl.BlockSpec((width, width), whole),
+            pl.BlockSpec(merged.shape, whole, pipeline_mode=once),
+            pl.BlockSpec((width, width), whole, pipeline_mode=once),
+            pl.BlockSpec(shards[0], whole, pipeline_mode=once),
+            pl.BlockSpec(shards[1], whole, pipeline_mode=once),
+            anywhere,
         ],
         out_shape=[
             jax.ShapeDtypeStruct((total, width), BF16),
             jax.ShapeDtypeStruct(merged.shape, BF16),
             jax.ShapeDtypeStruct((width, width), BF16),
+            jax.ShapeDtypeStruct(shards[0], F32),
+            jax.ShapeDtypeStruct(shards[1], F32),
+            jax.ShapeDtypeStruct((clips * blk,) + act.shape[2:], BF16),
         ],
         scratch_shapes=[
             pltpu.VMEM((seq, width), BF16),
@@ -387,11 +491,12 @@
             pltpu.VMEM((width, 3 * width), F32),
             pltpu.VMEM((width, width), F32),
             pltpu.VMEM((16, width), F32),
-        ],
+        ] + reduce_scratch(cube, [(shards[a][0], size) for a, _, size, _ in parts])
+        + exchange_semaphores(clips, blk),
         compiler_params=pltpu.CompilerParams(
-            dimension_semantics=("arbitrary",), vmem_limit_bytes=LIMIT),
+            dimension_semantics=("arbitrary",), vmem_limit_bytes=LIMIT, collective_id=cid, has_side_effects=True),
         name="attn_bwd",
-    )(xc, cot, dmid, dead, n1, qa, kv, mix, merged, output, vec, early)
+    )(xc, cot, dmid, dead, n1, qa, kv, mix, merged, output, vec, early, grad_expand, grad_shrink, act)
 
 
 def bits_of(size):
@@ -403,8 +508,9 @@
         self.sizes = (dp, blk)
         self.n_dp, self.n_blk = bits_of(dp), bits_of(blk)
         self.count = self.n_dp + self.n_blk
-        self.core = self.count - 1
-        self.cross = self.count - 2
+        far = list(range(self.n_dp - 1))
+        self.letters = {"X": list(range(self.n_dp, self.count - 1)), "Y": [self.n_dp - 1],
+                        "a": far[-1:], "b": far[:-1], "C": [self.count - 1]}
 
     def bind(self):
         self.at_dp, self.at_blk = lax.axis_index("dp"), lax.axis_index("blk")
@@ -433,12 +539,6 @@
             pl.semaphore_signal(sem, inc=1, device_id=other, device_id_type=MESH)
         pl.semaphore_wait(sem, len(others))
 
-    def order(self, letters):
-        far = [bit for bit in range(self.n_dp - 1)]
-        near = {"Y": [self.n_dp - 1], "X": [k for k in range(self.n_dp, self.count - 1)],
-                "a": far[-1:], "b": far[:-1]}
-        return [bit for letter in letters for bit in near[letter]]
-
 
 def remote(src, dst, send, recv, device):
     return pltpu.make_async_remote_copy(
@@ -446,35 +546,42 @@
 
 
 class Gather:
-    def __init__(self, cube, src, dst, cols, order, send, recv):
+    def __init__(self, cube, src, dst, cols, letters, send, recv):
         self.cube, self.src, self.dst, self.cols = cube, src, dst, cols
-        self.order = list(order) + [cube.core]
+        self.steps = [cube.letters[letter] for letter in letters + "C"]
+        self.order = sum(self.steps, [])
         self.send, self.recv, self.step = send, recv, 0
 
-    def start(self):
-        cube, s = self.cube, self.step
+    def copy(self, s):
+        cube = self.cube
         sel = tuple(slice(None) if bit in self.order[:s] else cube.mine[bit] for bit in range(cube.count))
         there = self.dst.at[sel + (slice(None), self.cols)]
         here = self.src.at[:, self.cols] if s == 0 else there
-        self.copy = remote(here, there, self.send.at[s], self.recv.at[s], cube.partner(self.order[s]))
-        self.copy.start()
+        return remote(here, there, self.send.at[s], self.recv.at[s], cube.partner(self.order[s]))
+
+    def start(self):
+        self.done = 0
+        self.copy(0).start()
 
     def advance(self):
-        self.copy.wait()
+        for _ in self.steps[self.step]:
+            self.copy(self.done).wait()
+            self.done += 1
+            if self.done < len(self.order):
+                self.copy(self.done).start()
         self.step += 1
-        if self.step < len(self.order):
-            self.start()
 
 
 class Reduce:
-    def __init__(self, cube, src, cols, order, held, landed, out, out_cols, send, recv, local):
+    def __init__(self, cube, src, cols, letters, held, landed, out, send, recv, local):
         self.cube, self.src, self.cols, self.held, self.landed = cube, src, cols, held, landed
-        self.order = [cube.core] + list(order)
-        self.out, self.out_cols = out, out_cols
+        self.steps = [cube.letters[letter] for letter in "C" + letters]
+        self.order = sum(self.steps, [])
+        self.out = out
         self.send, self.recv, self.local, self.step = send, recv, local, 0
 
-    def part(self, kept):
-        cube, s = self.cube, self.step
+    def part(self, s, kept):
+        cube = self.cube
         sel = []
         for bit in range(cube.count):
             if bit in self.order[:s]:
@@ -486,140 +593,148 @@
             sel.append(pick)
         return tuple(sel)
 
+    def own(self):
+        return pltpu.make_async_copy(
+            self.src.at[self.part(0, True) + (slice(None), self.cols)], self.held, self.local)
+
+    def copy(self, s):
+        if s == 0:
+            here = self.src.at[self.part(0, False) + (slice(None), self.cols)]
+        else:
+            here = self.held.at[self.part(s, False)[:-1]]
+        return remote(here, self.landed[s], self.send.at[s], self.recv.at[s], self.cube.partner(self.order[s]))
+
     def start(self):
-        s = self.step
-        if s == 0:
-            here = self.src.at[self.part(False) + (slice(None), self.cols)]
-            self.own = pltpu.make_async_copy(
-                self.src.at[self.part(True) + (slice(None), self.cols)], self.held, self.local)
-            self.own.start()
-        else:
-            here = self.held.at[self.part(False)[:-1]]
-        self.copy = remote(here, self.landed[s], self.send.at[s], self.recv.at[s],
-                           self.cube.partner(self.order[s]))
-        self.copy.start()
-
-    def advance(self):
-        s = self.step
-        self.copy.wait()
-        if s == 0:
-            self.own.wait()
-        keep = self.part(True)[:-1]
+        self.done = 0
+        self.own().start()
+        self.copy(0).start()
+
+    def add(self, s):
+        keep = self.part(s, True)[:-1]
         width = self.held.shape[-1]
         if s + 1 == len(self.order):
-            self.out[:, self.out_cols] = self.held[keep].astype(F32) + self.landed[s][...].astype(F32)
-        else:
-            wide = [slice(None)] * (len(self.landed[s].shape) - 1)
-            tile = LANES * max(k for k in (1, 2, 3) if width % (LANES * k) == 0)
-
-            def add(j, _):
-                cols = (pl.ds(pl.multiple_of(j * tile, tile), tile),)
-                at = keep + (slice(None),) + cols
-                self.held[at] = self.held[at] + self.landed[s][tuple(wide) + cols]
-                return 0
-
-            lax.fori_loop(0, width // tile, add, 0)
+            self.out[:, self.cols] = self.held[keep].astype(F32) + self.landed[s][...].astype(F32)
+            return
+        wide = (slice(None),) * (len(self.landed[s].shape) - 1)
+        tile = LANES * max(k for k in (1, 2, 3) if width % (LANES * k) == 0)
+
+        def some(j, _):
+            cols = (pl.ds(pl.multiple_of(j * tile, tile), tile),)
+            at = keep + (slice(None),) + cols
+            self.held[at] = self.held[at] + self.landed[s][wide + cols]
+            return 0
+
+        lax.fori_loop(0, width // tile, some, 0)
+
+    def advance(self):
+        for _ in self.steps[self.step]:
+            s = self.done
+            self.copy(s).wait()
+            if s == 0:
+                self.own().wait()
+            self.add(s)
+            self.done += 1
+            if self.done < len(self.order):
+                self.copy(self.done).start()
         self.step += 1
-        if self.step < len(self.order):
-            self.start()
-
-
-def comm_in_kernel(cube, parts, n_w, n_t, *refs):
-    cube.bind()
-    w_in, t_in = refs[:n_w], refs[n_w:n_w + n_t]
-    refs = refs[n_w + n_t:]
-    w_out, t_out = refs[:n_w], refs[n_w:n_w + n_t]
-    send, recv, local, t_send, t_recv, t_local = refs[n_w + n_t:]
-    cube.barrier()
-    gathers = [Gather(cube, w_in[a], w_out[a], pl.ds(start, size), cube.order(order), send.at[k], recv.at[k])
-               for k, (a, start, size, order) in enumerate(parts)]
+
+
+class Exchange:
+    def __init__(self, cube, src, dst, back, send, recv, local):
+        self.cube, self.src, self.dst, self.back = cube, src, dst, back
+        self.clips = (src if back else dst).shape[0]
+        self.send, self.recv, self.local = send, recv, local
+
+    def ends(self, to, clip):
+        if self.back:
+            return self.src.at[clip, to], self.dst.at[self.cube.at_blk * self.clips + clip]
+        return self.src.at[to * self.clips + clip], self.dst.at[clip, self.cube.at_blk]
+
+    def copies(self, clip):
+        found = [pltpu.make_async_copy(*self.ends(self.cube.at_blk, clip), self.local.at[clip])]
+        for k in range(1, self.cube.sizes[1]):
+            other = self.cube.row_peer(k)
+            found.append(remote(*self.ends(other[1], clip), self.send.at[clip, k - 1], self.recv.at[clip, k - 1], other))
+        return found
+
+    def start(self, clip):
+        for copy in self.copies(clip):
+            copy.start()
+
+    def wait(self, clip):
+        for copy in self.copies(clip):
+            copy.wait()
+
+
+def exchange_semaphores(clips, blk):
+    return [pltpu.SemaphoreType.DMA((clips, blk)), pltpu.SemaphoreType.DMA((clips, blk)),
+            pltpu.SemaphoreType.DMA((clips,))]
+
+
+def front_kernel(cube, parts, plan, *refs):
+    merged_in, xc_in, merged_out, xc_out, send, recv, local, t_send, t_recv, t_local = refs
+    cube.bind().barrier()
+    gathers = [Gather(cube, merged_in, merged_out, pl.ds(first, size), letters, send.at[k], recv.at[k])
+               for k, (first, size, letters) in enumerate(parts)]
     for gather in gathers:
         gather.start()
-    kept = []
-    for a in range(n_w):
-        kept.append(pltpu.make_async_copy(w_in[a], w_out[a].at[tuple(cube.mine)], local.at[a]))
-    exchanges = []
-    blk = cube.sizes[1]
-    for a in range(n_t):
-        clips = t_out[a].shape[0]
-        kept.append(pltpu.make_async_copy(
-            t_in[a].at[pl.ds(cube.at_blk * clips, clips)], t_out[a].at[:, cube.at_blk], t_local.at[a]))
-        for k in range(1, blk):
-            other = cube.row_peer(k)
-            exchanges.append(remote(
-                t_in[a].at[pl.ds(other[1] * clips, clips)], t_out[a].at[:, cube.at_blk],
-                t_send.at[a, k - 1], t_recv.at[a, k - 1], other))
-    for copy in kept + exchanges:
-        copy.start()
-    for copy in kept:
-        copy.wait()
-    for _ in range(cube.count):
-        for gather in gathers:
-            gather.advance()
-    for copy in exchanges:
-        copy.wait()
-
-
-def comm_in(weights, toks, dp, blk, parts, cid):
+    own = pltpu.make_async_copy(merged_in, merged_out.at[tuple(cube.mine)], local)
+    own.start()
+    exchange = Exchange(cube, xc_in, xc_out, False, t_send, t_recv, t_local)
+    own.wait()
+    for which in plan:
+        if which < 0:
+            exchange.start(-1 - which)
+        else:
+            gathers[which].advance()
+    for clip in range(exchange.clips):
+        exchange.wait(clip)
+
+
+def front(merged, xc, dp, blk, cid):
     cube = Cube(dp, blk)
-    n_w, n_t, n_p = len(weights), len(toks), len(parts)
+    clips = xc.shape[0] // blk
     anywhere = pl.BlockSpec(memory_space=pl.ANY)
-    outs = [jax.ShapeDtypeStruct((2,) * cube.count + w.shape, w.dtype) for w in weights]
-    outs += [jax.ShapeDtypeStruct((t.shape[0] // blk, blk) + t.shape[1:], t.dtype) for t in toks]
+    half = (merged.shape[1] // LANES + 1) // 2 * LANES
+    parts = [(0, half, "XbYa"), (half, merged.shape[1] - half, "XabY")]
+    plan = [0, 1] + [-1 - clip for clip in range(clips)] + [0, 1] * 4
     return pl.pallas_call(
-        functools.partial(comm_in_kernel, cube, parts, n_w, n_t),
-        in_specs=[anywhere] * (n_w + n_t),
-        out_specs=[anywhere] * (n_w + n_t),
-        out_shape=outs,
-        scratch_shapes=[
-            pltpu.SemaphoreType.DMA((n_p, cube.count)),
-            pltpu.SemaphoreType.DMA((n_p, cube.count)),
-            pltpu.SemaphoreType.DMA((n_w,)),
-            pltpu.SemaphoreType.DMA((max(n_t, 1), blk)),
-            pltpu.SemaphoreType.DMA((max(n_t, 1), blk)),
-            pltpu.SemaphoreType.DMA((max(n_t, 1),)),
-        ],
+        functools.partial(front_kernel, cube, parts, plan),
+        in_specs=[pl.BlockSpec(memory_space=pltpu.VMEM), anywhere],
+        out_specs=[anywhere] * 2,
+        out_shape=[jax.ShapeDtypeStruct((2,) * cube.count + merged.shape, BF16),
+                   jax.ShapeDtypeStruct((clips, blk) + xc.shape[1:], BF16)],
+        scratch_shapes=[pltpu.SemaphoreType.DMA((len(parts), cube.count)),
+                        pltpu.SemaphoreType.DMA((len(parts), cube.count)),
+                        pltpu.SemaphoreType.DMA] + exchange_semaphores(clips, blk),
         compiler_params=pltpu.CompilerParams(collective_id=cid, has_side_effects=True, vmem_limit_bytes=LIMIT),
-        name="comm_in",
-    )(*weights, *toks)
-
-
-def comm_out_kernel(cube, parts, n_w, n_t, *refs):
-    cube.bind()
-    w_in, t_in = refs[:n_w], refs[n_w:n_w + n_t]
-    refs = refs[n_w + n_t:]
-    w_out, norm, t_out = refs[:n_w], refs[n_w], refs[n_w + 1:n_w + 1 + n_t]
-    refs = refs[n_w + 1 + n_t:]
+        name="front",
+    )(merged, xc)
+
+
+def back_kernel(cube, parts, plan, *refs):
+    grads, early, toks = refs[:2], refs[2:4], refs[4]
+    outs, norm, home = refs[5:7], refs[7], refs[8]
+    refs = refs[9:]
     n_p = len(parts)
     held = refs[:n_p]
     landed = [refs[n_p + k * cube.count:n_p + (k + 1) * cube.count] for k in range(n_p)]
     send, recv, local, t_send, t_recv, t_local, sums, s_send, s_recv = refs[n_p * (1 + cube.count):]
     dp, blk = cube.sizes
-    cube.barrier()
-    reduces = [
-        Reduce(cube, w_in[a], pl.ds(start, size), cube.order(order), held[k], landed[k], w_out[a],
-               pl.ds(start, size), send.at[k], recv.at[k], local.at[k])
-        for k, (a, start, size, order) in enumerate(parts)]
+    cube.bind().barrier()
+    reduces = [Reduce(cube, grads[a], pl.ds(first, size), letters, held[k], landed[k], outs[a],
+                      send.at[k], recv.at[k], local.at[k])
+               for k, (a, first, size, letters) in enumerate(parts)]
     for reduce in reduces:
         reduce.start()
-    kept, exchanges = [], []
-    for a in range(n_t):
-        clips = t_in[a].shape[0]
-        here = pl.ds(cube.at_blk * clips, clips)
-        kept.append(pltpu.make_async_copy(t_in[a].at[:, cube.at_blk], t_out[a].at[here], t_local.at[a]))
-        for k in range(1, blk):
-            other = cube.row_peer(k)
-            exchanges.append(remote(t_in[a].at[:, other[1]], t_out[a].at[here],
-                                    t_send.at[a, k - 1], t_recv.at[a, k - 1], other))
-    for copy in kept + exchanges:
-        copy.start()
-    for _ in range(cube.count):
-        for reduce in reduces:
-            reduce.advance()
-    for copy in kept + exchanges:
-        copy.wait()
-    total = jnp.zeros((), F32)
-    for out in w_out:
+    exchange = Exchange(cube, toks, home, True, t_send, t_recv, t_local)
+    total = jnp.sum(early[0][...] * early[0][...]) + jnp.sum(early[1][...] * early[1][...])
+    for which in plan:
+        if which < 0:
+            exchange.start(-1 - which)
+        else:
+            reduces[which].advance()
+    for out in outs:
         total = total + jnp.sum(out[...] * out[...])
     for axis, (size, peer, at) in enumerate(((dp, cube.column_peer, cube.at_dp), (blk, cube.row_peer, cube.at_blk))):
         box = sums[axis]
@@ -635,40 +750,44 @@
             whole = whole + box[k]
         total = whole[0, 0]
     norm[...] = whole
-
-
-def comm_out(grads, toks, dp, blk, parts, cid):
+    for clip in range(exchange.clips):
+        exchange.wait(clip)
+
+
+def reduce_scratch(cube, shapes):
+    held = [pltpu.VMEM((2,) * (cube.count - 1) + s, BF16) for s in shapes]
+    landed = [pltpu.VMEM((2,) * (cube.count - 1 - k) + s, BF16) for s in shapes for k in range(cube.count)]
+    return held + landed + [pltpu.SemaphoreType.DMA((len(shapes), cube.count)),
+                            pltpu.SemaphoreType.DMA((len(shapes), cube.count)),
+                            pltpu.SemaphoreType.DMA((len(shapes),))]
+
+
+def back(merged, output, expand_share, shrink_share, dlt, dp, blk, cid):
     cube = Cube(dp, blk)
-    n_w, n_t, n_p = len(grads), len(toks), len(parts)
+    clips = dlt.shape[0]
     anywhere = pl.BlockSpec(memory_space=pl.ANY)
     inside = pl.BlockSpec(memory_space=pltpu.VMEM)
-    shards = [g.shape[-2:] for g in grads]
-    outs = [jax.ShapeDtypeStruct(s, F32) for s in shards] + [jax.ShapeDtypeStruct((8, LANES), F32)]
-    outs += [jax.ShapeDtypeStruct((t.shape[0] * blk,) + t.shape[2:], t.dtype) for t in toks]
-    held, landed = [], []
-    for a, _, size, _ in parts:
-        tail = (shards[a][0], size)
-        held.append(pltpu.VMEM((2,) * (cube.count - 1) + tail, BF16))
-        landed += [pltpu.VMEM((2,) * (cube.count - 1 - s) + tail, BF16) for s in range(cube.count)]
+    shards = [merged.shape[-2:], output.shape[-2:]]
+    third = shards[0][1] // LANES // 3 * LANES
+    parts = [(0, 0, shards[0][1] - 2 * third, "YbXa"), (0, shards[0][1] - 2 * third, third, "aYXb"),
+             (0, shards[0][1] - third, third, "aYXb"), (1, 0, shards[1][1], "YabX")]
+    plan = [0, 1, 2, 3] + [-1 - clip for clip in range(clips)] + [0, 1, 2, 3] * 4
     return pl.pallas_call(
-        functools.partial(comm_out_kernel, cube, parts, n_w, n_t),
-        in_specs=[anywhere] * (n_w + n_t),
-        out_specs=[inside] * (n_w + 1) + [anywhere] * n_t,
-        out_shape=outs,
-        scratch_shapes=held + landed + [
-            pltpu.SemaphoreType.DMA((n_p, cube.count)),
-            pltpu.SemaphoreType.DMA((n_p, cube.count)),
-            pltpu.SemaphoreType.DMA((n_p,)),
-            pltpu.SemaphoreType.DMA((max(n_t, 1), blk)),
-            pltpu.SemaphoreType.DMA((max(n_t, 1), blk)),
-            pltpu.SemaphoreType.DMA((max(n_t, 1),)),
+        functools.partial(back_kernel, cube, parts, plan),
+        in_specs=[anywhere] * 2 + [inside] * 2 + [anywhere],
+        out_specs=[inside] * 3 + [anywhere],
+        out_shape=[jax.ShapeDtypeStruct(s, F32) for s in shards] + [
+            jax.ShapeDtypeStruct((8, LANES), F32),
+            jax.ShapeDtypeStruct((clips * blk,) + dlt.shape[2:], BF16)],
+        scratch_shapes=reduce_scratch(cube, [(shards[a][0], size) for a, _, size, _ in parts])
+        + exchange_semaphores(clips, blk) + [
             [pltpu.VMEM((dp, 8, LANES), F32), pltpu.VMEM((blk, 8, LANES), F32)],
             [pltpu.SemaphoreType.DMA((dp,)), pltpu.SemaphoreType.DMA((blk,))],
             [pltpu.SemaphoreType.DMA((dp,)), pltpu.SemaphoreType.DMA((blk,))],
         ],
         compiler_params=pltpu.CompilerParams(collective_id=cid, has_side_effects=True, vmem_limit_bytes=LIMIT),
-        name="comm_out",
-    )(*grads, *toks)
+        name="back",
+    )(merged, output, expand_share, shrink_share, dlt)
 
 
 def key_columns(kept_time, kept_bands, blocks, own, segment, padded):
@@ -774,29 +893,29 @@
     merged_low = jnp.concatenate([weight_merged, columns], 1).astype(BF16)
     wide_low = jnp.concatenate([weight_output, weight_expand], 1).astype(BF16)
     xc_home, cot_home = prepare(tokens, cotangent, padded)
-    half = (merged_low.shape[1] // LANES + 1) // 2 * LANES
-    half_wide = wide_low.shape[1] // 2
-    merged, wide, shrink, xc, cot = comm_in(
-        [merged_low, wide_low, weight_shrink.astype(BF16)], [xc_home, cot_home], dp, blk,
-        [(0, 0, half, "XbYa"), (0, half, merged_low.shape[1] - half, "XabY"),
-         (1, 0, half_wide, "abXY"), (1, half_wide, half_wide, "XYab"), (2, 0, width, "bXYa")], 0)
+    shrink_low = weight_shrink.astype(BF16)
+    merged, xc = front(merged_low, xc_home, dp, blk, 0)
     merged = merged.reshape(width, merged_low.shape[1])
+    xc = xc.reshape(total, width)
+    vec = merged[:, 3 * width:3 * width + vectors.shape[0]].T.astype(F32)
+    dead = key_columns(kept_time, kept_bands, blk, own, segment, padded)
+    n1, qa, kv, mix, wide, shrink, cot = attn_fwd(
+        xc, dead, merged, vec, wide_low, shrink_low, cot_home, clips, HEADS, dp, blk, 1)
     wide = wide.reshape(width, wide_low.shape[1])
     shrink = shrink.reshape(ff, width)
-    xc, cot = xc.reshape(total, width), cot.reshape(total, width)
-    vec = merged[:, 3 * width:3 * width + vectors.shape[0]].T.astype(F32)
-    dead = key_columns(kept_time, kept_bands, blk, own, segment, padded)
-    n1, qa, kv, mix, mid = attn_fwd(xc, dead, merged, wide, vec, clips, HEADS)
-    act, dmid, grad_expand, grad_shrink, early = ffn(mid, xc, cot, wide, shrink, vec, blk * padded)
-    dlt, grad_merged, grad_output = attn_bwd(
-        xc, cot, dmid, dead, n1, qa, kv, mix, merged, wide, vec, early, clips, HEADS)
-    grads = [g.reshape(cube + (g.shape[0] // (dp * blk), g.shape[1]))
-             for g in (grad_merged, grad_output, grad_expand, grad_shrink)]
+    cot = cot.reshape(total, width)
+    act, dmid, grad_expand, grad_shrink, early = ffn(mix, xc, cot, wide, shrink, vec, blk * padded)
+
+    def by_device(grad):
+        return grad.reshape(cube + (grad.shape[0] // (dp * blk), grad.shape[1]))
+
     sent = (clips, blk, padded, width)
-    *shares, norm, act_home, dlt_home = comm_out(
-        grads, [act.reshape(sent), dlt.reshape(sent)], dp, blk,
-        [(0, 0, merged_low.shape[1], "YXba"), (1, 0, width, "aYXb"), (2, 0, ff // 2, "YbaX"),
-         (2, ff // 2, ff // 2, "YXab"), (3, 0, width, "aYXb")], 1)
+    dlt, grad_merged, grad_output, expand_share, shrink_share, act_home = attn_bwd(
+        xc, cot, dmid, dead, n1, qa, kv, mix, merged, wide, vec, early,
+        by_device(grad_expand), by_device(grad_shrink), act.reshape(sent), clips, HEADS, dp, blk, 2)
+    merged_share, output_share, norm, dlt_home = back(
+        by_device(grad_merged), by_device(grad_output), expand_share, shrink_share, dlt.reshape(sent), dp, blk, 3)
+    shares = [merged_share, output_share, expand_share, shrink_share]
     activations, token_grads = finish(tokens, cotangent, act_home, dlt_home)
     shares.append(shares[0][:, 3 * width:3 * width + vectors.shape[0]].T)
     shares[0] = shares[0][:, :3 * width]

time: 452 us -> 361 us (0.80)
  Pallas kernels: 432 us -> 342 us
    pallas_call x4, Pallas kernels: 335 us -> 241 us  [the longest x1 80.2 us: attn_bwd(): pl.pallas_call(functools.partial(attn_bwd_kernel, cube, parts, BWD_PLAN,...]
where the time goes in v3:
time: 361 us; the launch traced here: 360 us
  Pallas kernels  342 us (95%)
  other arithmetic  8.27 us (2%)
  local copies, waits for them, and re-layouts  7.74 us (2%)
    pallas_call x1, Pallas kernels, attn_bwd(): pl.pallas_call(functools.partial(attn_bwd_kernel, cube, parts, BWD_PLAN,...  80.2 us
    pallas_call x1, Pallas kernels, ffn(): pl.pallas_call(ffn_kernel, grid=(nf, ni), in_specs=[pl.BlockSpec((rows, w...  80 us
    pallas_call x1, Pallas kernels, attn_fwd(): pl.pallas_call(functools.partial(attn_fwd_kernel, cube, parts, FWD_PLAN,...  65.6 us
    pallas_call x1, Pallas kernels, back(): pl.pallas_call(functools.partial(back_kernel, cube, parts, plan), in_spec...  54.8 us
    pallas_call x1, Pallas kernels, front(): pl.pallas_call(functools.partial(front_kernel, cube, parts, plan), in_spe...  40.4 us
    pallas_call x1, Pallas kernels, finish(): pl.pallas_call(finish_kernel, grid=(clips // 2,), in_specs=[wide, wide, l...  9.52 us

profile of v3, /device:TPU:0, one launch (start us, length us, event | category | flops | bytes accessed | tf_op | source)
XLA Modules:
  0.0 360.4 jit_solution(3134387752523472036)
XLA Ops:
  0.7 0.1 pad.10.clone
  0.8 0.6 copy-done
  1.4 0.7 constant_dynamic-slice_fusion
  2.1 0.1 mul.27
  2.2 0.7 convert.17
  2.9 0.1 copy.50
  3.0 0.1 mul.31
  3.1 0.9 convert.18
  4.0 0.1 mul.28
  4.1 0.1 mul.29
  4.2 0.1 fusion.2
  4.3 0.9 convert.16
  5.3 0.7 fusion.1.refs_0_
  5.9 1.0 convert.19
  6.9 0.7 pad_maximum_fusion.wide_in
  7.6 1.6 convert_element_type.26.shrink_in
  9.2 1.0 select_convert_fusion.dead_ref
  10.3 7.2 %prepare.1 = (bf16[12,128,768]{2,1,0:T(8,128)(2,1)}, bf16[12,128,768]{2,1,0:T(8,128)(2,1)}) custom-call(f32[12,122,768]{2,1,0:T(8,128)} %tok_ref.3, f32[12,122,768]{2,1,0:T(8,128)} %cot_ref.3), custom_call_target="tpu_custom_call" | custom-call | tf_op jit(solution)/shard_map/prepare/pallas_call | solution.py:822
  17.4 40.4 %front.1 = (bf16[2,2,2,2,2,24,2432]{6,5,4,3,2,1,0:T(8,128)(2,1)}, bf16[3,4,128,768]{3,2,1,0:T(8,128)(2,1)}) custom-call(bf16[24,2432]{1,0:T(8,128)(2,1)} %fusion.1.refs_0_, bf16[12,128,768]{2,1,0:T(8,128)(2,1)} %get-tuple-element.71.refs_1_), custom_call_target="tpu_custom_call" | custom-call | tf_op jit(solution)/shard_map/front/pallas_call | solution.py:701
  57.8 0.9 slice.16
  58.7 0.1 copy.53
  58.8 0.6 convert_bitcast_fusion.vec_ref
  59.5 65.6 %attn_fwd.1 = (bf16[1536,768]{1,0:T(8,128)(2,1)}, bf16[12,1536,128]{2,1,0:T(8,128)(2,1)}, bf16[1536,1536]{1,0:T(8,128)(2,1)}, bf16[1536,768]{1,0:T(8,128)(2,1)},...) custom-call(bf16[1536,768]{1,0:T(8,128)(2,1)} %bitcast.22, ...), custom_call_target="tpu_custom_call" | custom-call | tf_op jit(solution)/shard_map/attn_fwd/pallas_call | solution.py:304
  125.1 80.0 %ffn.1 = (bf16[1536,768]{1,0:T(8,128)(2,1)}, f32[1536,768]{1,0:T(8,128)}, bf16[768,3072]{1,0:T(8,128)(2,1)}, bf16[3072,768]{1,0:T(8,128)(2,1)}, f32[16,768]{1,0:T(8,128)}) custom-call(bf16[1536,768]{1,0:T(8,128)(2,1)} %get-tuple-element.76.mix_ref, bf16[1536,768]{1,0:T(8,128)(2,1)} %bitcast.23, bf16[1536,768]{1,0:T(8,128)(2,1)} %bitcast.28, ...), custom_call_target="tpu_custom_call" | custom-call | tf_op jit(solution)/shard_map/ffn/pallas_call | solution.py:146
  205.1 80.2 %attn_bwd.1 = (bf16[1536,768]{1,0:T(8,128)(2,1)}, bf16[768,2432]{1,0:T(8,128)(2,1)}, bf16[768,768]{1,0:T(8,128)(2,1)}, f32[24,3072]{1,0:T(8,128)}, f32[96,768]{1,0:T(8,128)}, /*index=5*/bf16[12,128,768]{2,1,0:T(8,128)(2,1)}) custom-call(bf16[1536,768]{1,0:T(8,128)(2,1)} %bitcast.24, bf16[1536,768]{1,0:T(8,128)(2,1)} %bitcast.29, ...), custom_call_target="tpu_custom_call" | custom-call | tf_op jit(solution)/shard_map/attn_bwd/pallas_call | solution.py:454
  285.4 54.8 %back.1 = (f32[24,2432]{1,0:T(8,128)}, f32[24,768]{1,0:T(8,128)}, f32[8,128]{1,0:T(8,128)}, bf16[12,128,768]{2,1,0:T(8,128)(2,1)}) custom-call(bf16[2,2,2,2,2,24,2432]{6,5,4,3,2,1,0:T(8,128)(2,1)} %bitcast.33, bf16[2,2,2,2,2,24,768]{6,5,4,3,2,1,0:T(8,128)(2,1)} %bitcast.36, f32[24,3072]{1,0:T(8,128)} %get-tuple-element.90.refs_2_.refs_17_, ...), custom_call_target="tpu_custom_call" | custom-call | tf_op jit(solution)/shard_map/back/pallas_call | solution.py:775
  340.2 1.2 slice.13
  342.0 1.6 slice.14.refs_15_
  343.7 1.3 copy.52
  345.0 0.6 slice_bitcast_fusion.refs_19_
  345.6 4.1 %adamw.1 = (f32[24,2304]{1,0:T(8,128)}, f32[24,768]{1,0:T(8,128)}, f32[24,3072]{1,0:T(8,128)}, f32[96,768]{1,0:T(8,128)}, f32[12,24]{1,0:T(8,128)}, /*index=5*/f...) custom-call(f32[8,128]{1,0:T(8,128)} %get-tuple-element.96.norm_ref,, ...), custom_call_target="tpu_custom_call" | custom-call | tf_op jit(solution)/shard_map/adamw/pallas_call | solution.py:869
  349.8 9.5 %finish.1 = (f32[12,122,768]{2,1,0:T(8,128)}, f32[12,122,768]{2,1,0:T(8,128)}) custom-call(f32[12,122,768]{2,1,0:T(8,128)} %tok_ref.3, f32[12,122,768]{2,1,0:T(8,128)} %cot_ref.3, bf16[12,128,768]{2,1,0:T(8,128)(2,1)} %get-tuple-element.87.act_ref, bf16[12,128,768]{2,1,0:T(8,128)(2,1)} %get-tuple-element.93.dlt_ref), custom_call_target="tpu_custom_call" | custom-call | tf_op jit(solution)/shard_map/finish/pallas_call | solution.py:839
  (12 shorter events, 0.1 us)
Async XLA Ops:
  0.7 0.7 copy-start
  349.7 9.5 %copy-start.1 = (s32[12,48]{1,0:T(8,128)S(1)}, s32[12,48]{1,0:T(8,128)}, u32[]{:S(2)}) copy-start(s32[12,48]{1,0:T(8,128)} %param.20) | copy-start | bytes 6916

commit v4 on v3

--- a/solution.py
+++ b/solution.py
@@ -20,13 +20,20 @@
 EPS = 1e-06
 HALF = 64
 LANES = 128
-LIMIT = 62 * 1024 * 1024
+LIMIT = 127 * 512 * 1024
 MESH = pl.DeviceIdType.MESH
 
 FWD_PLAN = {1: [0, 2], 2: [1, 4], 4: [-1, 3], 5: [2], 6: [0, 1], 7: [-2], 10: [3, 4], 12: [0, 1], 14: [3], 15: [2],
             16: [4], -1: [-3, 1, 0, 3, 2, 4, 1, 0, 3, 2, 4]}
-BWD_PLAN = {0: [-1], 1: [0, 1], 2: [2], 3: [3, -2], 4: [4], 6: [1], 8: [-3, 0, 2], 9: [3], 10: [4], 12: [0, 1, 4],
-            15: [0, 3], 16: [2, 1], 17: [0], -1: [4, 3, 2, 1, 4, 3, 2]}
+FF_CHUNKS = 4
+FFN_LETTERS = ["aXYb", "aYXb"]
+FFN_ROOTS = ["XY", "XY"]
+FFN_PLAN = {8: [0, 2], 11: [0, 2], 13: [0, 2], 14: [1, 3], 15: [0], 17: [2, 3], 18: [1], 19: [0, 3], 20: [1], 22: [1],
+            23: [3], -1: [1]}
+BWD_LETTERS = ["YbaX", "bYaX", "aYbX"]
+BWD_ROOTS = ["YX", "XY"]
+BWD_PLAN = {0: [-1], 2: [0, 1, 2, 3, 4], 5: [-2], 6: [0, 4], 7: [1, 2, 3], 9: [4, -3], 11: [0, 1], 12: [2],
+            13: [4, 0, 3], 14: [1], 15: [2], -1: [3, 0, 1, 2]}
 
 
 def nn(a, b):
@@ -66,25 +73,39 @@
     return x * phi, phi + (0.3989422804014327 * x) * e
 
 
-def ffn_kernel(mix_ref, xc_ref, cot_ref, prj_ref, exp_ref, shr_ref, vec_ref,
-               act_ref, dmid_ref, ge_ref, gs_ref, sums_ref,
-               mid_s, n2_s, y_s, dn_s, ae_s, as_s):
+def ffn_kernel(cube, letters, plan, mix_ref, xc_ref, cot_ref, prj_ref, exp_ref, shr_ref, vec_ref,
+               act_ref, dmid_ref, ge_ref, gs_ref, go_ref, sums_ref, share_ref, shrink_ref,
+               n2_s, y_s, dn_s, ae_s, as_s, ao_s, *refs):
     f, i = pl.program_id(0), pl.program_id(1)
     nf, ni = pl.num_programs(0), pl.num_programs(1)
-    rows = mix_ref.shape[0]
+    rows, width = mix_ref.shape
     here = pl.ds(pl.multiple_of(i * rows, rows), rows)
+    cube.bind()
+    n_p = len(letters)
+    ready, held = refs[:n_p], refs[n_p:2 * n_p]
+    landed = [refs[2 * n_p + k * cube.count:2 * n_p + (k + 1) * cube.count] for k in range(n_p)]
+    refs = refs[n_p * (2 + cube.count):]
+    send, recv, local = refs[:3]
+    gs_ready, refs = refs[3:3 + n_p], refs[3 + n_p:]
+    reduces = [Reduce(cube, ready[k], slice(None), letters[k], held[k], landed[k],
+                      share_ref.at[:, pl.ds(k * width, width)], send.at[k], recv.at[k], local.at[k])
+               for k in range(n_p)]
+    reduces += root_reduces(cube, gs_ready, range(n_p), FF_CHUNKS, FFN_ROOTS, shrink_ref, refs)
+    points = Points(plan, reduces, None)
 
     @pl.when((f == 0) & (i == 0))
     def _():
+        cube.barrier()
+        shrink_ref[...] = jnp.zeros_like(shrink_ref)
         sums_ref[...] = jnp.zeros_like(sums_ref)
 
     @pl.when(f == 0)
     def _():
         mid = xc_ref[...].astype(F32) + nn(mix_ref[...], prj_ref[...]) + vec_ref[4:5, :]
-        mid_s[here, :] = mid
         xhat, _ = norm_stats(mid)
         n2_s[here, :] = (xhat * vec_ref[5:6, :] + vec_ref[6:7, :]).astype(BF16)
 
+    points.visit(2 * (f * ni + i), 0)
     n2 = n2_s[here, :]
     d2 = cot_ref[...]
     h = nn(n2, exp_ref[...]) + vec_ref[pl.ds(8 + f, 1), :]
@@ -96,19 +117,21 @@
     sums_ref[pl.ds(8 + f, 1), :] += jnp.sum(dh32, 0, keepdims=True)
     y = nn(g, shr_ref[...])
     dn = nt(dh, exp_ref[...])
+
+    @pl.when(f == 0)
+    def _():
+        y_s[here, :] = y
+        dn_s[here, :] = dn
+
+    @pl.when(f > 0)
+    def _():
+        y_s[here, :] += y
+        dn_s[here, :] += dn
+
+    points.visit(2 * (f * ni + i) + 1, 1)
     ge = tn(n2, dh)
     gs = tn(g, d2)
 
-    @pl.when(f == 0)
-    def _():
-        y_s[here, :] = y
-        dn_s[here, :] = dn
-
-    @pl.when(f > 0)
-    def _():
-        y_s[here, :] += y
-        dn_s[here, :] += dn
-
     @pl.when(i == 0)
     def _():
         ae_s[...] = ge
@@ -121,64 +144,116 @@
 
     @pl.when(i == ni - 1)
     def _():
-        ge_ref[...] = (ae_s[...] + ge).astype(ge_ref.dtype)
-        gs_ref[...] = (as_s[...] + gs).astype(gs_ref.dtype)
+        full_s = (as_s[...] + gs).astype(BF16)
+        full = (ae_s[...] + ge).astype(BF16)
+        for chunk in range(n_p):
+            @pl.when(f == chunk)
+            def _():
+                ready[chunk][...] = full.reshape(ready[chunk].shape)
+                reduces[chunk].start()
+                gs_ready[chunk][...] = full_s.reshape(gs_ready[chunk].shape)
+                reduces[n_p + chunk].start()
+
+        @pl.when(f >= n_p)
+        def _():
+            ge_ref[...] = full
+            gs_ref[...] = full_s
 
     @pl.when(f == nf - 1)
     def _():
-        mid = mid_s[here, :]
+        mix = mix_ref[...]
+        delta = nn(mix, prj_ref[...]) + vec_ref[4:5, :]
+        mid = xc_ref[...].astype(F32) + delta
         cot = d2.astype(F32)
         xhat, r = norm_stats(mid)
         dy = dn_s[here, :]
-        act_ref[...] = ((mid - xc_ref[...].astype(F32)) + (y_s[here, :] + vec_ref[7:8, :])).astype(BF16)
-        dmid_ref[...] = cot + norm_back(xhat, r, dy, vec_ref[5:6, :])
+        act_ref[...] = (delta + (y_s[here, :] + vec_ref[7:8, :])).astype(BF16)
+        dmid = cot + norm_back(xhat, r, dy, vec_ref[5:6, :])
+        dmid_ref[...] = dmid
+        d_one = dmid.astype(BF16)
+        sums_ref[4:5, :] += jnp.sum(d_one.astype(F32), 0, keepdims=True)
+        go = tn(mix, d_one)
+
+        @pl.when(i == 0)
+        def _():
+            ao_s[...] = go
+
+        @pl.when(i > 0)
+        def _():
+            ao_s[...] += go
+
+        @pl.when(i == ni - 1)
+        def _():
+            go_ref[...] = ao_s[...].astype(BF16)
+
         sums_ref[5:6, :] += jnp.sum(dy * xhat, 0, keepdims=True)
         sums_ref[6:7, :] += jnp.sum(dy, 0, keepdims=True)
         sums_ref[7:8, :] += jnp.sum(cot, 0, keepdims=True)
 
-
-def ffn(mix, xc, cot, expand, shrink, vec, rows):
+    @pl.when((f == nf - 1) & (i == ni - 1))
+    def _():
+        points.finish()
+
+
+def ffn(mix, xc, cot, expand, shrink, vec, rows, dp, blk, cid):
     total, width = xc.shape
+    cube = Cube(dp, blk)
     ff = expand.shape[1] - width
     nf, ni = ff // width, total // rows
+    letters = FFN_LETTERS
+    early = len(letters)
+    chunk = (width // (dp * blk), width)
+    own = (ff // (dp * blk), width)
     first = lambda f, i: (jnp.where((f == 0) | (f == nf - 1), i, ni - 1), 0)
     last = lambda f, i: (jnp.where(f == nf - 1, i, 0), 0)
+    once = pl.Buffered(1)
+    whole = lambda f, i: (0, 0)
     return pl.pallas_call(
-        ffn_kernel,
+        functools.partial(ffn_kernel, cube, letters, FFN_PLAN),
         grid=(nf, ni),
         in_specs=[
-            pl.BlockSpec((rows, width), lambda f, i: (jnp.where(f == 0, i, ni - 1), 0)),
+            pl.BlockSpec((rows, width), first),
             pl.BlockSpec((rows, width), first),
             pl.BlockSpec((rows, width), lambda f, i: (i, 0)),
-            pl.BlockSpec((width, width), lambda f, i: (0, 0)),
+            pl.BlockSpec((width, width), whole, pipeline_mode=once),
             pl.BlockSpec((width, width), lambda f, i: (0, f + 1)),
             pl.BlockSpec((width, width), lambda f, i: (f, 0)),
-            pl.BlockSpec(vec.shape, lambda f, i: (0, 0)),
+            pl.BlockSpec(vec.shape, whole),
         ],
         out_specs=[
             pl.BlockSpec((rows, width), last),
             pl.BlockSpec((rows, width), last),
-            pl.BlockSpec((width, width), lambda f, i: (0, f)),
-            pl.BlockSpec((width, width), lambda f, i: (f, 0)),
-            pl.BlockSpec((16, width), lambda f, i: (0, 0)),
+            pl.BlockSpec((width, width), lambda f, i: (0, jnp.maximum(f - early, 0)), pipeline_mode=once),
+            pl.BlockSpec((width, width), lambda f, i: (jnp.maximum(f - early, 0), 0), pipeline_mode=once),
+            pl.BlockSpec((width, width), whole, pipeline_mode=once),
+            pl.BlockSpec((16, width), whole),
+            pl.BlockSpec((chunk[0], width * early), whole, pipeline_mode=once),
+            pl.BlockSpec(own, whole, pipeline_mode=once),
         ],
         out_shape=[
             jax.ShapeDtypeStruct((total, width), BF16),
             jax.ShapeDtypeStruct((total, width), F32),
-            jax.ShapeDtypeStruct((width, ff), BF16),
-            jax.ShapeDtypeStruct((ff, width), BF16),
+            jax.ShapeDtypeStruct((width, ff - early * width), BF16),
+            jax.ShapeDtypeStruct((ff - early * width, width), BF16),
+            jax.ShapeDtypeStruct((width, width), BF16),
             jax.ShapeDtypeStruct((16, width), F32),
+            jax.ShapeDtypeStruct((chunk[0], width * early), F32),
+            jax.ShapeDtypeStruct(own, F32),
         ],
         scratch_shapes=[
-            pltpu.VMEM((total, width), F32),
             pltpu.VMEM((total, width), BF16),
             pltpu.VMEM((total, width), F32),
             pltpu.VMEM((total, width), F32),
             pltpu.VMEM((width, width), F32),
             pltpu.VMEM((width, width), F32),
-        ],
+            pltpu.VMEM((width, width), F32),
+        ] + [pltpu.VMEM((2,) * cube.count + chunk, BF16) for _ in letters]
+        + reduce_scratch(cube, [chunk] * early)
+        + [pltpu.VMEM((2,) * (cube.count - bits_of(FF_CHUNKS)) + own, BF16) for _ in letters]
+        + root_scratch(cube, early, FF_CHUNKS, own),
         compiler_params=pltpu.CompilerParams(
-            dimension_semantics=("arbitrary", "arbitrary"), vmem_limit_bytes=LIMIT),
+            dimension_semantics=("arbitrary", "arbitrary"), vmem_limit_bytes=LIMIT, collective_id=cid,
+            has_side_effects=True),
         name="ffn",
     )(mix, xc, cot, expand, expand, shrink, vec)
 
@@ -228,7 +303,7 @@
     ones = jnp.ones((seq, LANES), BF16)
 
     def pair(p, _):
-        points.visit(clip * pairs + p, False)
+        points.visit(clip * pairs + p)
         qcols = pl.ds(pl.multiple_of(p * LANES, LANES), LANES)
         kcols = pl.ds(pl.multiple_of(width + p * LANES, LANES), LANES)
         vcols = pl.ds(pl.multiple_of(2 * width + p * LANES, LANES), LANES)
@@ -271,24 +346,32 @@
 
 class Points:
     def __init__(self, plan, movers, exchange):
-        self.plan, self.movers, self.exchange = plan, movers, exchange
-
-    def act(self, which):
-        if which < 0:
-            self.exchange.start(-1 - which)
-        else:
-            self.movers[which].advance()
-
-    def visit(self, now, last):
-        for point in sorted(p for p in self.plan if p >= 0):
+        self.movers, self.exchange = movers, exchange
+        self.plan, taken = {}, {}
+        for point in sorted(plan, key=lambda p: p if p >= 0 else 1 << 20):
+            self.plan[point] = []
+            for which in plan[point]:
+                self.plan[point].append((which, taken.get(which, 0)))
+                taken[which] = taken.get(which, 0) + 1
+
+    def act(self, point):
+        for which, step in self.plan[point]:
+            if which < 0:
+                self.exchange.start(-1 - which)
+            else:
+                self.movers[which].advance(step)
+
+    def visit(self, now, parity=None):
+        for point in self.plan:
+            if point < 0 or (parity is not None and point % 2 != parity):
+                continue
+
             @pl.when(now == point)
             def _():
-                for which in self.plan[point]:
-                    self.act(which)
+                self.act(point)
 
     def finish(self):
-        for which in self.plan[-1]:
-            self.act(which)
+        self.act(-1)
 
 
 def attn_fwd(xc, dead, merged, vec, wide, shrink, cot, clips, heads, dp, blk, cid):
@@ -341,24 +424,39 @@
     )(xc, dead, merged, vec, wide, shrink, cot)
 
 
-def attn_bwd_kernel(cube, parts, plan, heads, xc_ref, cot_ref, dmid_ref, dead_ref, n1_ref, qa_ref, kv_ref, mix_ref,
-                    mrg_ref, out_ref, vec_ref, early_ref,
-                    ge_in, gs_in, act_in,
-                    dlt_ref, gm_ref, go_ref, ge_out, gs_out, act_out,
-                    dm_s, dp_s, am_s, ao_s, sums_ref, *refs):
+def attn_bwd_kernel(cube, late, tail, plan, heads, xc_ref, cot_ref, dmid_ref, dead_ref, n1_ref, qa_ref, kv_ref, mix_ref,
+                    mrg_ref, out_ref, vec_ref, early_ref, ge_early, gs_early,
+                    ge_in, gs_in, go_in, act_in,
+                    gm_out, gv_out, go_out, ge_out, gs_out, norm_ref, act_out, dlt_out,
+                    dm_s, dp_s, am_s, gm_s, gl_s, gw_s, gx_s, dlt_s, sums_ref, *refs):
     c = pl.program_id(0)
     n = pl.num_programs(0)
     seq, width = xc_ref.shape
     pairs = heads // 2
     cube.bind()
-    n_p = len(parts)
-    held = refs[:n_p]
-    landed = [refs[n_p + k * cube.count:n_p + (k + 1) * cube.count] for k in range(n_p)]
-    send, recv, local, t_send, t_recv, t_local = refs[n_p * (1 + cube.count):]
-    reduces = [Reduce(cube, (ge_in, gs_in)[a], pl.ds(first, size), letters, held[k], landed[k], (ge_out, gs_out)[a],
-                      send.at[k], recv.at[k], local.at[k])
-               for k, (a, first, size, letters) in enumerate(parts)]
-    exchange = Exchange(cube, act_in, act_out, True, t_send, t_recv, t_local)
+
+    def take(count):
+        nonlocal refs
+        taken, refs = refs[:count], refs[count:]
+        return taken
+
+    def sums_of(parts, sources, outs):
+        count = len(parts)
+        held = take(count)
+        landed = [take(cube.count) for _ in parts]
+        send, recv, local = take(3)
+        return [Reduce(cube, sources[a], pl.ds(first, size), letters, held[m], landed[m], outs[a],
+                       send.at[m], recv.at[m], local.at[m]) for m, (a, first, size, letters) in enumerate(parts)]
+
+    reduces = sums_of(late, (ge_in, go_in), (gx_s, go_out))
+    roots = FF_CHUNKS - gs_in.shape[0]
+    count = gs_in.shape[0]
+    reduces += root_reduces(cube, [gs_in.at[m] for m in range(count)], range(roots, FF_CHUNKS), FF_CHUNKS, BWD_ROOTS,
+                            gl_s, take(4 * count + count * (cube.count - bits_of(FF_CHUNKS)) - count + 3))
+    ends = sums_of(tail, (gm_s,), (gw_s,))
+    exchange = Exchange(cube, act_in, act_out, True, *take(3))
+    homeward = Exchange(cube, dlt_s, dlt_out, True, *take(3))
+    sums, s_send, s_recv = refs
     points = Points(plan, reduces, exchange)
 
     @pl.when(c == 0)
@@ -366,14 +464,12 @@
         cube.barrier()
         for reduce in reduces:
             reduce.start()
+        gl_s[...] = jnp.zeros_like(gl_s)
         sums_ref[...] = early_ref[...]
         am_s[...] = jnp.zeros_like(am_s)
-        ao_s[...] = jnp.zeros_like(ao_s)
 
     d_one = dmid_ref[...].astype(BF16)
     dm_s[...] = nt(d_one, out_ref[...]).astype(BF16)
-    ao_s[...] += tn(mix_ref[...], d_one)
-    sums_ref[4:5, :] += jnp.sum(d_one.astype(F32), 0, keepdims=True)
 
     lane = lax.broadcasted_iota(jnp.int32, (seq, LANES), 1)
     low = lane < HALF
@@ -382,7 +478,7 @@
     vone = jnp.where(in_half < 2, 1.0, 0.0).astype(BF16)
 
     def pair(p, _):
-        points.visit(c * pairs + p, False)
+        points.visit(c * pairs + p)
         qcols = pl.ds(pl.multiple_of(p * LANES, LANES), LANES)
         kcols = pl.ds(pl.multiple_of(width + p * LANES, LANES), LANES)
         vcols = pl.ds(pl.multiple_of(2 * width + p * LANES, LANES), LANES)
@@ -419,27 +515,66 @@
     lax.fori_loop(0, pairs, pair, 0)
     dp = dp_s[...]
     am_s[...] += tn(n1_ref[...], dp)
+
+    def by_device(values):
+        return values.astype(BF16).reshape((2,) * cube.count + (width // (1 << cube.count), values.shape[1]))
+
+    def hand_over(first, size):
+        def some(m, _):
+            cols = pl.ds(pl.multiple_of(first + m * LANES, LANES), LANES)
+            gm_s[(slice(None),) * (cube.count + 1) + (cols,)] = by_device(am_s[:, cols])
+            return 0
+
+        lax.fori_loop(0, size // LANES, some, 0)
+
+    @pl.when(c == n - 1)
+    def _():
+        for m, (_, first, size, _) in enumerate(tail[:-1]):
+            hand_over(first, size)
+            ends[m].start()
+
     dy = nt(dp, mrg_ref[:, :3 * width])
     xhat, r = norm_stats(xc_ref[...].astype(F32))
     sums_ref[0:1, :] += jnp.sum(dy * xhat, 0, keepdims=True)
     sums_ref[1:2, :] += jnp.sum(dy, 0, keepdims=True)
-    dlt_ref[...] = ((dmid_ref[...] - cot_ref[...].astype(F32))
-                    + norm_back(xhat, r, dy, vec_ref[0:1, :])).astype(BF16)
+    delta = ((dmid_ref[...] - cot_ref[...].astype(F32)) + norm_back(xhat, r, dy, vec_ref[0:1, :])).astype(BF16)
+    dlt_s[c] = delta.reshape(dlt_s.shape[1:])
+    for clip in range(homeward.clips):
+        @pl.when(c == clip)
+        def _():
+            homeward.start(clip)
 
     @pl.when(c == n - 1)
     def _():
-        gm_ref[:, :3 * width] = am_s[...].astype(gm_ref.dtype)
+        _, first, size, _ = tail[-1]
+        hand_over(first, 3 * width - first)
         columns = jnp.transpose(sums_ref[...])
-        gm_ref[:, 3 * width:] = jnp.concatenate(
-            [columns, jnp.zeros((width, LANES - columns.shape[1]), F32)], 1).astype(gm_ref.dtype)
-        go_ref[...] = ao_s[...].astype(go_ref.dtype)
+        blank = jnp.zeros((width, LANES - columns.shape[1]), F32)
+        gm_s[(slice(None),) * (cube.count + 1) + (pl.ds(3 * width, LANES),)] = by_device(
+            jnp.concatenate([columns, blank], 1))
+        ends[-1].start()
         points.finish()
-        for part in range(exchange.clips):
-            exchange.wait(part)
-
-
-def attn_bwd(xc, cot, dmid, dead, n1, qa, kv, mix, merged, output, vec, early,
-             grad_expand, grad_shrink, act, clips, heads, dp, blk, cid):
+        shrink = gs_early[...] + gl_s[...]
+        gs_out[...] = shrink
+        part = ge_early.shape[1]
+        ge_out[:, :part] = ge_early[...]
+        ge_out[:, part:] = gx_s[...]
+        total = jnp.sum(shrink * shrink) + jnp.sum(go_out[...] * go_out[...])
+        total = total + jnp.sum(ge_early[...] * ge_early[...]) + jnp.sum(gx_s[...] * gx_s[...])
+        for step in range(len(ends[0].steps)):
+            for end in ends:
+                end.advance(step)
+        gm_out[...] = gw_s[:, :3 * width]
+        gv_out[...] = gw_s[:, 3 * width:]
+        total = total + jnp.sum(gw_s[...] * gw_s[...])
+        norm_ref[...] = sum_everywhere(cube, total, sums, s_send, s_recv)
+        for clip in range(homeward.clips):
+            exchange.wait(clip)
+            homeward.wait(clip)
+
+
+def attn_bwd(xc, cot, dmid, dead, n1, qa, kv, mix, merged, output, vec, early, expand_early, shrink_early,
+             grad_expand, grad_shrink, grad_output, act, clips, heads, dp, blk, cid):
     total, width = xc.shape
     seq = total // clips
     cube = Cube(dp, blk)
@@ -447,12 +582,17 @@
     row = lambda c: (c, 0)
     once = pl.Buffered(1)
     anywhere = pl.BlockSpec(memory_space=pl.ANY)
-    shards = [grad_expand.shape[-2:], grad_shrink.shape[-2:]]
-    third, half = shards[0][1] // 3, shards[1][1] // 2
-    parts = [(0, 0, third, "bYaX"), (0, third, third, "YaXb"), (0, 2 * third, third, "YXab"),
-             (1, 0, half, "XbYa"), (1, half, half, "aYbX")]
+    rows, own = grad_expand.shape[-2], grad_shrink.shape[-2:]
+    half = grad_expand.shape[-1] // 2
+    third = merged.shape[1] // LANES // 3 * LANES
+    late = [(0, 0, half, BWD_LETTERS[0]), (0, half, half, BWD_LETTERS[1]), (1, 0, width, BWD_LETTERS[2])]
+    tail = [(0, 0, merged.shape[1] - 2 * third, "aYbX"), (0, merged.shape[1] - 2 * third, third, "XaYb"),
+            (0, merged.shape[1] - third, third, "YbaX")]
+    fixed = [(rows, 3 * width), (rows, merged.shape[1] - 3 * width), (rows, width),
+             (rows, expand_early.shape[1] + 2 * half), own, (8, LANES)]
+    home = (clips * blk,) + act.shape[2:]
     return pl.pallas_call(
-        functools.partial(attn_bwd_kernel, cube, parts, BWD_PLAN, heads),
+        functools.partial(attn_bwd_kernel, cube, late, tail, BWD_PLAN, heads),
         grid=(clips,),
         in_specs=[
             pl.BlockSpec((seq, width), row),
@@ -467,36 +607,31 @@
             pl.BlockSpec((width, width), whole, pipeline_mode=once),
             pl.BlockSpec(vec.shape, whole),
             pl.BlockSpec(early.shape, whole),
-            anywhere, anywhere, anywhere,
+            pl.BlockSpec(expand_early.shape, whole, pipeline_mode=once),
+            pl.BlockSpec(shrink_early.shape, whole, pipeline_mode=once),
+            anywhere, anywhere, anywhere, anywhere,
         ],
-        out_specs=[
-            pl.BlockSpec((seq, width), row),
-            pl.BlockSpec(merged.shape, whole, pipeline_mode=once),
-            pl.BlockSpec((width, width), whole, pipeline_mode=once),
-            pl.BlockSpec(shards[0], whole, pipeline_mode=once),
-            pl.BlockSpec(shards[1], whole, pipeline_mode=once),
-            anywhere,
-        ],
-        out_shape=[
-            jax.ShapeDtypeStruct((total, width), BF16),
-            jax.ShapeDtypeStruct(merged.shape, BF16),
-            jax.ShapeDtypeStruct((width, width), BF16),
-            jax.ShapeDtypeStruct(shards[0], F32),
-            jax.ShapeDtypeStruct(shards[1], F32),
-            jax.ShapeDtypeStruct((clips * blk,) + act.shape[2:], BF16),
-        ],
+        out_specs=[pl.BlockSpec(s, whole, pipeline_mode=once) for s in fixed] + [anywhere, anywhere],
+        out_shape=[jax.ShapeDtypeStruct(s, F32) for s in fixed] + [jax.ShapeDtypeStruct(home, BF16)] * 2,
         scratch_shapes=[
             pltpu.VMEM((seq, width), BF16),
             pltpu.VMEM((seq, 3 * width), BF16),
             pltpu.VMEM((width, 3 * width), F32),
-            pltpu.VMEM((width, width), F32),
+            pltpu.VMEM((2,) * cube.count + (rows, merged.shape[1]), BF16),
+            pltpu.VMEM(own, F32),
+            pltpu.VMEM((rows, merged.shape[1]), F32),
+            pltpu.VMEM((rows, 2 * half), F32),
+            pltpu.VMEM(act.shape, BF16),
             pltpu.VMEM((16, width), F32),
-        ] + reduce_scratch(cube, [(shards[a][0], size) for a, _, size, _ in parts])
-        + exchange_semaphores(clips, blk),
+        ] + reduce_scratch(cube, [(rows, size) for _, _, size, _ in late])
+        + root_scratch(cube, grad_shrink.shape[0], FF_CHUNKS, own)
+        + reduce_scratch(cube, [(rows, size) for _, _, size, _ in tail])
+        + exchange_semaphores(clips, blk) + exchange_semaphores(clips, blk) + sum_scratch(dp, blk),
         compiler_params=pltpu.CompilerParams(
             dimension_semantics=("arbitrary",), vmem_limit_bytes=LIMIT, collective_id=cid, has_side_effects=True),
         name="attn_bwd",
-    )(xc, cot, dmid, dead, n1, qa, kv, mix, merged, output, vec, early, grad_expand, grad_shrink, act)
+    )(xc, cot, dmid, dead, n1, qa, kv, mix, merged, output, vec, early, expand_early, shrink_early,
+      grad_expand, grad_shrink, grad_output, act)
 
 
 def bits_of(size):
@@ -550,7 +685,7 @@
         self.cube, self.src, self.dst, self.cols = cube, src, dst, cols
         self.steps = [cube.letters[letter] for letter in letters + "C"]
         self.order = sum(self.steps, [])
-        self.send, self.recv, self.step = send, recv, 0
+        self.send, self.recv = send, recv
 
     def copy(self, s):
         cube = self.cube
@@ -560,30 +695,29 @@
         return remote(here, there, self.send.at[s], self.recv.at[s], cube.partner(self.order[s]))
 
     def start(self):
-        self.done = 0
         self.copy(0).start()
 
-    def advance(self):
-        for _ in self.steps[self.step]:
-            self.copy(self.done).wait()
-            self.done += 1
-            if self.done < len(self.order):
-                self.copy(self.done).start()
-        self.step += 1
+    def advance(self, step):
+        first = sum(len(bits) for bits in self.steps[:step])
+        for s in range(first, first + len(self.steps[step])):
+            self.copy(s).wait()
+            if s + 1 < len(self.order):
+                self.copy(s + 1).start()
 
 
 class Reduce:
     def __init__(self, cube, src, cols, letters, held, landed, out, send, recv, local):
         self.cube, self.src, self.cols, self.held, self.landed = cube, src, cols, held, landed
+        self.dims = range(cube.count)
         self.steps = [cube.letters[letter] for letter in "C" + letters]
         self.order = sum(self.steps, [])
         self.out = out
-        self.send, self.recv, self.local, self.step = send, recv, local, 0
+        self.send, self.recv, self.local = send, recv, local
 
     def part(self, s, kept):
         cube = self.cube
         sel = []
-        for bit in range(cube.count):
+        for bit in self.dims:
             if bit in self.order[:s]:
                 pick = cube.mine[bit]
             elif bit == self.order[s]:
@@ -605,7 +739,6 @@
         return remote(here, self.landed[s], self.send.at[s], self.recv.at[s], self.cube.partner(self.order[s]))
 
     def start(self):
-        self.done = 0
         self.own().start()
         self.copy(0).start()
 
@@ -613,7 +746,7 @@
         keep = self.part(s, True)[:-1]
         width = self.held.shape[-1]
         if s + 1 == len(self.order):
-            self.out[:, self.cols] = self.held[keep].astype(F32) + self.landed[s][...].astype(F32)
+            self.last(self.held[keep].astype(F32) + self.landed[s][...].astype(F32))
             return
         wide = (slice(None),) * (len(self.landed[s].shape) - 1)
         tile = LANES * max(k for k in (1, 2, 3) if width % (LANES * k) == 0)
@@ -626,17 +759,90 @@
 
         lax.fori_loop(0, width // tile, some, 0)
 
-    def advance(self):
-        for _ in self.steps[self.step]:
-            s = self.done
+    def last(self, total):
+        self.out[:, self.cols] = total
+
+    def advance(self, step):
+        first = sum(len(bits) for bits in self.steps[:step])
+        for s in range(first, first + len(self.steps[step])):
             self.copy(s).wait()
             if s == 0:
                 self.own().wait()
             self.add(s)
-            self.done += 1
-            if self.done < len(self.order):
-                self.copy(self.done).start()
-        self.step += 1
+            if s + 1 < len(self.order):
+                self.copy(s + 1).start()
+
+
+class RootReduce(Reduce):
+    def __init__(self, cube, chunk, chunks, src, letters, held, landed, partial, arrived, out, send, recv, local):
+        lead = bits_of(chunks)
+        super().__init__(cube, src, slice(None), letters, held, landed, out, send, recv, local)
+        self.dims = range(lead, cube.count)
+        near = {"X": cube.letters["X"], "Y": [b for b in cube.letters["b"] + cube.letters["a"] if b >= lead] + cube.letters["Y"]}
+        self.steps = [cube.letters["C"]] + [near[letter] for letter in letters]
+        self.order = sum(self.steps, [])
+        self.chunk, self.chunks, self.partial, self.arrived = chunk, chunks, partial, arrived
+        self.group = cube.at_dp // (cube.sizes[0] // chunks)
+
+    def owner(self):
+        cube, size = self.cube, self.cube.sizes[0] // self.chunks
+        slot = lax.rem(self.group + 2 * self.chunks - self.chunk - 1, self.chunks)
+        base = len(self.order)
+        return remote(self.partial, self.arrived.at[slot], self.send.at[base], self.recv.at[base + slot],
+                      (cube.at_dp + (self.chunk - self.group) * size, cube.at_blk))
+
+    def last(self, total):
+        @pl.when(self.group == self.chunk)
+        def _():
+            self.out[...] = total
+
+        @pl.when(self.group != self.chunk)
+        def _():
+            self.partial[...] = total.astype(BF16)
+            self.owner().start()
+
+    def advance(self, step):
+        if step < len(self.steps):
+            super().advance(step)
+            return
+
+        @pl.when(self.group == self.chunk)
+        def _():
+            base = len(self.order)
+            total = self.out[...]
+            for slot in range(self.chunks - 1):
+                remote(self.partial, self.arrived.at[slot], self.send.at[base], self.recv.at[base + slot],
+                       (self.cube.at_dp, self.cube.at_blk)).wait_recv()
+                total = total + self.arrived[slot].astype(F32)
+            self.out[...] = total
+
+        @pl.when(self.group != self.chunk)
+        def _():
+            self.owner().wait_send()
+
+
+def root_scratch(cube, count, chunks, tail):
+    rest = cube.count - bits_of(chunks)
+    kinds = []
+    for _ in range(count):
+        kinds.append(pltpu.VMEM((2,) * (rest - 1) + tail, BF16))
+    for _ in range(count):
+        kinds += [pltpu.VMEM((2,) * (rest - 1 - s) + tail, BF16) for s in range(rest)]
+    for _ in range(count):
+        kinds += [pltpu.VMEM(tail, BF16), pltpu.VMEM((chunks - 1,) + tail, BF16)]
+    sems = rest + chunks
+    return kinds + [pltpu.SemaphoreType.DMA((count, sems)), pltpu.SemaphoreType.DMA((count, sems)),
+                    pltpu.SemaphoreType.DMA((count,))]
+
+
+def root_reduces(cube, sources, names, chunks, letters, out, refs):
+    count, rest = len(names), cube.count - bits_of(chunks)
+    held = refs[:count]
+    landed = [refs[count + n * rest:count + (n + 1) * rest] for n in range(count)]
+    refs = refs[count * (1 + rest):]
+    send, recv, local = refs[2 * count:2 * count + 3]
+    return [RootReduce(cube, names[n], chunks, sources[n], letters[n], held[n], landed[n], refs[2 * n], refs[2 * n + 1],
+                       out, send.at[n], recv.at[n], local.at[n]) for n in range(count)]
 
 
 class Exchange:
@@ -682,11 +888,8 @@
     own.start()
     exchange = Exchange(cube, xc_in, xc_out, False, t_send, t_recv, t_local)
     own.wait()
-    for which in plan:
-        if which < 0:
-            exchange.start(-1 - which)
-        else:
-            gathers[which].advance()
+    points = Points({-1: plan}, gathers, exchange)
+    points.finish()
     for clip in range(exchange.clips):
         exchange.wait(clip)
 
@@ -712,34 +915,12 @@
     )(merged, xc)
 
 
-def back_kernel(cube, parts, plan, *refs):
-    grads, early, toks = refs[:2], refs[2:4], refs[4]
-    outs, norm, home = refs[5:7], refs[7], refs[8]
-    refs = refs[9:]
-    n_p = len(parts)
-    held = refs[:n_p]
-    landed = [refs[n_p + k * cube.count:n_p + (k + 1) * cube.count] for k in range(n_p)]
-    send, recv, local, t_send, t_recv, t_local, sums, s_send, s_recv = refs[n_p * (1 + cube.count):]
+def sum_everywhere(cube, total, sums, send, recv):
     dp, blk = cube.sizes
-    cube.bind().barrier()
-    reduces = [Reduce(cube, grads[a], pl.ds(first, size), letters, held[k], landed[k], outs[a],
-                      send.at[k], recv.at[k], local.at[k])
-               for k, (a, first, size, letters) in enumerate(parts)]
-    for reduce in reduces:
-        reduce.start()
-    exchange = Exchange(cube, toks, home, True, t_send, t_recv, t_local)
-    total = jnp.sum(early[0][...] * early[0][...]) + jnp.sum(early[1][...] * early[1][...])
-    for which in plan:
-        if which < 0:
-            exchange.start(-1 - which)
-        else:
-            reduces[which].advance()
-    for out in outs:
-        total = total + jnp.sum(out[...] * out[...])
     for axis, (size, peer, at) in enumerate(((dp, cube.column_peer, cube.at_dp), (blk, cube.row_peer, cube.at_blk))):
         box = sums[axis]
         box[at] = jnp.full(box.shape[1:], total, F32)
-        copies = [remote(box.at[at], box.at[at], s_send[axis].at[k - 1], s_recv[axis].at[k - 1], peer(k))
+        copies = [remote(box.at[at], box.at[at], send[axis].at[k - 1], recv[axis].at[k - 1], peer(k))
                   for k in range(1, size)]
         for copy in copies:
             copy.start()
@@ -749,9 +930,13 @@
         for k in range(1, size):
             whole = whole + box[k]
         total = whole[0, 0]
-    norm[...] = whole
-    for clip in range(exchange.clips):
-        exchange.wait(clip)
+    return whole
+
+
+def sum_scratch(dp, blk):
+    return [[pltpu.VMEM((dp, 8, LANES), F32), pltpu.VMEM((blk, 8, LANES), F32)],
+            [pltpu.SemaphoreType.DMA((dp,)), pltpu.SemaphoreType.DMA((blk,))],
+            [pltpu.SemaphoreType.DMA((dp,)), pltpu.SemaphoreType.DMA((blk,))]]
 
 
 def reduce_scratch(cube, shapes):
@@ -760,34 +945,6 @@
     return held + landed + [pltpu.SemaphoreType.DMA((len(shapes), cube.count)),
                             pltpu.SemaphoreType.DMA((len(shapes), cube.count)),
                             pltpu.SemaphoreType.DMA((len(shapes),))]
-
-
-def back(merged, output, expand_share, shrink_share, dlt, dp, blk, cid):
-    cube = Cube(dp, blk)
-    clips = dlt.shape[0]
-    anywhere = pl.BlockSpec(memory_space=pl.ANY)
-    inside = pl.BlockSpec(memory_space=pltpu.VMEM)
-    shards = [merged.shape[-2:], output.shape[-2:]]
-    third = shards[0][1] // LANES // 3 * LANES
-    parts = [(0, 0, shards[0][1] - 2 * third, "YbXa"), (0, shards[0][1] - 2 * third, third, "aYXb"),
-             (0, shards[0][1] - third, third, "aYXb"), (1, 0, shards[1][1], "YabX")]
-    plan = [0, 1, 2, 3] + [-1 - clip for clip in range(clips)] + [0, 1, 2, 3] * 4
-    return pl.pallas_call(
-        functools.partial(back_kernel, cube, parts, plan),
-        in_specs=[anywhere] * 2 + [inside] * 2 + [anywhere],
-        out_specs=[inside] * 3 + [anywhere],
-        out_shape=[jax.ShapeDtypeStruct(s, F32) for s in shards] + [
-            jax.ShapeDtypeStruct((8, LANES), F32),
-            jax.ShapeDtypeStruct((clips * blk,) + dlt.shape[2:], BF16)],
-        scratch_shapes=reduce_scratch(cube, [(shards[a][0], size) for a, _, size, _ in parts])
-        + exchange_semaphores(clips, blk) + [
-            [pltpu.VMEM((dp, 8, LANES), F32), pltpu.VMEM((blk, 8, LANES), F32)],
-            [pltpu.SemaphoreType.DMA((dp,)), pltpu.SemaphoreType.DMA((blk,))],
-            [pltpu.SemaphoreType.DMA((dp,)), pltpu.SemaphoreType.DMA((blk,))],
-        ],
-        compiler_params=pltpu.CompilerParams(collective_id=cid, has_side_effects=True, vmem_limit_bytes=LIMIT),
-        name="back",
-    )(merged, output, expand_share, shrink_share, dlt)
 
 
 def key_columns(kept_time, kept_bands, blocks, own, segment, padded):
@@ -904,21 +1061,20 @@
     wide = wide.reshape(width, wide_low.shape[1])
     shrink = shrink.reshape(ff, width)
     cot = cot.reshape(total, width)
-    act, dmid, grad_expand, grad_shrink, early = ffn(mix, xc, cot, wide, shrink, vec, blk * padded)
+    act, dmid, grad_expand, grad_shrink, grad_output, early, expand_early, shrink_early = ffn(
+        mix, xc, cot, wide, shrink, vec, blk * padded, dp, blk, 2)
 
     def by_device(grad):
         return grad.reshape(cube + (grad.shape[0] // (dp * blk), grad.shape[1]))
 
     sent = (clips, blk, padded, width)
-    dlt, grad_merged, grad_output, expand_share, shrink_share, act_home = attn_bwd(
-        xc, cot, dmid, dead, n1, qa, kv, mix, merged, wide, vec, early,
-        by_device(grad_expand), by_device(grad_shrink), act.reshape(sent), clips, HEADS, dp, blk, 2)
-    merged_share, output_share, norm, dlt_home = back(
-        by_device(grad_merged), by_device(grad_output), expand_share, shrink_share, dlt.reshape(sent), dp, blk, 3)
-    shares = [merged_share, output_share, expand_share, shrink_share]
+    owners = (2,) * (len(cube) - bits_of(FF_CHUNKS))
+    merged_share, vector_share, output_share, expand_share, shrink_share, norm, act_home, dlt_home = attn_bwd(
+        xc, cot, dmid, dead, n1, qa, kv, mix, merged, wide, vec, early, expand_early, shrink_early,
+        by_device(grad_expand), grad_shrink.reshape((-1,) + owners + weight_shrink.shape), by_device(grad_output),
+        act.reshape(sent), clips, HEADS, dp, blk, 3)
+    shares = [merged_share, output_share, expand_share, shrink_share, vector_share[:, :vectors.shape[0]].T]
     activations, token_grads = finish(tokens, cotangent, act_home, dlt_home)
-    shares.append(shares[0][:, 3 * width:3 * width + vectors.shape[0]].T)
-    shares[0] = shares[0][:, :3 * width]
     steps_out = adamw(
         norm, (weight_merged, weight_output, weight_expand, weight_shrink, vectors),
         (first_merged, first_output, first_expand, first_shrink, first_vectors),

time: 361 us -> 346 us (0.958)
  Pallas kernels: 342 us -> 329 us
    pallas_call x3 -> x2, Pallas kernels: 215 us -> 202 us  [the longest x1 106 us: attn_bwd(): pl.pallas_call(functools.partial(attn_bwd_kernel, cube, late, tail, BWD_P...]
where the time goes in v4:
time: 346 us; the launch traced here: 345 us
  Pallas kernels  329 us (95%)
  other arithmetic  8.28 us (2%)
  local copies, waits for them, and re-layouts  5.57 us (2%)
    pallas_call x1, Pallas kernels, attn_bwd(): pl.pallas_call(functools.partial(attn_bwd_kernel, cube, late, tail, BWD_P...  106 us
    pallas_call x1, Pallas kernels, ffn(): pl.pallas_call(functools.partial(ffn_kernel, cube, letters, FFN_PLAN), gr...  95.5 us
    pallas_call x1, Pallas kernels, attn_fwd(): pl.pallas_call(functools.partial(attn_fwd_kernel, cube, parts, FWD_PLAN,...  65.6 us
    pallas_call x1, Pallas kernels, front(): pl.pallas_call(functools.partial(front_kernel, cube, parts, plan), in_spe...  40.4 us
    pallas_call x1, Pallas kernels, finish(): pl.pallas_call(finish_kernel, grid=(clips // 2,), in_specs=[wide, wide, l...  9.52 us
    pallas_call x1, Pallas kernels, prepare(): pl.pallas_call(prepare_kernel, grid=(clips // 2,), in_specs=[wide, wide],...  7.16 us

profile of v4, /device:TPU:0, one launch (start us, length us, event | category | flops | bytes accessed | tf_op | source)
XLA Modules:
  0.0 345.1 jit_solution(1538151629527435930)
XLA Ops:
  0.7 0.0 copy-start
  0.7 0.1 pad.10.clone
  0.8 0.6 copy-done
  1.4 0.7 constant_dynamic-slice_fusion
  2.1 0.1 mul.27
  2.2 0.7 convert.17
  2.9 0.1 copy.50
  3.0 0.1 broadcast_in_dim.52
  3.0 0.1 mul.31
  3.1 0.9 convert.18
  4.0 0.1 mul.28
  4.1 0.1 mul.29
  4.2 0.1 fusion.2
  4.3 0.9 convert.16
  5.3 0.7 fusion.1.refs_0_
  5.9 1.0 convert.19
  6.9 0.7 pad_maximum_fusion.wide_in
  7.6 1.6 convert_element_type.26.shrink_in
  9.2 1.0 select_convert_fusion.dead_ref
  10.3 7.2 %prepare.1 = (bf16[12,128,768]{2,1,0:T(8,128)(2,1)}, bf16[12,128,768]{2,1,0:T(8,128)(2,1)}) custom-call(f32[12,122,768]{2,1,0:T(8,128)} %tok_ref.3, f32[12,122,768]{2,1,0:T(8,128)} %cot_ref.3), custom_call_target="tpu_custom_call" | custom-call | tf_op jit(solution)/shard_map/prepare/pallas_call | solution.py:979
  17.4 40.4 %front.1 = (bf16[2,2,2,2,2,24,2432]{6,5,4,3,2,1,0:T(8,128)(2,1)}, bf16[3,4,128,768]{3,2,1,0:T(8,128)(2,1)}) custom-call(bf16[24,2432]{1,0:T(8,128)(2,1)} %fusion.1.refs_0_, bf16[12,128,768]{2,1,0:T(8,128)(2,1)} %get-tuple-element.72.refs_1_), custom_call_target="tpu_custom_call" | custom-call | tf_op jit(solution)/shard_map/front/pallas_call | solution.py:904
  57.8 0.9 slice.12
  58.7 0.1 copy.53
  58.9 0.6 convert_bitcast_fusion.vec_ref
  59.5 65.6 %attn_fwd.1 = (bf16[1536,768]{1,0:T(8,128)(2,1)}, bf16[12,1536,128]{2,1,0:T(8,128)(2,1)}, bf16[1536,1536]{1,0:T(8,128)(2,1)}, bf16[1536,768]{1,0:T(8,128)(2,1)},...) custom-call(bf16[1536,768]{1,0:T(8,128)(2,1)} %bitcast.20, ...), custom_call_target="tpu_custom_call" | custom-call | tf_op jit(solution)/shard_map/attn_fwd/pallas_call | solution.py:387
  125.1 95.5 %ffn.1 = (bf16[1536,768]{1,0:T(8,128)(2,1)}, f32[1536,768]{1,0:T(8,128)}, bf16[768,1536]{1,0:T(8,128)(2,1)}, bf16[1536,768]{1,0:T(8,128)(2,1)}, bf16[768,768]{1,...) custom-call(bf16[1536,768]{1,0:T(8,128)(2,1)} %get-tuple-element.77.mix_ref, ...), custom_call_target="tpu_custom_call" | custom-call | tf_op jit(solution)/shard_map/ffn/pallas_call | solution.py:211
  220.6 106.4 %attn_bwd.1 = (f32[24,2304]{1,0:T(8,128)}, f32[24,128]{1,0:T(8,128)}, f32[24,768]{1,0:T(8,128)}, f32[24,3072]{1,0:T(8,128)}, f32[96,768]{1,0:T(8,128)}, /*index=...) custom-call(bf16[1536,768]{1,0:T(8,128)(2,1)} %bitcast.22, bf16[1536,768]{1,0:T(8,128)(2,1)} %bitcast.27, ...), custom_call_target="tpu_custom_call" | custom-call | tf_op jit(solution)/shard_map/attn_bwd/pallas_call | solution.py:594
  327.0 1.2 slice.10
  328.9 0.8 copy.52
  329.7 0.6 slice_bitcast_fusion.refs_19_
  330.3 4.2 %adamw.1 = (f32[24,2304]{1,0:T(8,128)}, f32[24,768]{1,0:T(8,128)}, f32[24,3072]{1,0:T(8,128)}, f32[96,768]{1,0:T(8,128)}, f32[12,24]{1,0:T(8,128)}, /*index=5*/f...) custom-call(f32[8,128]{1,0:T(8,128)} %get-tuple-element.95.norm_ref,, ...), custom_call_target="tpu_custom_call" | custom-call | tf_op jit(solution)/shard_map/adamw/pallas_call | solution.py:1026
  334.5 9.5 %finish.1 = (f32[12,122,768]{2,1,0:T(8,128)}, f32[12,122,768]{2,1,0:T(8,128)}) custom-call(f32[12,122,768]{2,1,0:T(8,128)} %tok_ref.3, f32[12,122,768]{2,1,0:T(8,128)} %cot_ref.3, bf16[12,128,768]{2,1,0:T(8,128)(2,1)} %get-tuple-element.91.act_ref, bf16[12,128,768]{2,1,0:T(8,128)(2,1)} %get-tuple-element.92.dlt_ref), custom_call_target="tpu_custom_call" | custom-call | tf_op jit(solution)/shard_map/finish/pallas_call | solution.py:996
  (10 shorter events, 0.1 us)
Async XLA Ops:
  0.7 0.7 copy-start
  334.5 9.5 %copy-start.1 = (s32[12,48]{1,0:T(8,128)S(1)}, s32[12,48]{1,0:T(8,128)}, u32[]{:S(2)}) copy-start(s32[12,48]{1,0:T(8,128)} %param.20) | copy-start | bytes 6916

commit v5 on v4

--- a/solution.py
+++ b/solution.py
@@ -34,6 +34,8 @@
 BWD_ROOTS = ["YX", "XY"]
 BWD_PLAN = {0: [-1], 2: [0, 1, 2, 3, 4], 5: [-2], 6: [0, 4], 7: [1, 2, 3], 9: [4, -3], 11: [0, 1], 12: [2],
             13: [4, 0, 3], 14: [1], 15: [2], -1: [3, 0, 1, 2]}
+END_LETTERS = ["abYX", "XYab", "YbaX", "XYba", "XaYb"]
+END_PLAN = {4: [0], 6: [1], 7: [0, 2, 3, 4], -1: [1, 2, 3, 4, 0, 1, 3, 4, 2, 0, 1, 4, 2, 3, 0, 1, 4, 2, 3]}
 
 
 def nn(a, b):
@@ -361,9 +363,9 @@
             else:
                 self.movers[which].advance(step)
 
-    def visit(self, now, parity=None):
+    def visit(self, now, at=None, period=2, limit=1 << 20):
         for point in self.plan:
-            if point < 0 or (parity is not None and point % 2 != parity):
+            if point < 0 or point >= limit or (at is not None and point % period != at):
                 continue
 
             @pl.when(now == point)
@@ -428,7 +430,7 @@
                     mrg_ref, out_ref, vec_ref, early_ref, ge_early, gs_early,
                     ge_in, gs_in, go_in, act_in,
                     gm_out, gv_out, go_out, ge_out, gs_out, norm_ref, act_out, dlt_out,
-                    dm_s, dp_s, am_s, gm_s, gl_s, gw_s, gx_s, dlt_s, sums_ref, *refs):
+                    dm_s, dp_s, nt_s, am_s, gm_s, gl_s, gw_s, gx_s, dlt_s, sums_ref, *refs):
     c = pl.program_id(0)
     n = pl.num_programs(0)
     seq, width = xc_ref.shape
@@ -458,6 +460,7 @@
     homeward = Exchange(cube, dlt_s, dlt_out, True, *take(3))
     sums, s_send, s_recv = refs
     points = Points(plan, reduces, exchange)
+    finale = Points(END_PLAN, ends, None)
 
     @pl.when(c == 0)
     def _():
@@ -470,6 +473,11 @@
 
     d_one = dmid_ref[...].astype(BF16)
     dm_s[...] = nt(d_one, out_ref[...]).astype(BF16)
+    nt_s[...] = jnp.transpose(n1_ref[...])
+    group = 3 * LANES
+
+    def by_device(values):
+        return values.astype(BF16).reshape((2,) * cube.count + (width // (1 << cube.count), values.shape[1]))
 
     lane = lax.broadcasted_iota(jnp.int32, (seq, LANES), 1)
     low = lane < HALF
@@ -479,6 +487,7 @@
 
     def pair(p, _):
         points.visit(c * pairs + p)
+        finale.visit(jnp.where(c == n - 1, p, -1), limit=pairs)
         qcols = pl.ds(pl.multiple_of(p * LANES, LANES), LANES)
         kcols = pl.ds(pl.multiple_of(width + p * LANES, LANES), LANES)
         vcols = pl.ds(pl.multiple_of(2 * width + p * LANES, LANES), LANES)
@@ -507,31 +516,30 @@
         dv = jnp.where(low, dvs[0], dvs[1])
         sums_ref[2:3, qcols] += jnp.sum(dq, 0, keepdims=True)
         sums_ref[3:4, qcols] += jnp.sum(dv, 0, keepdims=True)
-        dp_s[:, qcols] = dq.astype(BF16)
-        dp_s[:, kcols] = dk.astype(BF16)
-        dp_s[:, vcols] = dv.astype(BF16)
+        three = jnp.concatenate([dq, dk, dv], 1).astype(BF16)
+        dp_s[:, qcols] = three[:, :LANES]
+        dp_s[:, kcols] = three[:, LANES:2 * LANES]
+        dp_s[:, vcols] = three[:, 2 * LANES:]
+        mine = pl.ds(pl.multiple_of(p * group, group), group)
+        grad = am_s[:, mine] + nn(nt_s[...], three)
+        am_s[:, mine] = grad
+
+        @pl.when(c == n - 1)
+        def _():
+            gm_s[(slice(None),) * (cube.count + 1) + (mine,)] = by_device(grad)
+            for m, (_, first, size, _) in enumerate(tail[:-1]):
+                @pl.when(first + size == (p + 1) * group)
+                def _():
+                    ends[m].start()
+
         return 0
 
     lax.fori_loop(0, pairs, pair, 0)
     dp = dp_s[...]
-    am_s[...] += tn(n1_ref[...], dp)
-
-    def by_device(values):
-        return values.astype(BF16).reshape((2,) * cube.count + (width // (1 << cube.count), values.shape[1]))
-
-    def hand_over(first, size):
-        def some(m, _):
-            cols = pl.ds(pl.multiple_of(first + m * LANES, LANES), LANES)
-            gm_s[(slice(None),) * (cube.count + 1) + (cols,)] = by_device(am_s[:, cols])
-            return 0
-
-        lax.fori_loop(0, size // LANES, some, 0)
 
     @pl.when(c == n - 1)
     def _():
-        for m, (_, first, size, _) in enumerate(tail[:-1]):
-            hand_over(first, size)
-            ends[m].start()
+        finale.act(pairs)
 
     dy = nt(dp, mrg_ref[:, :3 * width])
     xhat, r = norm_stats(xc_ref[...].astype(F32))
@@ -539,21 +547,22 @@
     sums_ref[1:2, :] += jnp.sum(dy, 0, keepdims=True)
     delta = ((dmid_ref[...] - cot_ref[...].astype(F32)) + norm_back(xhat, r, dy, vec_ref[0:1, :])).astype(BF16)
     dlt_s[c] = delta.reshape(dlt_s.shape[1:])
-    for clip in range(homeward.clips):
+    for clip in range(homeward.clips - 1):
         @pl.when(c == clip)
         def _():
             homeward.start(clip)
 
     @pl.when(c == n - 1)
     def _():
-        _, first, size, _ = tail[-1]
-        hand_over(first, 3 * width - first)
         columns = jnp.transpose(sums_ref[...])
         blank = jnp.zeros((width, LANES - columns.shape[1]), F32)
         gm_s[(slice(None),) * (cube.count + 1) + (pl.ds(3 * width, LANES),)] = by_device(
             jnp.concatenate([columns, blank], 1))
         ends[-1].start()
+        finale.act(pairs + 1)
+        homeward.start(homeward.clips - 1)
         points.finish()
+        finale.finish()
         shrink = gs_early[...] + gl_s[...]
         gs_out[...] = shrink
         part = ge_early.shape[1]
@@ -561,10 +570,10 @@
         ge_out[:, part:] = gx_s[...]
         total = jnp.sum(shrink * shrink) + jnp.sum(go_out[...] * go_out[...])
         total = total + jnp.sum(ge_early[...] * ge_early[...]) + jnp.sum(gx_s[...] * gx_s[...])
-        for step in range(len(ends[0].steps)):
-            for end in ends:
-                end.advance(step)
-        gm_out[...] = gw_s[:, :3 * width]
+        for p in range(pairs):
+            for third in range(3):
+                gm_out[:, third * width + p * LANES:third * width + (p + 1) * LANES] = (
+                    gw_s[:, p * group + third * LANES:p * group + (third + 1) * LANES])
         gv_out[...] = gw_s[:, 3 * width:]
         total = total + jnp.sum(gw_s[...] * gw_s[...])
         norm_ref[...] = sum_everywhere(cube, total, sums, s_send, s_recv)
@@ -584,10 +593,10 @@
     anywhere = pl.BlockSpec(memory_space=pl.ANY)
     rows, own = grad_expand.shape[-2], grad_shrink.shape[-2:]
     half = grad_expand.shape[-1] // 2
-    third = merged.shape[1] // LANES // 3 * LANES
     late = [(0, 0, half, BWD_LETTERS[0]), (0, half, half, BWD_LETTERS[1]), (1, 0, width, BWD_LETTERS[2])]
-    tail = [(0, 0, merged.shape[1] - 2 * third, "aYbX"), (0, merged.shape[1] - 2 * third, third, "XaYb"),
-            (0, merged.shape[1] - third, third, "YbaX")]
+    sixth = width // 2
+    cuts = [0, 2 * sixth, 4 * sixth, 5 * sixth, 6 * sixth, merged.shape[1]]
+    tail = [(0, cuts[m], cuts[m + 1] - cuts[m], END_LETTERS[m]) for m in range(5)]
     fixed = [(rows, 3 * width), (rows, merged.shape[1] - 3 * width), (rows, width),
              (rows, expand_early.shape[1] + 2 * half), own, (8, LANES)]
     home = (clips * blk,) + act.shape[2:]
@@ -616,6 +625,7 @@
         scratch_shapes=[
             pltpu.VMEM((seq, width), BF16),
             pltpu.VMEM((seq, 3 * width), BF16),
+            pltpu.VMEM((width, seq), BF16),
             pltpu.VMEM((width, 3 * width), F32),
             pltpu.VMEM((2,) * cube.count + (rows, merged.shape[1]), BF16),
             pltpu.VMEM(own, F32),
@@ -962,49 +972,59 @@
     return jnp.where(lane == 0, bias, jnp.where(lane < 4, 1.0, 0.0)).astype(BF16)
 
 
-def prepare_kernel(tok_ref, cot_ref, xc_ref, low_ref):
-    segment, extra = tok_ref.shape[1], xc_ref.shape[1] - tok_ref.shape[1]
+def prepare_kernel(tok_ref, cot_ref, mrg_ref, col_ref, out_ref, exp_ref, shr_ref,
+                   xc_ref, low_ref, merged_ref, wide_ref, shrink_ref):
+    extra = xc_ref.shape[1] - tok_ref.shape[1]
     values = tok_ref[...]
     centred = (values - jnp.mean(values, -1, keepdims=True)).astype(BF16)
     blank = jnp.zeros((values.shape[0], extra, values.shape[2]), BF16)
     xc_ref[...] = jnp.concatenate([centred, blank], 1)
     low_ref[...] = jnp.concatenate([cot_ref[...].astype(BF16), blank], 1)
 
-
-def prepare(tokens, cotangent, padded):
+    @pl.when(pl.program_id(0) == 0)
+    def _():
+        first = mrg_ref.shape[1]
+        merged_ref[:, :first] = mrg_ref[...].astype(BF16)
+        merged_ref[:, first:] = col_ref[...].astype(BF16)
+        first = out_ref.shape[1]
+        wide_ref[:, :first] = out_ref[...].astype(BF16)
+        wide_ref[:, first:] = exp_ref[...].astype(BF16)
+        shrink_ref[...] = shr_ref[...].astype(BF16)
+
+
+def prepare(tokens, cotangent, merged, columns, output, expand, shrink, padded):
     clips, segment, width = tokens.shape
-    wide = pl.BlockSpec((2, segment, width), lambda i: (i, 0, 0))
-    out = pl.BlockSpec((2, padded, width), lambda i: (i, 0, 0))
+    some = 3 if clips % 3 == 0 else 1
+    wide = pl.BlockSpec((some, segment, width), lambda i: (i, 0, 0))
+    out = pl.BlockSpec((some, padded, width), lambda i: (i, 0, 0))
     shape = jax.ShapeDtypeStruct((clips, padded, width), BF16)
+    shards = [(merged.shape[0], merged.shape[1] + columns.shape[1]),
+              (output.shape[0], output.shape[1] + expand.shape[1]), shrink.shape]
     return pl.pallas_call(
-        prepare_kernel, grid=(clips // 2,), in_specs=[wide, wide], out_specs=[out, out], out_shape=[shape, shape],
+        prepare_kernel, grid=(clips // some,),
+        in_specs=[wide, wide] + [pl.BlockSpec(w.shape, lambda i: (0, 0)) for w in (merged, columns, output, expand, shrink)],
+        out_specs=[out, out] + [pl.BlockSpec(s, lambda i: (0, 0)) for s in shards],
+        out_shape=[shape, shape] + [jax.ShapeDtypeStruct(s, BF16) for s in shards],
         compiler_params=pltpu.CompilerParams(dimension_semantics=("arbitrary",), vmem_limit_bytes=LIMIT),
-        name="prepare")(tokens, cotangent)
-
-
-def finish_kernel(tok_ref, cot_ref, act_ref, dlt_ref, out_ref, grad_ref):
+        name="prepare")(tokens, cotangent, merged, columns, output, expand, shrink)
+
+
+RATES = (MATRIX_RATE, MATRIX_RATE, MATRIX_RATE, MATRIX_RATE, VECTOR_RATE)
+DECAYS = (MATRIX_DECAY, MATRIX_DECAY, MATRIX_DECAY, MATRIX_DECAY, 0.0)
+
+
+def finish_kernel(tok_ref, cot_ref, act_ref, dlt_ref, norm_ref, *refs):
+    refs, out_ref, grad_ref = refs[:-2], refs[-2], refs[-1]
     segment = tok_ref.shape[1]
     out_ref[...] = tok_ref[...] + act_ref[...].astype(F32)[:, :segment]
     grad_ref[...] = cot_ref[...] + dlt_ref[...].astype(F32)[:, :segment]
 
-
-def finish(tokens, cotangent, act, dlt):
-    clips, segment, width = tokens.shape
-    wide = pl.BlockSpec((2, segment, width), lambda i: (i, 0, 0))
-    low = pl.BlockSpec((2,) + act.shape[1:], lambda i: (i, 0, 0))
-    shape = jax.ShapeDtypeStruct(tokens.shape, F32)
-    return pl.pallas_call(
-        finish_kernel, grid=(clips // 2,), in_specs=[wide, wide, low, low], out_specs=[wide, wide],
-        out_shape=[shape, shape],
-        compiler_params=pltpu.CompilerParams(dimension_semantics=("arbitrary",), vmem_limit_bytes=LIMIT),
-        name="finish")(tokens, cotangent, act, dlt)
-
-
-RATES = (MATRIX_RATE, MATRIX_RATE, MATRIX_RATE, MATRIX_RATE, VECTOR_RATE)
-DECAYS = (MATRIX_DECAY, MATRIX_DECAY, MATRIX_DECAY, MATRIX_DECAY, 0.0)
-
-
-def adamw_kernel(norm_ref, *refs):
+    @pl.when(pl.program_id(0) == 0)
+    def _():
+        adamw_step(norm_ref, *refs)
+
+
+def adamw_step(norm_ref, *refs):
     weights, firsts, seconds, shares = refs[:5], refs[5:10], refs[10:15], refs[15:20]
     outs = refs[20:]
     factor = CLIP_LIMIT / jnp.maximum(jnp.sqrt(norm_ref[0:1, 0:1]), CLIP_LIMIT)
@@ -1021,13 +1041,19 @@
             outs[5 * kind + index][...] = value
 
 
-def adamw(norm, weights, firsts, seconds, shares):
-    inside = pl.BlockSpec(memory_space=pltpu.VMEM)
+def finish(tokens, cotangent, act, dlt, norm, weights, firsts, seconds, shares):
+    clips, segment, width = tokens.shape
+    some = 3 if clips % 3 == 0 else 1
+    wide = pl.BlockSpec((some, segment, width), lambda i: (i, 0, 0))
+    low = pl.BlockSpec((some,) + act.shape[1:], lambda i: (i, 0, 0))
+    fixed = [pl.BlockSpec(a.shape, lambda i: (0, 0))
+             for a in (norm, *weights, *firsts, *seconds, *shares)]
+    outs = [jax.ShapeDtypeStruct(w.shape, F32) for w in weights] * 4 + [jax.ShapeDtypeStruct(tokens.shape, F32)] * 2
     return pl.pallas_call(
-        adamw_kernel, in_specs=[inside] * 21, out_specs=[inside] * 20,
-        out_shape=[jax.ShapeDtypeStruct(w.shape, F32) for w in weights] * 4,
-        compiler_params=pltpu.CompilerParams(vmem_limit_bytes=LIMIT),
-        name="adamw")(norm, *weights, *firsts, *seconds, *shares)
+        finish_kernel, grid=(clips // some,), in_specs=[wide, wide, low, low] + fixed,
+        out_specs=[pl.BlockSpec(w.shape, lambda i: (0, 0)) for w in weights] * 4 + [wide, wide], out_shape=outs,
+        compiler_params=pltpu.CompilerParams(dimension_semantics=("arbitrary",), vmem_limit_bytes=LIMIT),
+        name="finish")(tokens, cotangent, act, dlt, norm, *weights, *firsts, *seconds, *shares)
 
 
 def shards(
@@ -1047,10 +1073,8 @@
     cube = (2,) * (bits_of(dp) + bits_of(blk))
 
     columns = jnp.pad(vectors.T, ((0, 0), (0, LANES - vectors.shape[0])))
-    merged_low = jnp.concatenate([weight_merged, columns], 1).astype(BF16)
-    wide_low = jnp.concatenate([weight_output, weight_expand], 1).astype(BF16)
-    xc_home, cot_home = prepare(tokens, cotangent, padded)
-    shrink_low = weight_shrink.astype(BF16)
+    xc_home, cot_home, merged_low, wide_low, shrink_low = prepare(
+        tokens, cotangent, weight_merged, columns, weight_output, weight_expand, weight_shrink, padded)
     merged, xc = front(merged_low, xc_home, dp, blk, 0)
     merged = merged.reshape(width, merged_low.shape[1])
     xc = xc.reshape(total, width)
@@ -1074,9 +1098,8 @@
         by_device(grad_expand), grad_shrink.reshape((-1,) + owners + weight_shrink.shape), by_device(grad_output),
         act.reshape(sent), clips, HEADS, dp, blk, 3)
     shares = [merged_share, output_share, expand_share, shrink_share, vector_share[:, :vectors.shape[0]].T]
-    activations, token_grads = finish(tokens, cotangent, act_home, dlt_home)
-    steps_out = adamw(
-        norm, (weight_merged, weight_output, weight_expand, weight_shrink, vectors),
+    *steps_out, activations, token_grads = finish(
+        tokens, cotangent, act_home, dlt_home, norm, (weight_merged, weight_output, weight_expand, weight_shrink, vectors),
         (first_merged, first_output, first_expand, first_shrink, first_vectors),
         (second_merged, second_output, second_expand, second_shrink, second_vectors), shares)
     return (activations, token_grads, jnp.sqrt(norm[0, 0]), *steps_out)

time: 346 us -> 328 us (0.948)
  Pallas kernels: 329 us -> 316 us
  other arithmetic: 8.28 us -> 1.77 us
    pallas_call x1, Pallas kernels: 106 us -> 95.7 us  [attn_bwd(): pl.pallas_call(functools.partial(attn_bwd_kernel, cube, late, tail, BWD_P...]
    another operation x4 -> x0, other arithmetic: 3.52 us -> none
    pallas_call x3 -> x2, Pallas kernels: 20.8 us -> 19.1 us  [the longest x1 12.4 us: finish(): pl.pallas_call(finish_kernel, grid=(clips // some,), in_specs=[wide, wide...]
where the time goes in v5:
time: 328 us; the launch traced here: 327 us
  Pallas kernels  316 us (96%)
  local copies, waits for them, and re-layouts  6.85 us (2%)
    pallas_call x1, Pallas kernels, attn_bwd(): pl.pallas_call(functools.partial(attn_bwd_kernel, cube, late, tail, BWD_P...  95.7 us
    pallas_call x1, Pallas kernels, ffn(): pl.pallas_call(functools.partial(ffn_kernel, cube, letters, FFN_PLAN), gr...  95.4 us
    pallas_call x1, Pallas kernels, attn_fwd(): pl.pallas_call(functools.partial(attn_fwd_kernel, cube, parts, FWD_PLAN,...  65.6 us
    pallas_call x1, Pallas kernels, front(): pl.pallas_call(functools.partial(front_kernel, cube, parts, plan), in_spe...  40.4 us
    pallas_call x1, Pallas kernels, finish(): pl.pallas_call(finish_kernel, grid=(clips // some,), in_specs=[wide, wide...  12.4 us
    pallas_call x1, Pallas kernels, prepare(): pl.pallas_call(prepare_kernel, grid=(clips // some,), in_specs=[wide, wid...  6.69 us

profile of v5, /device:TPU:0, one launch (start us, length us, event | category | flops | bytes accessed | tf_op | source)
XLA Modules:
  0.0 327.5 jit_solution(12644957482267155904)
XLA Ops:
  0.7 0.0 copy-start
  0.7 0.1 pad.7.clone
  0.8 0.6 copy-done
  1.4 0.7 constant_dynamic-slice_fusion
  2.1 0.1 mul.27
  2.2 0.1 broadcast_in_dim.52
  2.2 0.8 copy.47
  3.0 0.6 pad.4.col_ref
  3.6 0.1 mul.31
  3.7 0.1 mul.28
  3.8 0.1 mul.29
  3.9 0.1 fusion
  4.0 1.0 select_convert_fusion.dead_ref
  5.0 6.7 %prepare.1 = (bf16[12,128,768]{2,1,0:T(8,128)(2,1)}, bf16[12,128,768]{2,1,0:T(8,128)(2,1)}, bf16[24,2432]{1,0:T(8,128)(2,1)}, bf16[24,3840]{1,0:T(8,128)(2,1)}, bf16[96,768]{1,0:T(8,128)(2,1)}) custom-call(f32[12,122,768]{2,1,0:T(8,128)} %tok_ref.3, f32[12,122,768]{2,1,0:T(8,128)} %cot_ref.3, f32[24,2304]{1,0:T(8,128)} %refs_0_.1, f32[24,128]{1,0:T(8,128)} %pad.4.col_ref, ...), custom_call_target="tpu_custom_call" | custom-call | tf_op jit(solution)/shard_map/prepare/pallas_call | solution.py:1003
  11.7 40.4 %front.1 = (bf16[2,2,2,2,2,24,2432]{6,5,4,3,2,1,0:T(8,128)(2,1)}, bf16[3,4,128,768]{3,2,1,0:T(8,128)(2,1)}) custom-call(bf16[24,2432]{1,0:T(8,128)(2,1)} %get-tuple-element.75.refs_0_, bf16[12,128,768]{2,1,0:T(8,128)(2,1)} %get-tuple-element.76.refs_1_), custom_call_target="tpu_custom_call" | custom-call | tf_op jit(solution)/shard_map/front/pallas_call | solution.py:914
  52.1 0.9 slice.12
  53.0 0.1 copy.50
  53.2 0.6 convert_bitcast_fusion.vec_ref
  53.8 65.6 %attn_fwd.1 = (bf16[1536,768]{1,0:T(8,128)(2,1)}, bf16[12,1536,128]{2,1,0:T(8,128)(2,1)}, bf16[1536,1536]{1,0:T(8,128)(2,1)}, bf16[1536,768]{1,0:T(8,128)(2,1)},...) custom-call(bf16[1536,768]{1,0:T(8,128)(2,1)} %bitcast.20, ...), custom_call_target="tpu_custom_call" | custom-call | tf_op jit(solution)/shard_map/attn_fwd/pallas_call | solution.py:389
  119.4 95.4 %ffn.1 = (bf16[1536,768]{1,0:T(8,128)(2,1)}, f32[1536,768]{1,0:T(8,128)}, bf16[768,1536]{1,0:T(8,128)(2,1)}, bf16[1536,768]{1,0:T(8,128)(2,1)}, bf16[768,768]{1,...) custom-call(bf16[1536,768]{1,0:T(8,128)(2,1)} %get-tuple-element.83.mix_ref, ...), custom_call_target="tpu_custom_call" | custom-call | tf_op jit(solution)/shard_map/ffn/pallas_call | solution.py:213
  214.9 95.7 %attn_bwd.1 = (f32[24,2304]{1,0:T(8,128)}, f32[24,128]{1,0:T(8,128)}, f32[24,768]{1,0:T(8,128)}, f32[24,3072]{1,0:T(8,128)}, f32[96,768]{1,0:T(8,128)}, /*index=...) custom-call(bf16[1536,768]{1,0:T(8,128)(2,1)} %bitcast.22, bf16[1536,768]{1,0:T(8,128)(2,1)} %bitcast.27, ...), custom_call_target="tpu_custom_call" | custom-call | tf_op jit(solution)/shard_map/attn_bwd/pallas_call | solution.py:603
  310.7 1.2 slice.11
  312.5 0.8 copy.49
  313.3 0.6 slice_bitcast_fusion.refs_19_
  313.9 0.0 copy-start.1
  313.9 12.4 %finish.1 = (f32[24,2304]{1,0:T(8,128)}, f32[24,768]{1,0:T(8,128)}, f32[24,3072]{1,0:T(8,128)}, f32[96,768]{1,0:T(8,128)}, f32[12,24]{1,0:T(8,128)}, /*index=5*/...) custom-call(f32[12,122,768]{2,1,0:T(8,128)} %tok_ref.3, ...), custom_call_target="tpu_custom_call" | custom-call | tf_op jit(solution)/shard_map/finish/pallas_call | solution.py:1052
  326.4 0.0 copy-done.1
  (8 shorter events, 0.1 us)
Async XLA Ops:
  0.7 0.7 copy-start
  313.9 12.4 %copy-start.1 = (s32[12,48]{1,0:T(8,128)S(1)}, s32[12,48]{1,0:T(8,128)}, u32[]{:S(2)}) copy-start(s32[12,48]{1,0:T(8,128)} %param.20) | copy-start | bytes 6916

commit v6 on v5

--- a/solution.py
+++ b/solution.py
@@ -23,8 +23,10 @@
 LIMIT = 127 * 512 * 1024
 MESH = pl.DeviceIdType.MESH
 
-FWD_PLAN = {1: [0, 2], 2: [1, 4], 4: [-1, 3], 5: [2], 6: [0, 1], 7: [-2], 10: [3, 4], 12: [0, 1], 14: [3], 15: [2],
-            16: [4], -1: [-3, 1, 0, 3, 2, 4, 1, 0, 3, 2, 4]}
+FWD_LETTERS = ["XaYb", "baXY", "abYX", "abXY", "bXYa", "aYbX", "XbaY", "bXYa"]
+FWD_PLAN = {1: [-1], 3: [0], 4: [2, 1, 6, 3], 5: [4, 5], 6: [7, 0], 7: [5, 1, 2], 9: [4, -2], 10: [7, 6], 11: [0],
+            12: [1, 3, 2], 13: [4], 16: [7, 5, 6], 17: [-3],
+            -1: [3, 1, 2, 1, 2, 0, 4, 6, 0, 4, 5, 6, 3, 7, 5, 3, 7]}
 FF_CHUNKS = 4
 FFN_LETTERS = ["aXYb", "aYXb"]
 FFN_ROOTS = ["XY", "XY"]
@@ -383,9 +385,9 @@
     whole = lambda c: (0, 0)
     row = lambda c: (c, 0)
     anywhere = pl.BlockSpec(memory_space=pl.ANY)
-    third, half = wide.shape[1] // 3, shrink.shape[1] // 2
-    parts = [(0, 0, third, "XbYa"), (0, third, third, "baXY"), (0, 2 * third, third, "YXba"),
-             (1, 0, half, "baYX"), (1, half, half, "XbaY")]
+    fifth, third = wide.shape[1] // 5, shrink.shape[1] // 3
+    parts = [(0, m * fifth, fifth, FWD_LETTERS[m]) for m in range(5)]
+    parts += [(1, m * third, third, FWD_LETTERS[5 + m]) for m in range(3)]
     return pl.pallas_call(
         functools.partial(attn_fwd_kernel, cube, parts, FWD_PLAN, heads),
         grid=(clips,),

time: 328 us -> 325 us (level)
  no operation moved by 1% of the time
where the time goes in v6:
time: 325 us
  Pallas kernels  313 us (96%)
  local copies, waits for them, and re-layouts  6.85 us (2%)
    pallas_call x1, Pallas kernels, attn_bwd(): pl.pallas_call(functools.partial(attn_bwd_kernel, cube, late, tail, BWD_P...  94.8 us
    pallas_call x1, Pallas kernels, ffn(): pl.pallas_call(functools.partial(ffn_kernel, cube, letters, FFN_PLAN), gr...  94 us
    pallas_call x1, Pallas kernels, attn_fwd(): pl.pallas_call(functools.partial(attn_fwd_kernel, cube, parts, FWD_PLAN,...  65 us
    pallas_call x1, Pallas kernels, front(): pl.pallas_call(functools.partial(front_kernel, cube, parts, plan), in_spe...  40.4 us
    pallas_call x1, Pallas kernels, finish(): pl.pallas_call(finish_kernel, grid=(clips // some,), in_specs=[wide, wide...  12.4 us
    pallas_call x1, Pallas kernels, prepare(): pl.pallas_call(prepare_kernel, grid=(clips // some,), in_specs=[wide, wid...  6.69 us

profile of v6, /device:TPU:0, one launch (start us, length us, event | category | flops | bytes accessed | tf_op | source)
XLA Modules:
  0.0 324.5 jit_solution(16996826680732458001)
XLA Ops:
  0.7 0.0 copy-start
  0.7 0.1 pad.7.clone
  0.8 0.6 copy-done
  1.4 0.7 constant_dynamic-slice_fusion
  2.1 0.1 mul.27
  2.2 0.1 broadcast_in_dim.52
  2.2 0.8 copy.47
  3.0 0.6 pad.4.col_ref
  3.6 0.1 mul.31
  3.7 0.1 mul.28
  3.8 0.1 mul.29
  3.9 0.1 fusion
  4.0 1.0 select_convert_fusion.dead_ref
  5.0 6.7 %prepare.1 = (bf16[12,128,768]{2,1,0:T(8,128)(2,1)}, bf16[12,128,768]{2,1,0:T(8,128)(2,1)}, bf16[24,2432]{1,0:T(8,128)(2,1)}, bf16[24,3840]{1,0:T(8,128)(2,1)}, bf16[96,768]{1,0:T(8,128)(2,1)}) custom-call(f32[12,122,768]{2,1,0:T(8,128)} %tok_ref.3, f32[12,122,768]{2,1,0:T(8,128)} %cot_ref.3, f32[24,2304]{1,0:T(8,128)} %refs_0_.1, f32[24,128]{1,0:T(8,128)} %pad.4.col_ref, ...), custom_call_target="tpu_custom_call" | custom-call | tf_op jit(solution)/shard_map/prepare/pallas_call | solution.py:1005
  11.7 40.4 %front.1 = (bf16[2,2,2,2,2,24,2432]{6,5,4,3,2,1,0:T(8,128)(2,1)}, bf16[3,4,128,768]{3,2,1,0:T(8,128)(2,1)}) custom-call(bf16[24,2432]{1,0:T(8,128)(2,1)} %get-tuple-element.75.refs_0_, bf16[12,128,768]{2,1,0:T(8,128)(2,1)} %get-tuple-element.76.refs_1_), custom_call_target="tpu_custom_call" | custom-call | tf_op jit(solution)/shard_map/front/pallas_call | solution.py:916
  52.1 0.9 slice.12
  53.0 0.1 copy.50
  53.2 0.6 convert_bitcast_fusion.vec_ref
  53.8 65.0 %attn_fwd.1 = (bf16[1536,768]{1,0:T(8,128)(2,1)}, bf16[12,1536,128]{2,1,0:T(8,128)(2,1)}, bf16[1536,1536]{1,0:T(8,128)(2,1)}, bf16[1536,768]{1,0:T(8,128)(2,1)},...) custom-call(bf16[1536,768]{1,0:T(8,128)(2,1)} %bitcast.20, ...), custom_call_target="tpu_custom_call" | custom-call | tf_op jit(solution)/shard_map/attn_fwd/pallas_call | solution.py:391
  118.8 94.0 %ffn.1 = (bf16[1536,768]{1,0:T(8,128)(2,1)}, f32[1536,768]{1,0:T(8,128)}, bf16[768,1536]{1,0:T(8,128)(2,1)}, bf16[1536,768]{1,0:T(8,128)(2,1)}, bf16[768,768]{1,...) custom-call(bf16[1536,768]{1,0:T(8,128)(2,1)} %get-tuple-element.83.mix_ref, ...), custom_call_target="tpu_custom_call" | custom-call | tf_op jit(solution)/shard_map/ffn/pallas_call | solution.py:215
  212.8 94.8 %attn_bwd.1 = (f32[24,2304]{1,0:T(8,128)}, f32[24,128]{1,0:T(8,128)}, f32[24,768]{1,0:T(8,128)}, f32[24,3072]{1,0:T(8,128)}, f32[96,768]{1,0:T(8,128)}, /*index=...) custom-call(bf16[1536,768]{1,0:T(8,128)(2,1)} %bitcast.22, bf16[1536,768]{1,0:T(8,128)(2,1)} %bitcast.27, ...), custom_call_target="tpu_custom_call" | custom-call | tf_op jit(solution)/shard_map/attn_bwd/pallas_call | solution.py:605
  307.7 1.2 slice.11
  309.6 0.8 copy.49
  310.4 0.6 slice_bitcast_fusion.refs_19_
  311.0 0.0 copy-start.1
  311.0 12.4 %finish.1 = (f32[24,2304]{1,0:T(8,128)}, f32[24,768]{1,0:T(8,128)}, f32[24,3072]{1,0:T(8,128)}, f32[96,768]{1,0:T(8,128)}, f32[12,24]{1,0:T(8,128)}, /*index=5*/...) custom-call(f32[12,122,768]{2,1,0:T(8,128)} %tok_ref.3, ...), custom_call_target="tpu_custom_call" | custom-call | tf_op jit(solution)/shard_map/finish/pallas_call | solution.py:1054
  323.4 0.0 copy-done.1
  (8 shorter events, 0.1 us)
Async XLA Ops:
  0.7 0.7 copy-start
  311.0 12.4 %copy-start.1 = (s32[12,48]{1,0:T(8,128)S(1)}, s32[12,48]{1,0:T(8,128)}, u32[]{:S(2)}) copy-start(s32[12,48]{1,0:T(8,128)} %param.20) | copy-start | bytes 6916
